TPU v7x, 512 devices: a whole 4x8x8 slice. The times are simulated.
512 devices in a mesh: term: 16 (over z, core), block: 32 (over y, x).
Axes of the slice: x: 4, y: 8, z: 8, core: 2. Of those that a mesh axis runs over, the one named last changes fastest.
Arguments:
- start: float32 [32, 256, 256], P('block'), may hold values from -6 to 6
- diagonal: float32 [32, 256, 256], P('block'), may hold values from -0.5 to 5
- left_ops: float32 [64, 32, 256, 256], P('term', 'block'), as said below
- right_ops: float32 [64, 32, 256, 256], P('term', 'block')
- offsets: int32 [64, 32], P('term', 'block'), may hold values from -1 to 1, as said below
- sizes: int32 [32], P('block'), may hold values from 128 to 256, as said below
Outputs:
- wave: float32 [32, 256, 256], P('block')
- image: float32 [32, 256, 256], P('block')
- energies: float32 [3], replicated
Inputs may be any that keep to these rules, and one draw needn't show every extreme that they name: `sizes`: each entry is 128 or 256; both occur in every draw. `offsets`: each term has one offset for all blocks; term 0 has offset 1 and term 1 offset 0; term t + 32 has the opposite offset of term t. For t < 32 with offset o, left_ops[t + 32, c] is the transpose of left_ops[t, c + o] wherever c + o is a block; likewise right_ops, so that H is symmetric.
All inputs are finite; a program needn't handle non-finite values.
Results may differ from a plain program's by a relative error of at most 0.0003.
Values sent between devices are 32-bit elements; how exact they have to be, the bound alone decides.
No kernel may reach another device: no remote copies, remote signals or barrier semaphores. Data moves between devices by JAX's collectives and lax.ppermute only.
A program may use at most 64 MiB of HBM per device.

v0:
```python
import math

import jax
import jax.numpy as jnp
from jax import lax
from jax.sharding import PartitionSpec as P

ITERS = 3


def padded_2(cells, sides, width):
    for axis, dim in sides:
        count = lax.axis_size(axis)
        ends = count - 1
        head = lax.slice_in_dim(cells, 0, width, axis=dim)
        tail = lax.slice_in_dim(cells, cells.shape[dim] - width, cells.shape[dim], axis=dim)
        cells = jnp.concatenate(
            [
                lax.ppermute(tail, axis, [(i, (i + 1) % count) for i in range(ends)]),
                cells,
                lax.ppermute(head, axis, [((i + 1) % count, i) for i in range(ends)]),
            ],
            axis=dim,
        )
    return cells


def per_device(start, diagonal, left_ops, right_ops, offsets, sizes):
    tile_rows = start.shape[1]
    local_blocks = start.shape[0]
    factor = math.sqrt(lax.axis_size("block") * local_blocks * tile_rows * tile_rows)
    live_rows = (jnp.arange(tile_rows, dtype=jnp.int32)[None, :] < sizes[:, None]).astype(
        jnp.float32
    )
    live_mask = live_rows[:, :, None] * live_rows[:, None, :]

    def reduce_terms(operand):
        return lax.psum(operand, "term")

    def global_sum(values):
        return lax.psum(values, "block")

    source_index = jnp.arange(local_blocks, dtype=jnp.int32)[None, :] + 1 - offsets

    def apply(part_vec):
        padded = padded_2(part_vec, (("block", 0),), 1)
        source = jnp.take(padded, source_index, axis=0)
        left_half = jnp.einsum("tbij,tbjk->tbik", left_ops, source, precision=lax.Precision.HIGHEST)
        term_sum = jnp.einsum(
            "tbik,tbkl->bil", left_half, right_ops, precision=lax.Precision.HIGHEST
        )
        return reduce_terms(term_sum) * live_mask

    initial = start * live_mask
    squares = global_sum(jnp.sum(initial * initial))
    vector = initial / jnp.sqrt(squares + 1e-12)
    image_vec = apply(vector)
    energies = []
    for iteration in range(ITERS):
        rayleigh = global_sum(jnp.sum(vector * image_vec))
        residual = image_vec - rayleigh * vector
        trial_vec = residual / jnp.maximum(jnp.abs(diagonal - rayleigh), 1.0)
        projection = global_sum(jnp.sum(vector * trial_vec))
        orthogonal = trial_vec - projection * vector
        norm_sq = global_sum(jnp.sum(orthogonal * orthogonal))
        unit_vec = orthogonal / jnp.sqrt(norm_sq + 1e-12)
        image_unit = apply(unit_vec)
        coupling, curvature = global_sum(
            (jnp.sum(unit_vec * image_vec), jnp.sum(unit_vec * image_unit))
        )
        lowest = 0.5 * (rayleigh + curvature) - jnp.sqrt(
            (0.5 * (rayleigh - curvature)) ** 2 + coupling * coupling
        )
        gap_value = curvature - lowest
        length = jnp.sqrt(gap_value * gap_value + coupling * coupling)
        vector = (gap_value * vector - coupling * unit_vec) / length
        image_vec = (gap_value * image_vec - coupling * image_unit) / length
        energies.append(lowest)
    wave, image = (vector, image_vec)
    return (wave * factor, image * factor, jnp.stack(energies))


def solution(mesh):
    return jax.shard_map(
        per_device,
        mesh=mesh,
        in_specs=(
            P("block", None, None),
            P("block", None, None),
            P("term", "block", None, None),
            P("term", "block", None, None),
            P("term", "block"),
            P("block"),
        ),
        out_specs=(P("block", None, None), P("block", None, None), P()),
        check_vma=False,
    )
```

profile of v0, /device:TPU:1, one launch (start us, length us, event | category | flops | bytes accessed | tf_op | source)
XLA Modules:
  0.0 1524.7 jit_solution(4545318461517179759)
XLA Ops:
  8.0 1.7 multiply_reduce_fusion.15
  9.7 62.5 %psum.140 = f32[]{:T(128)} all-reduce(f32[]{:T(128)} %multiply_reduce_fusion.15), channel_id=1, replica_groups=mesh['term'=16,'block'=32] {'block'}, use_global_device_ids=true, to_apply=%region_1.0 | all-reduce | flops 1 | bytes 8 | tf_op jit(solution)/shard_map/psum | solution.py:41
  74.4 4.0 collective-permute-start
  78.4 1.8 collective-permute-done.1
  81.7 1.6 gather_fusion
  83.3 2.6 convolution_bitcast_fusion.3
  85.9 1.7 convolution_bitcast_fusion.7
  87.8 133.0 %all-reduce.8.cloned.1.call-done = f32[1,256,256]{2,1,0:T(8,128)} async-done(((f32[1,256,256]{2,1,0:T(8,128)}), f32[1,256,256]{2,1,0:T(8,128)}) %all-reduce.8.cloned.1.call-update) | async-done | bytes 262160 | tf_op jit(solution)/shard_map/psum | solution.py:38
  220.7 1.8 multiply_reduce_fusion.14
  222.5 61.0 %psum.142 = f32[]{:T(128)} all-reduce(f32[]{:T(128)} %multiply_reduce_fusion.14), channel_id=1, replica_groups=mesh['term'=16,'block'=32] {'block'}, use_global_device_ids=true, to_apply=%region_4.6 | all-reduce | flops 1 | bytes 8 | tf_op jit(solution)/shard_map/psum | solution.py:41
  284.9 56.7 %psum.143 = f32[]{:T(128)} all-reduce(f32[]{:T(128)} %multiply_reduce_fusion.13), channel_id=1, replica_groups=mesh['term'=16,'block'=32] {'block'}, use_global_device_ids=true, to_apply=%region_6.8 | all-reduce | flops 1 | bytes 8 | tf_op jit(solution)/shard_map/psum | solution.py:41
  341.6 2.1 multiply_reduce_fusion.12
  343.7 57.7 %psum.144 = f32[]{:T(128)} all-reduce(f32[]{:T(128)} %multiply_reduce_fusion.12), channel_id=1, replica_groups=mesh['term'=16,'block'=32] {'block'}, use_global_device_ids=true, to_apply=%region_8.10 | all-reduce | flops 1 | bytes 8 | tf_op jit(solution)/shard_map/psum | solution.py:41
  404.9 4.0 collective-permute-start.2
  408.9 2.0 collective-permute-done.3
  413.2 2.7 gather_fusion.1
  415.9 2.5 convolution_bitcast_fusion.2
  418.4 1.7 convolution_bitcast_fusion.6
  420.2 157.4 %all-reduce.10.cloned.1.call-done = f32[1,256,256]{2,1,0:T(8,128)} async-done(((f32[1,256,256]{2,1,0:T(8,128)}), f32[1,256,256]{2,1,0:T(8,128)}) %all-reduce.10.cloned.1.call-update) | async-done | bytes 262160 | tf_op jit(solution)/shard_map/psum | solution.py:38
  577.6 1.7 multiply_reduce_fusion.10
  579.3 61.1 %all-reduce.2 = (f32[]{:T(128)}, f32[]{:T(128)}) all-reduce(f32[]{:T(128)} %get-tuple-element.5, f32[]{:T(128)} %get-tuple-element.4), channel_id=1, replica_groups=mesh['term'=16,'block'=32] {'block'}, use_global_device_ids=true, to_apply=%region_11.13 | all-reduce | flops 2 | bytes 16 | tf_op jit(solution)/shard_map/psum | solution.py:41
  644.9 2.5 multiply_reduce_fusion.9
  647.4 56.7 %psum.148 = f32[]{:T(128)} all-reduce(f32[]{:T(128)} %get-tuple-element.19), channel_id=1, replica_groups=mesh['term'=16,'block'=32] {'block'}, use_global_device_ids=true, to_apply=%region_15.17 | all-reduce | flops 1 | bytes 8 | tf_op jit(solution)/shard_map/psum | solution.py:41
  705.4 57.7 %psum.149 = f32[]{:T(128)} all-reduce(f32[]{:T(128)} %multiply_reduce_fusion.8), channel_id=1, replica_groups=mesh['term'=16,'block'=32] {'block'}, use_global_device_ids=true, to_apply=%region_17.19 | all-reduce | flops 1 | bytes 8 | tf_op jit(solution)/shard_map/psum | solution.py:41
  763.2 2.0 multiply_reduce_fusion.7
  765.1 56.5 %psum.150 = f32[]{:T(128)} all-reduce(f32[]{:T(128)} %multiply_reduce_fusion.7), channel_id=1, replica_groups=mesh['term'=16,'block'=32] {'block'}, use_global_device_ids=true, to_apply=%region_19.21 | all-reduce | flops 1 | bytes 8 | tf_op jit(solution)/shard_map/psum | solution.py:41
  825.1 4.1 collective-permute-start.4
  829.2 1.9 collective-permute-done.5
  833.4 2.7 gather_fusion.2
  836.2 2.5 convolution_bitcast_fusion.1
  838.7 1.7 convolution_bitcast_fusion.5
  840.5 172.6 %all-reduce.12.cloned.1.call-done = f32[1,256,256]{2,1,0:T(8,128)} async-done(((f32[1,256,256]{2,1,0:T(8,128)}), f32[1,256,256]{2,1,0:T(8,128)}) %all-reduce.12.cloned.1.call-update) | async-done | bytes 262160 | tf_op jit(solution)/shard_map/psum | solution.py:38
  1013.1 1.7 multiply_reduce_fusion.5
  1014.8 61.1 %all-reduce.1 = (f32[]{:T(128)}, f32[]{:T(128)}) all-reduce(f32[]{:T(128)} %get-tuple-element.9, f32[]{:T(128)} %get-tuple-element.8), channel_id=1, replica_groups=mesh['term'=16,'block'=32] {'block'}, use_global_device_ids=true, to_apply=%region_22.24 | all-reduce | flops 2 | bytes 16 | tf_op jit(solution)/shard_map/psum | solution.py:41
  1080.4 2.4 multiply_reduce_fusion.4
  1082.8 56.7 %psum.154 = f32[]{:T(128)} all-reduce(f32[]{:T(128)} %get-tuple-element.16), channel_id=1, replica_groups=mesh['term'=16,'block'=32] {'block'}, use_global_device_ids=true, to_apply=%region_26.28 | all-reduce | flops 1 | bytes 8 | tf_op jit(solution)/shard_map/psum | solution.py:41
  1140.8 57.7 %psum.155 = f32[]{:T(128)} all-reduce(f32[]{:T(128)} %multiply_reduce_fusion.3), channel_id=1, replica_groups=mesh['term'=16,'block'=32] {'block'}, use_global_device_ids=true, to_apply=%region_28.30 | all-reduce | flops 1 | bytes 8 | tf_op jit(solution)/shard_map/psum | solution.py:41
  1198.5 2.0 multiply_reduce_fusion.2
  1200.5 56.5 %psum.156 = f32[]{:T(128)} all-reduce(f32[]{:T(128)} %multiply_reduce_fusion.2), channel_id=1, replica_groups=mesh['term'=16,'block'=32] {'block'}, use_global_device_ids=true, to_apply=%region_30.32 | all-reduce | flops 1 | bytes 8 | tf_op jit(solution)/shard_map/psum | solution.py:41
  1260.4 4.3 collective-permute-start.6
  1264.7 1.7 collective-permute-done.7
  1268.8 2.7 gather_fusion.3
  1271.6 2.5 convolution_bitcast_fusion
  1274.1 1.7 convolution_bitcast_fusion.4
  1275.8 172.8 %all-reduce.14.cloned.1.call-done = f32[1,256,256]{2,1,0:T(8,128)} async-done(((f32[1,256,256]{2,1,0:T(8,128)}), f32[1,256,256]{2,1,0:T(8,128)}) %all-reduce.14.cloned.1.call-update) | async-done | bytes 262160 | tf_op jit(solution)/shard_map/psum | solution.py:38
  1448.6 1.8 multiply_reduce_fusion
  1450.4 61.1 %all-reduce = (f32[]{:T(128)}, f32[]{:T(128)}) all-reduce(f32[]{:T(128)} %get-tuple-element.7, f32[]{:T(128)} %get-tuple-element.6), channel_id=1, replica_groups=mesh['term'=16,'block'=32] {'block'}, use_global_device_ids=true, to_apply=%region_33.35 | all-reduce | flops 2 | bytes 16 | tf_op jit(solution)/shard_map/psum | solution.py:41
  1516.6 1.5 divide_multiply_fusion
  (50 shorter events, 23.1 us)
Async XLA Ops:
  7.2 76.2 %copy-start = (f32[4,1,256,256]{3,2,1,0:T(8,128)S(1)}, f32[4,1,256,256]{3,2,1,0:T(8,128)}, u32[]{:S(2)}) copy-start(f32[4,1,256,256]{3,2,1,0:T(8,128)} %param.10) | copy-start | bytes 3145732
  7.2 65.8 %copy-start.3 = (f32[1,256,256]{2,1,0:T(8,128)S(1)}, f32[1,256,256]{2,1,0:T(8,128)}, u32[]{:S(2)}) copy-start(f32[1,256,256]{2,1,0:T(8,128)} %param.8) | copy-start | bytes 786436
  7.2 213.5 %all-reduce.8.cloned.1.call-start = ((), (), s32[]{:S(2)}) async-start(), calls=%async_computation | async-start | bytes 524288 | tf_op jit(solution)/shard_map/psum | solution.py:38
  72.9 5.4 copy-start.8
  73.1 7.1 collective-permute-start.1
  74.4 7.3 collective-permute-start
  83.3 2.6 copy-start.2
  87.7 195.8 %copy-start.1 = (f32[1,256,256]{2,1,0:T(8,128)S(1)}, f32[1,256,256]{2,1,0:T(8,128)}, u32[]{:S(2)}) copy-start(f32[1,256,256]{2,1,0:T(8,128)} %param.9) | copy-start | bytes 786436
  87.7 489.9 %all-reduce.10.cloned.1.call-start = ((), (), s32[]{:S(2)}) async-start(), calls=%async_computation.1 | async-start | bytes 524288 | tf_op jit(solution)/shard_map/psum | solution.py:38
  220.7 62.8 %copy-start.4 = (f32[1,256,256]{2,1,0:T(8,128)S(1)}, f32[1,256,256]{2,1,0:T(8,128)}, u32[]{:S(2)}) copy-start(f32[1,256,256]{2,1,0:T(8,128)} %all-reduce.8.cloned.1.call-done) | copy-start | bytes 786436
  403.5 174.1 %copy-start.6 = (f32[1,256,256]{2,1,0:T(8,128)}, f32[1,256,256]{2,1,0:T(8,128)S(1)}, u32[]{:S(2)}) copy-start(f32[1,256,256]{2,1,0:T(8,128)S(1)} %broadcast_divide_fusion.2) | copy-start | bytes 786436
  403.6 7.3 collective-permute-start.3
  404.9 7.3 collective-permute-start.2
  420.2 592.9 %all-reduce.12.cloned.1.call-start = ((), (), s32[]{:S(2)}) async-start(), calls=%async_computation.2 | async-start | bytes 524288 | tf_op jit(solution)/shard_map/psum | solution.py:38
  823.8 189.3 %copy-start.5 = (f32[1,256,256]{2,1,0:T(8,128)}, f32[1,256,256]{2,1,0:T(8,128)S(1)}, u32[]{:S(2)}) copy-start(f32[1,256,256]{2,1,0:T(8,128)S(1)} %broadcast_divide_fusion.1) | copy-start | bytes 786436
  823.8 7.3 collective-permute-start.5
  825.1 7.4 collective-permute-start.4
  840.5 608.2 %all-reduce.14.cloned.1.call-start = ((), (), s32[]{:S(2)}) async-start(), calls=%async_computation.3 | async-start | bytes 524288 | tf_op jit(solution)/shard_map/psum | solution.py:38
  1259.1 7.3 collective-permute-start.7
  1260.4 7.4 collective-permute-start.6
  1448.6 68.0 %copy-start.7 = (f32[1,256,256]{2,1,0:T(8,128)S(1)}, f32[1,256,256]{2,1,0:T(8,128)}, u32[]{:S(2)}) copy-start(f32[1,256,256]{2,1,0:T(8,128)} %all-reduce.14.cloned.1.call-done) | copy-start | bytes 786436
Sparse Core Ops, SparseCore 0:
  87.8 132.8 all-reduce.7
  420.3 157.2 all-reduce.9
  840.6 172.4 all-reduce.11
  1275.9 172.6 all-reduce.13
where the time goes:
time: 1540 us; the launch traced here: 1520 us
  blocking collectives  763 us (50%)
  waiting for transfers between devices  649 us (42%)
  other arithmetic  33.2 us (2%)
  between operations  31.2 us (2%)
  starting transfers between devices  21.7 us (1%)
  matrix products  17.1 us (1%)
    psum x13, blocking collectives, global_sum(): return lax.psum(values, 'block')  763 us
    psum x4, waiting for transfers between devices, reduce_terms(): return lax.psum(operand, 'term')  636 us
  transfers between devices with their start and end apart: 12, of which 12 were waited for; matrix products, arithmetic and copies ran while one was open for 0% of the time, Pallas kernels for 0%

commit v1 on v0

v1 whole, which is shorter than its diff:
```python
import math

import jax
import jax.numpy as jnp
import numpy as np
from jax import lax
from jax.experimental import pallas as pl
from jax.experimental.pallas import tpu as pltpu
from jax.sharding import Mesh, PartitionSpec as P

ITERS = 3
ZS, CORES, BLOCKS = 8, 2, 32
GROUP = ZS * CORES
M = 256
PIECE = M // ZS
HALF = PIECE // CORES
SCAL = 8
TERM = ("z", "core")
ALL = ("z", "core", "block")
VMEM = pl.BlockSpec(memory_space=pltpu.VMEM)
SMEM = pl.BlockSpec(memory_space=pltpu.SMEM)
BF16, F32 = jnp.bfloat16, jnp.float32


def split(x):
    high = x.astype(BF16)
    return high, (x - high.astype(F32)).astype(BF16)


def dot3(a, b):
    def mm(x, y):
        return lax.dot_general(x, y, (((1,), (0,)), ((), ())), preferred_element_type=F32)

    return mm(a[0], b[0]) + (mm(a[0], b[1]) + mm(a[1], b[0]))


def column_sum(x):
    return jnp.sum(x, axis=0, keepdims=True)


def apply_terms(info, left, right, t_high, t_low, t_own, v_own, r_own, part):
    total = jnp.zeros((M, M), F32)
    for term in range(left.shape[0]):
        sel = 1 - info[2 + term]
        half = dot3(split(left[term]), (t_high[sel], t_low[sel]))
        total = total + dot3(split(half), split(right[term]))
    size = info[1]
    live = (lax.broadcasted_iota(jnp.int32, (M, M), 0) < size) & (
        lax.broadcasted_iota(jnp.int32, (M, M), 1) < size
    )
    total = jnp.where(live, total, 0.0)
    share = 1.0 / GROUP
    rows = [
        column_sum(t_own * t_own) * share,
        column_sum(t_own * total),
    ]
    if v_own is not None:
        rows += [
            column_sum(v_own * t_own) * share,
            column_sum(t_own * r_own) * share,
            column_sum(v_own * total),
        ]
    rows.append(jnp.zeros((SCAL - len(rows), M), F32))
    scal = jnp.concatenate(rows, axis=0)
    for z in range(ZS):
        part[z, :PIECE] = total[z * PIECE : (z + 1) * PIECE]
        part[z, PIECE:] = scal


def first_kernel(info, left, right, x3, part, t_high, t_low):
    for i in range(3):
        t_high[i], t_low[i] = split(x3[i])
    apply_terms(info, left, right, t_high, t_low, x3[1], None, None, part)


def global_sums(info, gathered, row):
    shift = lax.shift_right_logical(info[0], 1)
    total = None
    for m in range(GROUP):
        piece = gathered[lax.rem(m + GROUP - shift, GROUP), row : row + SCAL]
        total = piece if total is None else total + piece
    return jnp.sum(total, axis=1, keepdims=True)


def scalars(first, sums, state):
    tt, th = sums[0:1], sums[1:2]
    if first:
        scale = tt + 1e-12
        return None, jnp.sqrt(scale), None, None, None, th / scale, tt / scale, None
    p, tr, vh = sums[2:3], sums[3:4], sums[4:5]
    rho, vv = state[0:1, 0:1], state[1:2, 0:1]
    norm_sq = jnp.maximum(tt - 2.0 * p * p + p * p * vv, 0.0)
    n_sq = norm_sq + 1e-12
    n = jnp.sqrt(n_sq)
    tw = tr + rho * p
    coupling = tr / n
    curvature = (th - p * tw - p * vh + p * p * rho) / n_sq
    lowest = 0.5 * (rho + curvature) - jnp.sqrt((0.5 * (rho - curvature)) ** 2 + coupling * coupling)
    gap = curvature - lowest
    len_sq = gap * gap + coupling * coupling
    length = jnp.sqrt(len_sq)
    v_image = (vh - p * rho) / n
    v_unit = (p - p * vv) / n
    unit_sq = norm_sq / n_sq
    next_rho = (gap * gap * rho - gap * coupling * (v_image + coupling) + coupling * coupling * curvature) / len_sq
    next_vv = (gap * gap * vv - 2.0 * gap * coupling * v_unit + coupling * coupling * unit_sq) / len_sq
    return p, n, gap, coupling, length, next_rho, next_vv, lowest


def combine(first, scal, v, w, t, y):
    p, n, gap, coupling, length = scal[:5]
    if first:
        return t / n, y / n
    by_unit = coupling / (n * length)
    by_old = gap / length + p * by_unit
    return by_old * v - by_unit * t, by_old * w - by_unit * y


def state_rows(first, scal, state, iteration):
    rows = [scal[5], scal[6]]
    for i in range(ITERS):
        if i < iteration - 1:
            rows.append(state[2 + i : 3 + i, 0:1])
        elif i == iteration - 1 and not first:
            rows.append(scal[7])
        else:
            rows.append(jnp.zeros((1, 1), F32))
    rows.append(jnp.zeros((SCAL - len(rows), 1), F32))
    return jnp.broadcast_to(jnp.concatenate(rows, axis=0), (SCAL, 128))


def step_kernel(iteration, *refs):
    first = iteration == 0
    if first:
        info, left, right, diag3, gathered, t3, state_out, v_out, w_out, t_out, part, t_high, t_low = refs
        v3 = w3 = state = None
    else:
        (info, left, right, diag3, gathered, v3, w3, t3, state, state_out, v_out, w_out, t_out, part,
         t_high, t_low) = refs
    scal = scalars(first, global_sums(info, gathered, PIECE + HALF), None if first else state)
    rho = scal[5]
    state_out[...] = state_rows(first, scal, state, iteration)

    def update(block, rows, y):
        old = (None, None) if first else (v3[block, rows], w3[block, rows])
        v, w = combine(first, scal, *old, t3[block, rows], y)
        r = w - rho * v
        t = r / jnp.maximum(jnp.abs(diag3[block, rows] - rho), 1.0)
        v_out[block, rows] = v
        w_out[block, rows] = w
        t_out[block, rows] = t
        t_high[block, rows], t_low[block, rows] = split(t)

    for z in range(ZS):
        rows = pl.ds(z * PIECE, PIECE)
        update(0, rows, gathered[2 * z, :PIECE])
        update(2, rows, gathered[2 * z + 1, :PIECE])
        update(1, rows, jnp.concatenate(
            [gathered[2 * z, PIECE : PIECE + HALF], gathered[2 * z + 1, PIECE : PIECE + HALF]], axis=0))
    v_own = v_out[1]
    apply_terms(info, left, right, t_high, t_low, t_out[1], v_own, w_out[1] - rho * v_own, part)


def last_kernel(factor, info, gathered, v3, w3, t3, state, wave, image, state_out):
    scal = scalars(False, global_sums(info, gathered, HALF), state)
    state_out[...] = state_rows(False, scal, state, ITERS)
    for j in range(GROUP):
        rows = pl.ds(j * HALF, HALF)
        v, w = combine(False, scal, v3[0, rows], w3[0, rows], t3[0, rows], gathered[j, :HALF])
        wave[0, rows] = v * factor
        image[0, rows] = w * factor


def shape(*dims):
    return jax.ShapeDtypeStruct(dims, F32)


PARAMS = pltpu.CompilerParams(vmem_limit_bytes=24 * 1024 * 1024)
SPLITS = [pltpu.VMEM((3, M, M), BF16), pltpu.VMEM((3, M, M), BF16)]
PART = shape(ZS, PIECE + SCAL, M)


def run_first(info, left, right, x3):
    return pl.pallas_call(
        first_kernel,
        out_shape=PART,
        in_specs=[SMEM] + [VMEM] * 3,
        out_specs=VMEM,
        scratch_shapes=SPLITS,
        compiler_params=PARAMS,
        name="first",
    )(info, left, right, x3)


def run_step(iteration, info, *arrays):
    def body(*refs):
        step_kernel(iteration, *refs)

    return pl.pallas_call(
        body,
        out_shape=(shape(SCAL, 128), shape(3, M, M), shape(3, M, M), shape(3, M, M), PART),
        in_specs=[SMEM] + [VMEM] * len(arrays),
        out_specs=(VMEM,) * 5,
        scratch_shapes=SPLITS,
        compiler_params=PARAMS,
        name="step",
    )(info, *arrays)


def run_last(info, gathered, v3, w3, t3, state):
    factor = math.sqrt(BLOCKS * M * M)

    def body(*refs):
        last_kernel(factor, *refs)

    own = pl.BlockSpec((1, M, M), lambda i: (1, 0, 0))

    def whole(x):
        return pl.BlockSpec(x.shape, lambda i: (0,) * x.ndim)

    out = pl.BlockSpec((1, M, M), lambda i: (0, 0, 0))
    return pl.pallas_call(
        body,
        grid=(1,),
        out_shape=(shape(1, M, M), shape(1, M, M), shape(SCAL, 128)),
        in_specs=[SMEM, whole(gathered), own, own, own, whole(state)],
        out_specs=(out, out, whole(state)),
        compiler_params=PARAMS,
        name="last",
    )(info, gathered, v3, w3, t3, state)


def halo_pairs():
    pairs = []
    for z in range(ZS):
        for core in range(CORES):
            for b in range(BLOCKS):
                source = b - 1 if core == 0 else b + 1
                if 0 <= source < BLOCKS:
                    base = (z * CORES + core) * BLOCKS
                    pairs.append((base + source, base + b))
    return pairs


def spread_pairs(flip):
    return [
        (j * BLOCKS + ((b ^ flip) + 2 * j) % BLOCKS, j * BLOCKS + b)
        for j in range(GROUP)
        for b in range(BLOCKS)
    ]


def halo_whole(block):
    got = lax.ppermute(block, ALL, halo_pairs())
    both = lax.all_gather(got, "core", axis=0)
    return jnp.stack([both[0], block, both[1]])


def exchange(part, with_halo):
    pair = lax.all_gather(part, "core", axis=0)
    summed = pair[0] + pair[1]
    pieces = lax.all_to_all(summed, "z", 0, 0, tiled=True)
    mine = jnp.sum(pieces, axis=0)
    rows, scal = mine[:PIECE], mine[PIECE:]
    parts = []
    if with_halo:
        parts.append(lax.ppermute(rows, ALL, halo_pairs()))
    spread = lax.ppermute(scal, ALL, spread_pairs(0)) + lax.ppermute(scal, ALL, spread_pairs(1))
    parts.append(lax.dynamic_slice_in_dim(rows, lax.axis_index("core") * HALF, HALF, 0))
    parts.append(spread)
    return lax.all_gather(jnp.concatenate(parts, axis=0), TERM, axis=0)


def per_device(start, diagonal, left_ops, right_ops, offsets, sizes):
    left, right = left_ops[:, 0], right_ops[:, 0]
    info = jnp.concatenate([lax.axis_index("block")[None].astype(jnp.int32), sizes, offsets[:, 0]])
    live = jnp.arange(M, dtype=jnp.int32) < sizes[0]
    masked = jnp.where(live[:, None] & live[None, :], start[0], 0.0)
    x3 = halo_whole(masked)
    part = run_first(info, left, right, x3)
    diag3 = halo_whole(diagonal[0])
    gathered = exchange(part, True)
    state, v3, w3, t3, part = run_step(0, info, left, right, diag3, gathered, x3)
    for iteration in range(1, ITERS):
        gathered = exchange(part, True)
        state, v3, w3, t3, part = run_step(
            iteration, info, left, right, diag3, gathered, v3, w3, t3, state)
    gathered = exchange(part, False)
    wave, image, state = run_last(info, gathered, v3, w3, t3, state)
    return wave, image, state[2 : 2 + ITERS, 0]


def solution(mesh):
    grid = Mesh(np.asarray(mesh.devices).reshape(ZS, CORES, BLOCKS), ALL)
    return jax.shard_map(
        per_device,
        mesh=grid,
        in_specs=(
            P("block", None, None),
            P("block", None, None),
            P(TERM, "block", None, None),
            P(TERM, "block", None, None),
            P(TERM, "block"),
            P("block"),
        ),
        out_specs=(P("block", None, None), P("block", None, None), P()),
        check_vma=False,
    )
```

time: 1540 us -> 254 us (0.16)
  waiting for transfers between devices: 649 us -> 27.6 us
  blocking collectives: 763 us -> 149 us
  other arithmetic: 33.2 us -> 3.39 us
  between operations: 31.2 us -> 1.77 us
  starting transfers between devices: 21.7 us -> 49.3 us
  matrix products: 17.1 us -> 0 us
    psum x13 -> x0, blocking collectives: 763 us -> none  [global_sum(): return lax.psum(values, 'block')]
    psum x4 -> x0, waiting for transfers between devices: 636 us -> none  [reduce_terms(): return lax.psum(operand, 'term')]
    all_gather x0 -> x10, blocking collectives: none -> 93.6 us  [the longest x4 75.9 us: exchange(): return lax.all_gather(jnp.concatenate(parts, axis=0), TERM, axis=0)]
    all_to_all x0 -> x3, blocking collectives: none -> 55.1 us  [exchange(): pieces = lax.all_to_all(summed, 'z', 0, 0, tiled=True)]
    reduce_sum x13 -> x4, other arithmetic: 23.7 us -> 0.09 us  [exchange(): mine = jnp.sum(pieces, axis=0)]
    ppermute x8 -> x13, starting transfers between devices: 21.6 us -> 42.1 us  [the longest x4 22.7 us: exchange(): lax.ppermute(scal, ALL, spread_pairs(1))]
    dot_general x8 -> x0, matrix products: 17.1 us -> none  [the longest x4 10.1 us: apply(): jnp.einsum('tbij,tbjk->tbik', left_ops, source, precision=lax.Precision.H...]
  transfers between devices with their start and end apart: 12 -> 14, of which waited for: 12 -> 9; matrix products, arithmetic and copies ran while one was open for 0% -> 1% of each run, Pallas kernels for 0% -> 1%
where the time goes in v1:
time: 254 us; the launch traced here: 253 us
  blocking collectives  149 us (59%)
  starting transfers between devices  49.3 us (19%)
  waiting for transfers between devices  27.6 us (11%)
  local copies, waits for them, and re-layouts  11.5 us (5%)
  Pallas kernels  10.6 us (4%)
  other arithmetic  3.39 us (1%)
    all_gather x4, blocking collectives, exchange(): return lax.all_gather(jnp.concatenate(parts, axis=0), TERM, axis=0)  75.9 us
    all_to_all x3, blocking collectives, exchange(): pieces = lax.all_to_all(summed, 'z', 0, 0, tiled=True)  55.1 us
    ppermute x4, starting transfers between devices, exchange(): lax.ppermute(scal, ALL, spread_pairs(1))  22.7 us
    ppermute x4, starting transfers between devices, exchange(): lax.ppermute(scal, ALL, spread_pairs(0))  13 us
    unnamed x48, local copies, waits for them, and re-layouts  10.8 us
    all_to_all x1, waiting for transfers between devices, exchange(): pieces = lax.all_to_all(summed, 'z', 0, 0, tiled=True)  10.1 us
    all_gather x4, blocking collectives, exchange(): pair = lax.all_gather(part, 'core', axis=0)  9.07 us
    all_gather x2, blocking collectives, halo_whole(): both = lax.all_gather(got, 'core', axis=0)  8.6 us
  transfers between devices with their start and end apart: 14, of which 9 were waited for; matrix products, arithmetic and copies ran while one was open for 1% of the time, Pallas kernels for 1%

profile of v1, /device:TPU:1, one launch (start us, length us, event | category | flops | bytes accessed | tf_op | source)
XLA Modules:
  0.0 253.0 jit_solution(7569080834164582106)
XLA Ops:
  1.3 1.1 bitcast_select_fusion
  2.4 1.3 collective-permute-start.1
  3.7 1.3 collective-permute-start
  5.9 4.3 %collective-permute-done.1 = f32[256,256]{1,0:T(8,128)S(1)} collective-permute-done((f32[256,256]{1,0:T(8,128)S(1)}, f32[256,256]{1,0:T(8,128)S(1)}, u32[]{:S(2)}, u32[]{:S(2)}) %collective-permute-start.1) | collective-permute-done | bytes 262176 | tf_op jit(solution)/shard_map/ppermute | solution.py:254
  10.1 6.1 %all-gather.1 = f32[512,256]{1,0:T(8,128)S(1)} all-gather(f32[256,256]{1,0:T(8,128)S(1)} %collective-permute-done.1), channel_id=3, replica_groups=mesh['z'=8,'core'=2,'block'=32] {'core'}, dimensions={0}, use_global_device_ids=true | all-gather | bytes 786432 | tf_op jit(solution)/shard_map/all_gather | solution.py:255
  16.4 1.4 copy-done.1
  18.1 1.9 first.1
  20.0 2.3 all-gather.2
  23.1 7.2 %all-to-all-start = ((f32[8,40,256]{2,1,0:T(8,128)}), f32[8,40,256]{2,1,0:T(8,128)S(1)}, u32[]{:S(2)}, u32[]{:S(2)}) async-start(f32[8,40,256]{2,1,0:T(8,128)} %slice_add_fusion.3), calls=%async_computation | async-start | bytes 655360 | tf_op jit(solution)/shard_map/all_to_all | solution.py:262
  30.3 2.5 all-gather
  32.8 1.0 pad_maximum_fusion.refs_3_
  33.8 10.1 %all-to-all-done = f32[8,40,256]{2,1,0:T(8,128)S(1)} async-done(((f32[8,40,256]{2,1,0:T(8,128)}), f32[8,40,256]{2,1,0:T(8,128)S(1)}, u32[]{:S(2)}, u32[]{:S(2)}) %all-to-all-start) | async-done | bytes 327712 | tf_op jit(solution)/shard_map/all_to_all | solution.py:262
  43.9 8.0 %collective-permute-start.4 = (f32[8,256]{1,0:T(8,128)S(1)}, f32[8,256]{1,0:T(8,128)S(1)}, u32[]{:S(2)}, u32[]{:S(2)}) collective-permute-start(f32[8,256]{1,0:T(8,128)S(1)} %slice.103), channel_id=1, source_target_pairs={{1,0},{0,1},{3,2},{2,3},{5,4},{4,5},{7,6},{6,7},{9,8},{8,9},{11,10... | collective-permute-start | bytes 24584 | tf_op jit(solution)/shard_map/ppermute | solution.py:268
  51.9 2.4 collective-permute-start.3
  54.4 1.3 collective-permute-start.2
  55.7 2.1 collective-permute-done.3
  57.8 2.1 collective-permute-done.2
  60.0 18.4 %all-gather.3 = f32[896,256]{1,0:T(8,128)S(1)} all-gather(f32[56,256]{1,0:T(8,128)S(1)} %pad_maximum_fusion.2), channel_id=5, replica_groups=mesh['z'=8,'core'=2,'block'=32] {'z','core'}, dimensions={0}, use_global_device_ids=true | all-gather | bytes 974848 | tf_op jit(solution)/shard_map/all_gather | solution.py:271
  78.3 2.3 step.3
  81.5 2.3 all-gather.4
  83.8 17.8 %all_to_all.20 = f32[8,40,256]{2,1,0:T(8,128)S(1)} all-to-all(f32[8,40,256]{2,1,0:T(8,128)S(1)} %slice_add_fusion.2), channel_id=1, replica_groups=mesh['z'=8,'core'=2,'block'=32] {'z'}, dimensions={0} | all-to-all | bytes 655360 | tf_op jit(solution)/shard_map/all_to_all | solution.py:262
  101.6 5.2 %collective-permute-start.7 = (f32[8,256]{1,0:T(8,128)S(1)}, f32[8,256]{1,0:T(8,128)S(1)}, u32[]{:S(2)}, u32[]{:S(2)}) collective-permute-start(f32[8,256]{1,0:T(8,128)S(1)} %slice.107), channel_id=1, source_target_pairs={{1,0},{0,1},{3,2},{2,3},{5,4},{4,5},{7,6},{6,7},{9,8},{8,9},{11,10... | collective-permute-start | bytes 24584 | tf_op jit(solution)/shard_map/ppermute | solution.py:268
  106.9 3.8 %collective-permute-start.6 = (f32[8,256]{1,0:T(8,128)S(1)}, f32[8,256]{1,0:T(8,128)S(1)}, u32[]{:S(2)}, u32[]{:S(2)}) collective-permute-start(f32[8,256]{1,0:T(8,128)S(1)} %slice.107), channel_id=1, source_target_pairs={{0,0},{1,1},{2,2},{3,3},{4,4},{5,5},{6,6},{7,7},{8,8},{9,9},{10,10... | collective-permute-start | bytes 24584 | tf_op jit(solution)/shard_map/ppermute | solution.py:268
  110.6 1.3 collective-permute-start.5
  112.8 2.6 %collective-permute-done.5 = f32[32,256]{1,0:T(8,128)S(1)} collective-permute-done((f32[32,256]{1,0:T(8,128)S(1)}, f32[32,256]{1,0:T(8,128)S(1)}, u32[]{:S(2)}, u32[]{:S(2)}) %collective-permute-start.5) | collective-permute-done | bytes 32800 | tf_op jit(solution)/shard_map/ppermute | solution.py:267
  115.4 18.5 %all-gather.5 = f32[896,256]{1,0:T(8,128)S(1)} all-gather(f32[56,256]{1,0:T(8,128)S(1)} %pad_maximum_fusion.3), channel_id=7, replica_groups=mesh['z'=8,'core'=2,'block'=32] {'z','core'}, dimensions={0}, use_global_device_ids=true | all-gather | bytes 974848 | tf_op jit(solution)/shard_map/all_gather | solution.py:271
  133.8 1.1 copy-done.19
  135.0 1.1 copy-done.21
  136.1 2.4 step.4
  139.4 2.3 all-gather.6
  141.8 18.7 %all_to_all.21 = f32[8,40,256]{2,1,0:T(8,128)S(1)} all-to-all(f32[8,40,256]{2,1,0:T(8,128)S(1)} %slice_add_fusion.1), channel_id=1, replica_groups=mesh['z'=8,'core'=2,'block'=32] {'z'}, dimensions={0} | all-to-all | bytes 655360 | tf_op jit(solution)/shard_map/all_to_all | solution.py:262
  160.5 5.3 %collective-permute-start.10 = (f32[8,256]{1,0:T(8,128)S(1)}, f32[8,256]{1,0:T(8,128)S(1)}, u32[]{:S(2)}, u32[]{:S(2)}) collective-permute-start(f32[8,256]{1,0:T(8,128)S(1)} %slice.111), channel_id=1, source_target_pairs={{1,0},{0,1},{3,2},{2,3},{5,4},{4,5},{7,6},{6,7},{9,8},{8,9},{11,10... | collective-permute-start | bytes 24584 | tf_op jit(solution)/shard_map/ppermute | solution.py:268
  165.9 2.7 %collective-permute-start.9 = (f32[8,256]{1,0:T(8,128)S(1)}, f32[8,256]{1,0:T(8,128)S(1)}, u32[]{:S(2)}, u32[]{:S(2)}) collective-permute-start(f32[8,256]{1,0:T(8,128)S(1)} %slice.111), channel_id=1, source_target_pairs={{0,0},{1,1},{2,2},{3,3},{4,4},{5,5},{6,6},{7,7},{8,8},{9,9},{10,10... | collective-permute-start | bytes 24584 | tf_op jit(solution)/shard_map/ppermute | solution.py:268
  168.5 1.3 collective-permute-start.8
  169.8 2.0 collective-permute-done.9
  171.8 1.9 collective-permute-done.8
  173.8 20.2 %all-gather.7 = f32[896,256]{1,0:T(8,128)S(1)} all-gather(f32[56,256]{1,0:T(8,128)S(1)} %pad_maximum_fusion.4), channel_id=9, replica_groups=mesh['z'=8,'core'=2,'block'=32] {'z','core'}, dimensions={0}, use_global_device_ids=true | all-gather | bytes 974848 | tf_op jit(solution)/shard_map/all_gather | solution.py:271
  193.9 1.1 copy-done.13
  195.1 1.1 copy-done.15
  196.2 2.4 step.5
  199.6 2.3 all-gather.8
  201.9 18.7 %all_to_all.22 = f32[8,40,256]{2,1,0:T(8,128)S(1)} all-to-all(f32[8,40,256]{2,1,0:T(8,128)S(1)} %slice_add_fusion), channel_id=1, replica_groups=mesh['z'=8,'core'=2,'block'=32] {'z'}, dimensions={0} | all-to-all | bytes 655360 | tf_op jit(solution)/shard_map/all_to_all | solution.py:262
  220.6 4.1 %collective-permute-start.12 = (f32[8,256]{1,0:T(8,128)S(1)}, f32[8,256]{1,0:T(8,128)S(1)}, u32[]{:S(2)}, u32[]{:S(2)}) collective-permute-start(f32[8,256]{1,0:T(8,128)S(1)} %slice.115), channel_id=1, source_target_pairs={{1,0},{0,1},{3,2},{2,3},{5,4},{4,5},{7,6},{6,7},{9,8},{8,9},{11,10... | collective-permute-start | bytes 24584 | tf_op jit(solution)/shard_map/ppermute | solution.py:268
  224.7 4.2 %collective-permute-start.11 = (f32[8,256]{1,0:T(8,128)S(1)}, f32[8,256]{1,0:T(8,128)S(1)}, u32[]{:S(2)}, u32[]{:S(2)}) collective-permute-start(f32[8,256]{1,0:T(8,128)S(1)} %slice.115), channel_id=1, source_target_pairs={{0,0},{1,1},{2,2},{3,3},{4,4},{5,5},{6,6},{7,7},{8,8},{9,9},{10,10... | collective-permute-start | bytes 24584 | tf_op jit(solution)/shard_map/ppermute | solution.py:268
  229.0 1.7 collective-permute-done.11
  230.7 18.9 %all-gather.9 = f32[384,256]{1,0:T(8,128)S(1)} all-gather(f32[24,256]{1,0:T(8,128)S(1)} %pad_maximum_fusion.5), channel_id=11, replica_groups=mesh['z'=8,'core'=2,'block'=32] {'z','core'}, dimensions={0}, use_global_device_ids=true | all-gather | bytes 417792 | tf_op jit(solution)/shard_map/all_gather | solution.py:271
  249.6 1.1 copy-done.7
  250.7 1.6 last.1
  (83 shorter events, 6.6 us)
Async XLA Ops:
  1.3 4.5 %copy-start.22 = (f32[1,256,256]{2,1,0:T(8,128)S(1)}, f32[1,256,256]{2,1,0:T(8,128)}, u32[]{:S(2)}) copy-start(f32[1,256,256]{2,1,0:T(8,128)} %param.6) | copy-start | bytes 786436
  2.4 7.7 %collective-permute-start.1 = (f32[256,256]{1,0:T(8,128)S(1)}, f32[256,256]{1,0:T(8,128)S(1)}, u32[]{:S(2)}, u32[]{:S(2)}) collective-permute-start(f32[256,256]{1,0:T(8,128)S(1)} %bitcast_select_fusion), channel_id=1, source_target_pairs={{0,1},{1,2},{2,3},{3,4},{4,5},{5,6},{6,7},{7,8},{8,9},{9,10},{10,1... | collective-permute-start | bytes 786440 | tf_op jit(solution)/shard_map/ppermute | solution.py:254
  3.7 26.5 %collective-permute-start = (f32[256,256]{1,0:T(8,128)}, f32[256,256]{1,0:T(8,128)S(1)}, u32[]{:S(2)}, u32[]{:S(2)}) collective-permute-start(f32[256,256]{1,0:T(8,128)} %bitcast.4), channel_id=1, source_target_pairs={{0,1},{1,2},{2,3},{3,4},{4,5},{5,6},{6,7},{7,8},{8,9},{9,10},{10,1... | collective-permute-start | bytes 786440 | tf_op jit(solution)/shard_map/ppermute | solution.py:254
  5.0 0.7 copy-start.23
  16.3 1.5 copy-start.1
  16.3 1.8 copy-start
  16.4 3.6 %copy-start.2 = (f32[3,256,256]{2,1,0:T(8,128)}, f32[3,256,256]{2,1,0:T(8,128)S(1)}, u32[]{:S(2)}) copy-start(f32[3,256,256]{2,1,0:T(8,128)S(1)} %pad_maximum_fusion.1.x3.refs_5_) | copy-start | bytes 2359300
  23.1 20.8 %all-to-all-start = ((f32[8,40,256]{2,1,0:T(8,128)}), f32[8,40,256]{2,1,0:T(8,128)S(1)}, u32[]{:S(2)}, u32[]{:S(2)}) async-start(f32[8,40,256]{2,1,0:T(8,128)} %slice_add_fusion.3), calls=%async_computation | async-start | bytes 655360 | tf_op jit(solution)/shard_map/all_to_all | solution.py:262
  43.9 34.4 %copy-start.3 = (f32[3,256,256]{2,1,0:T(8,128)S(1)}, f32[3,256,256]{2,1,0:T(8,128)}, u32[]{:S(2)}) copy-start(f32[3,256,256]{2,1,0:T(8,128)} %copy-done.2) | copy-start | bytes 2359300
  43.9 11.8 %collective-permute-start.4 = (f32[8,256]{1,0:T(8,128)S(1)}, f32[8,256]{1,0:T(8,128)S(1)}, u32[]{:S(2)}, u32[]{:S(2)}) collective-permute-start(f32[8,256]{1,0:T(8,128)S(1)} %slice.103), channel_id=1, source_target_pairs={{1,0},{0,1},{3,2},{2,3},{5,4},{4,5},{7,6},{6,7},{9,8},{8,9},{11,10... | collective-permute-start | bytes 24584 | tf_op jit(solution)/shard_map/ppermute | solution.py:268
  51.9 5.9 %collective-permute-start.3 = (f32[8,256]{1,0:T(8,128)S(1)}, f32[8,256]{1,0:T(8,128)S(1)}, u32[]{:S(2)}, u32[]{:S(2)}) collective-permute-start(f32[8,256]{1,0:T(8,128)S(1)} %slice.103), channel_id=1, source_target_pairs={{0,0},{1,1},{2,2},{3,3},{4,4},{5,5},{6,6},{7,7},{8,8},{9,9},{10,10... | collective-permute-start | bytes 24584 | tf_op jit(solution)/shard_map/ppermute | solution.py:268
  54.4 5.6 %collective-permute-start.2 = (f32[32,256]{1,0:T(8,128)S(1)}, f32[32,256]{1,0:T(8,128)S(1)}, u32[]{:S(2)}, u32[]{:S(2)}) collective-permute-start(f32[32,256]{1,0:T(8,128)S(1)} %slice.102), channel_id=1, source_target_pairs={{0,1},{1,2},{2,3},{3,4},{4,5},{5,6},{6,7},{7,8},{8,9},{9,10},{10,1... | collective-permute-start | bytes 98312 | tf_op jit(solution)/shard_map/ppermute | solution.py:267
  80.6 0.9 copy-start.20
  81.5 2.3 copy-start.16
  81.5 2.3 copy-start.18
  101.6 32.2 %copy-start.17 = (f32[3,256,256]{2,1,0:T(8,128)S(1)}, f32[3,256,256]{2,1,0:T(8,128)}, u32[]{:S(2)}) copy-start(f32[3,256,256]{2,1,0:T(8,128)} %copy-done.16) | copy-start | bytes 2359300
  101.6 10.3 %collective-permute-start.7 = (f32[8,256]{1,0:T(8,128)S(1)}, f32[8,256]{1,0:T(8,128)S(1)}, u32[]{:S(2)}, u32[]{:S(2)}) collective-permute-start(f32[8,256]{1,0:T(8,128)S(1)} %slice.107), channel_id=1, source_target_pairs={{1,0},{0,1},{3,2},{2,3},{5,4},{4,5},{7,6},{6,7},{9,8},{8,9},{11,10... | collective-permute-start | bytes 24584 | tf_op jit(solution)/shard_map/ppermute | solution.py:268
  106.9 5.9 %collective-permute-start.6 = (f32[8,256]{1,0:T(8,128)S(1)}, f32[8,256]{1,0:T(8,128)S(1)}, u32[]{:S(2)}, u32[]{:S(2)}) collective-permute-start(f32[8,256]{1,0:T(8,128)S(1)} %slice.107), channel_id=1, source_target_pairs={{0,0},{1,1},{2,2},{3,3},{4,4},{5,5},{6,6},{7,7},{8,8},{9,9},{10,10... | collective-permute-start | bytes 24584 | tf_op jit(solution)/shard_map/ppermute | solution.py:268
  110.6 4.7 %collective-permute-start.5 = (f32[32,256]{1,0:T(8,128)S(1)}, f32[32,256]{1,0:T(8,128)S(1)}, u32[]{:S(2)}, u32[]{:S(2)}) collective-permute-start(f32[32,256]{1,0:T(8,128)S(1)} %slice.106), channel_id=1, source_target_pairs={{0,1},{1,2},{2,3},{3,4},{4,5},{5,6},{6,7},{7,8},{8,9},{9,10},{10,1... | collective-permute-start | bytes 98312 | tf_op jit(solution)/shard_map/ppermute | solution.py:267
  133.8 1.1 copy-start.19
  135.0 1.1 copy-start.21
  138.5 0.9 copy-start.14
  139.4 2.3 copy-start.10
  139.4 2.3 copy-start.12
  160.5 33.5 %copy-start.11 = (f32[3,256,256]{2,1,0:T(8,128)S(1)}, f32[3,256,256]{2,1,0:T(8,128)}, u32[]{:S(2)}) copy-start(f32[3,256,256]{2,1,0:T(8,128)} %copy-done.10) | copy-start | bytes 2359300
  160.5 9.3 %collective-permute-start.10 = (f32[8,256]{1,0:T(8,128)S(1)}, f32[8,256]{1,0:T(8,128)S(1)}, u32[]{:S(2)}, u32[]{:S(2)}) collective-permute-start(f32[8,256]{1,0:T(8,128)S(1)} %slice.111), channel_id=1, source_target_pairs={{1,0},{0,1},{3,2},{2,3},{5,4},{4,5},{7,6},{6,7},{9,8},{8,9},{11,10... | collective-permute-start | bytes 24584 | tf_op jit(solution)/shard_map/ppermute | solution.py:268
  165.9 6.0 %collective-permute-start.9 = (f32[8,256]{1,0:T(8,128)S(1)}, f32[8,256]{1,0:T(8,128)S(1)}, u32[]{:S(2)}, u32[]{:S(2)}) collective-permute-start(f32[8,256]{1,0:T(8,128)S(1)} %slice.111), channel_id=1, source_target_pairs={{0,0},{1,1},{2,2},{3,3},{4,4},{5,5},{6,6},{7,7},{8,8},{9,9},{10,10... | collective-permute-start | bytes 24584 | tf_op jit(solution)/shard_map/ppermute | solution.py:268
  168.5 5.2 %collective-permute-start.8 = (f32[32,256]{1,0:T(8,128)S(1)}, f32[32,256]{1,0:T(8,128)S(1)}, u32[]{:S(2)}, u32[]{:S(2)}) collective-permute-start(f32[32,256]{1,0:T(8,128)S(1)} %slice.110), channel_id=1, source_target_pairs={{0,1},{1,2},{2,3},{3,4},{4,5},{5,6},{6,7},{7,8},{8,9},{9,10},{10,1... | collective-permute-start | bytes 98312 | tf_op jit(solution)/shard_map/ppermute | solution.py:267
  193.9 1.1 copy-start.13
  195.1 1.1 copy-start.15
  198.7 0.9 copy-start.8
  199.6 2.3 copy-start.4
  199.6 2.3 copy-start.6
  201.9 47.7 %copy-start.9 = (f32[3,256,256]{2,1,0:T(8,128)S(1)}, f32[3,256,256]{2,1,0:T(8,128)}, u32[]{:S(2)}) copy-start(f32[3,256,256]{2,1,0:T(8,128)} %copy-done.8) | copy-start | bytes 2359300
  220.5 29.1 %copy-start.5 = (f32[3,256,256]{2,1,0:T(8,128)S(1)}, f32[3,256,256]{2,1,0:T(8,128)}, u32[]{:S(2)}) copy-start(f32[3,256,256]{2,1,0:T(8,128)} %copy-done.4) | copy-start | bytes 2359300
  220.6 8.4 %collective-permute-start.12 = (f32[8,256]{1,0:T(8,128)S(1)}, f32[8,256]{1,0:T(8,128)S(1)}, u32[]{:S(2)}, u32[]{:S(2)}) collective-permute-start(f32[8,256]{1,0:T(8,128)S(1)} %slice.115), channel_id=1, source_target_pairs={{1,0},{0,1},{3,2},{2,3},{5,4},{4,5},{7,6},{6,7},{9,8},{8,9},{11,10... | collective-permute-start | bytes 24584 | tf_op jit(solution)/shard_map/ppermute | solution.py:268
  224.7 5.9 %collective-permute-start.11 = (f32[8,256]{1,0:T(8,128)S(1)}, f32[8,256]{1,0:T(8,128)S(1)}, u32[]{:S(2)}, u32[]{:S(2)}) collective-permute-start(f32[8,256]{1,0:T(8,128)S(1)} %slice.115), channel_id=1, source_target_pairs={{0,0},{1,1},{2,2},{3,3},{4,4},{5,5},{6,6},{7,7},{8,8},{9,9},{10,10... | collective-permute-start | bytes 24584 | tf_op jit(solution)/shard_map/ppermute | solution.py:268
  249.6 1.1 copy-start.7

commit v2 on v1

v2 whole, which is shorter than its diff:
```python
import math

import jax
import jax.numpy as jnp
import numpy as np
from jax import lax
from jax.experimental import pallas as pl
from jax.experimental.pallas import tpu as pltpu
from jax.sharding import Mesh, PartitionSpec as P

ITERS = 3
ZS, CORES, BLOCKS = 8, 2, 32
GROUP = ZS * CORES
M = 256
PIECE = M // ZS
LANES = M // CORES
ROWS = PIECE * CORES
SCAL = 8
XS = 4
YS = BLOCKS // XS
TERM = ("z", "core")
ALL = ("z", "core", "block")
VMEM = pl.BlockSpec(memory_space=pltpu.VMEM)
SMEM = pl.BlockSpec(memory_space=pltpu.SMEM)
HBM = pl.BlockSpec(memory_space=pltpu.HBM)
BF16, F32 = jnp.bfloat16, jnp.float32


def split(x):
    high = x.astype(BF16)
    return high, (x - high.astype(F32)).astype(BF16)


def dot3(a, b):
    def mm(x, y):
        return lax.dot_general(x, y, (((1,), (0,)), ((), ())), preferred_element_type=F32)

    return mm(a[0], b[0]) + (mm(a[0], b[1]) + mm(a[1], b[0]))


def column_sum(x):
    folded = x[:, :LANES] + x[:, LANES:]
    return jnp.sum(folded, axis=0, keepdims=True)


def apply_terms(info, left, right, t_high, t_low, t_own, v_own, r_own, part):
    total = jnp.zeros((M, M), F32)
    for term in range(left.shape[0]):
        sel = 1 - info[2 + term]
        half = dot3(split(left[term]), (t_high[sel], t_low[sel]))
        total = total + dot3(split(half), split(right[term]))
    size = info[1]
    live = (lax.broadcasted_iota(jnp.int32, (M, M), 0) < size) & (
        lax.broadcasted_iota(jnp.int32, (M, M), 1) < size
    )
    total = jnp.where(live, total, 0.0)
    share = 1.0 / GROUP
    rows = [
        column_sum(t_own * t_own) * share,
        column_sum(t_own * total),
    ]
    if v_own is not None:
        rows += [
            column_sum(v_own * t_own) * share,
            column_sum(t_own * r_own) * share,
            column_sum(v_own * total),
        ]
    rows.append(jnp.zeros((SCAL - len(rows), LANES), F32))
    scal = jnp.concatenate(rows, axis=0)
    for z in range(ZS):
        for core in range(CORES):
            part[z, core * PIECE : (core + 1) * PIECE] = total[
                z * PIECE : (z + 1) * PIECE, core * LANES : (core + 1) * LANES]
        part[z, ROWS:] = scal


def first_kernel(info, left, right, x_own, x_side, part, t_high, t_low):
    t_high[0], t_low[0] = split(x_side[0])
    t_high[1], t_low[1] = split(x_own[...])
    t_high[2], t_low[2] = split(x_side[1])
    apply_terms(info, left, right, t_high, t_low, x_own[...], None, None, part)


def global_sums(info, gathered, row):
    y, x = lax.shift_right_logical(info[0], 2), info[0] & (XS - 1)
    total = None
    for block in range(BLOCKS):
        far = (block % XS - x) & (XS - 1)
        slot = lax.shift_right_logical(far, 1)
        z = (block // XS - y - slot * (YS // 2)) & (YS - 1)
        at = pl.ds(pl.multiple_of(row + SCAL * slot, SCAL), SCAL)
        piece = gathered[CORES * z + (far & 1), at]
        total = piece if total is None else total + piece
    return jnp.sum(total, axis=1, keepdims=True)


def scalars(first, sums, state):
    tt, th = sums[0:1], sums[1:2]
    if first:
        scale = tt + 1e-12
        return None, jnp.sqrt(scale), None, None, None, th / scale, tt / scale, None
    p, tr, vh = sums[2:3], sums[3:4], sums[4:5]
    rho, vv = state[0:1, 0:1], state[1:2, 0:1]
    norm_sq = jnp.maximum(tt - 2.0 * p * p + p * p * vv, 0.0)
    n_sq = norm_sq + 1e-12
    n = jnp.sqrt(n_sq)
    tw = tr + rho * p
    coupling = tr / n
    curvature = (th - p * tw - p * vh + p * p * rho) / n_sq
    lowest = 0.5 * (rho + curvature) - jnp.sqrt((0.5 * (rho - curvature)) ** 2 + coupling * coupling)
    gap = curvature - lowest
    len_sq = gap * gap + coupling * coupling
    length = jnp.sqrt(len_sq)
    v_image = (vh - p * rho) / n
    v_unit = (p - p * vv) / n
    unit_sq = norm_sq / n_sq
    next_rho = (gap * gap * rho - gap * coupling * (v_image + coupling) + coupling * coupling * curvature) / len_sq
    next_vv = (gap * gap * vv - 2.0 * gap * coupling * v_unit + coupling * coupling * unit_sq) / len_sq
    return p, n, gap, coupling, length, next_rho, next_vv, lowest


def combine(first, scal, v, w, t, y):
    p, n, gap, coupling, length = scal[:5]
    if first:
        return t / n, y / n
    by_unit = coupling / (n * length)
    by_old = gap / length + p * by_unit
    return by_old * v - by_unit * t, by_old * w - by_unit * y


def state_rows(first, scal, state, iteration):
    rows = [scal[5], scal[6]]
    for i in range(ITERS):
        if i < iteration - 1:
            rows.append(state[2 + i : 3 + i, 0:1])
        elif i == iteration - 1 and not first:
            rows.append(scal[7])
        else:
            rows.append(jnp.zeros((1, 1), F32))
    rows.append(jnp.zeros((SCAL - len(rows), 1), F32))
    return jnp.broadcast_to(jnp.concatenate(rows, axis=0), (SCAL, 128))


def trial(v, w, diag, rho):
    r = w - rho * v
    return r, r / jnp.maximum(jnp.abs(diag - rho), 1.0)


def copies_in(pairs, sems):
    made = [
        [pltpu.make_async_copy(src, dst, sems.at[i, k]) for k, (src, dst) in enumerate(group)]
        for i, group in enumerate(pairs)
    ]
    for group in made:
        for copy in group:
            copy.start()
    return made


def step_kernel(iteration, kept, *refs):
    first = iteration == 0
    if first:
        (info, left, right, gathered, d_own, d_side, x_own, x_side, state_out, v_out, w_out, part,
         t_high, t_low, d_buf, v_buf, w_buf, in_sems, out_sems) = refs
        state = None
    else:
        (info, left, right, gathered, d_own, d_side, v_in, w_in, state, state_out, v_out, w_out, part,
         t_high, t_low, d_buf, v_buf, w_buf, in_sems, out_sems) = refs

    def side(own, sides, block):
        return own if block == 1 else sides.at[block // 2]

    loads = []
    for block in range(3):
        group = [(side(d_own, d_side, block), d_buf.at[block])]
        if first:
            group.append((side(x_own, x_side, block), v_buf.at[block]))
        else:
            group += [(v_in.at[block], v_buf.at[block]), (w_in.at[block], w_buf.at[block])]
        loads.append(group)
    loads = copies_in(loads, in_sems)

    scal = scalars(first, global_sums(info, gathered, ROWS + PIECE), None if first else state)
    rho = scal[5]
    state_out[...] = state_rows(first, scal, state, iteration)
    old_rho = None if first else state[0:1, 0:1]
    stores = []
    for block in (0, 2, 1):
        for copy in loads[block]:
            copy.wait()
        for z in range(ZS):
            rows = pl.ds(z * PIECE, PIECE)
            if block == 1:
                halves = [gathered[CORES * z + c, ROWS : ROWS + PIECE] for c in range(CORES)]
            else:
                halves = [gathered[CORES * z + block // 2, c * PIECE : (c + 1) * PIECE] for c in range(CORES)]
            image = jnp.concatenate(halves, axis=1)
            diag = d_buf[block, rows]
            if first:
                v, w = combine(True, scal, None, None, v_buf[block, rows], image)
            else:
                v, w = v_buf[block, rows], w_buf[block, rows]
                v, w = combine(False, scal, v, w, trial(v, w, diag, old_rho)[1], image)
            t = trial(v, w, diag, rho)[1]
            v_buf[block, rows] = v
            w_buf[block, rows] = w
            t_high[block, rows], t_low[block, rows] = split(t)
        if block in kept:
            at = kept.index(block)
            for k, (buf, out) in enumerate(((v_buf, v_out), (w_buf, w_out))):
                copy = pltpu.make_async_copy(buf.at[block], out.at[at], out_sems.at[k, at])
                copy.start()
                stores.append(copy)
    v_own = v_buf[1]
    r_own, t_own = trial(v_own, w_buf[1], d_buf[1], rho)
    apply_terms(info, left, right, t_high, t_low, t_own, v_own, r_own, part)
    for copy in stores:
        copy.wait()


def last_kernel(factor, info, gathered, d_own, v_in, w_in, state, wave, image, state_out):
    scal = scalars(False, global_sums(info, gathered, PIECE), state)
    state_out[...] = state_rows(False, scal, state, ITERS)
    old_rho = state[0:1, 0:1]
    for z in range(ZS):
        rows = pl.ds(z * PIECE, PIECE)
        got = jnp.concatenate([gathered[CORES * z + c, :PIECE] for c in range(CORES)], axis=1)
        v, w = v_in[0, rows], w_in[0, rows]
        v, w = combine(False, scal, v, w, trial(v, w, d_own[rows], old_rho)[1], got)
        wave[0, rows] = v * factor
        image[0, rows] = w * factor


def shape(*dims):
    return jax.ShapeDtypeStruct(dims, F32)


PARAMS = pltpu.CompilerParams(vmem_limit_bytes=24 * 1024 * 1024)
SPLITS = [pltpu.VMEM((3, M, M), BF16), pltpu.VMEM((3, M, M), BF16)]
PART = shape(ZS, ROWS + SCAL, LANES)


def run_first(info, left, right, x_own, x_side):
    return pl.pallas_call(
        first_kernel,
        out_shape=PART,
        in_specs=[SMEM] + [VMEM] * 4,
        out_specs=VMEM,
        scratch_shapes=SPLITS,
        compiler_params=PARAMS,
        name="first",
    )(info, left, right, x_own, x_side)


def run_step(iteration, info, left, right, gathered, *arrays):
    kept = (0, 1, 2) if iteration < ITERS - 1 else (1,)

    def body(*refs):
        step_kernel(iteration, kept, *refs)

    state = [] if iteration == 0 else [VMEM]
    return pl.pallas_call(
        body,
        out_shape=(shape(SCAL, 128), shape(len(kept), M, M), shape(len(kept), M, M), PART),
        in_specs=[SMEM] + [VMEM] * 3 + [HBM] * 4 + state,
        out_specs=(VMEM, HBM, HBM, VMEM),
        scratch_shapes=SPLITS + [pltpu.VMEM((3, M, M), F32)] * 3 + [
            pltpu.SemaphoreType.DMA((3, 3)), pltpu.SemaphoreType.DMA((2, 3))],
        compiler_params=PARAMS,
        name="step",
    )(info, left, right, gathered, *arrays)


def run_last(info, *arrays):
    factor = math.sqrt(BLOCKS * M * M)

    def body(*refs):
        last_kernel(factor, *refs)

    return pl.pallas_call(
        body,
        out_shape=(shape(1, M, M), shape(1, M, M), shape(SCAL, 128)),
        in_specs=[SMEM] + [VMEM] * 5,
        out_specs=(VMEM,) * 3,
        compiler_params=PARAMS,
        name="last",
    )(info, *arrays)


def halo_pairs():
    pairs = []
    for z in range(ZS):
        for core in range(CORES):
            for b in range(BLOCKS):
                source = b - 1 if core == 0 else b + 1
                if 0 <= source < BLOCKS:
                    base = (z * CORES + core) * BLOCKS
                    pairs.append((base + source, base + b))
    return pairs


def spread_pairs(slot):
    pairs = []
    for z in range(ZS):
        for core in range(CORES):
            for b in range(BLOCKS):
                y = (b // XS + z + slot * (YS // 2)) % YS
                x = (b % XS + core + 2 * slot) % XS
                base = (z * CORES + core) * BLOCKS
                pairs.append((base + y * XS + x, base + b))
    return pairs


def halo_whole(block):
    got = lax.ppermute(block, ALL, halo_pairs())
    return lax.all_gather(got, "core", axis=0)


def exchange(part, with_halo):
    pieces = lax.all_to_all(part, "z", 0, 0, tiled=True)
    both = lax.all_gather(jnp.sum(pieces, axis=0), "core", axis=0)
    mine = both[0] + both[1]
    rows, scal = mine[:ROWS], mine[ROWS:]
    parts = []
    if with_halo:
        parts.append(lax.ppermute(rows, ALL, halo_pairs()))
    parts.append(lax.dynamic_slice_in_dim(rows, lax.axis_index("core") * PIECE, PIECE, 0))
    parts += [lax.ppermute(scal, ALL, spread_pairs(slot)) for slot in range(2)]
    return lax.all_gather(jnp.concatenate(parts, axis=0), TERM, axis=0)


def per_device(start, diagonal, left_ops, right_ops, offsets, sizes):
    left, right = left_ops[:, 0], right_ops[:, 0]
    info = jnp.concatenate([lax.axis_index("block")[None].astype(jnp.int32), sizes, offsets[:, 0]])
    live = jnp.arange(M, dtype=jnp.int32) < sizes[0]
    x_own = jnp.where(live[:, None] & live[None, :], start[0], 0.0)
    x_side = halo_whole(x_own)
    part = run_first(info, left, right, x_own, x_side)
    d_own = diagonal[0]
    d_side = halo_whole(d_own)
    gathered = exchange(part, True)
    state, v, w, part = run_step(0, info, left, right, gathered, d_own, d_side, x_own, x_side)
    for iteration in range(1, ITERS):
        gathered = exchange(part, True)
        state, v, w, part = run_step(iteration, info, left, right, gathered, d_own, d_side, v, w, state)
    gathered = exchange(part, False)
    wave, image, state = run_last(info, gathered, d_own, v, w, state)
    return wave, image, state[2 : 2 + ITERS, 0]


def solution(mesh):
    grid = Mesh(np.asarray(mesh.devices).reshape(ZS, CORES, BLOCKS), ALL)
    return jax.shard_map(
        per_device,
        mesh=grid,
        in_specs=(
            P("block", None, None),
            P("block", None, None),
            P(TERM, "block", None, None),
            P(TERM, "block", None, None),
            P(TERM, "block"),
            P("block"),
        ),
        out_specs=(P("block", None, None), P("block", None, None), P()),
        check_vma=False,
    )
```

time: 254 us -> 257 us (1.012)
  starting transfers between devices: 49.3 us -> 64.4 us
  blocking collectives: 149 us -> 139 us
  Pallas kernels: 10.6 us -> 13.4 us
    ppermute x8, starting transfers between devices: 35.7 us -> 51 us  [exchange(): parts += [lax.ppermute(scal, ALL, spread_pairs(slot)) for slot in range(2)]]
    ppermute x2, waiting for transfers between devices: 4.25 us -> 12.6 us  [halo_whole(): got = lax.ppermute(block, ALL, halo_pairs())]
    all_to_all x1, waiting for transfers between devices: 10.1 us -> 1.79 us  [exchange(): pieces = lax.all_to_all(part, 'z', 0, 0, tiled=True)]
    ppermute x8, waiting for transfers between devices: 6.66 us -> 1.03 us  [exchange(): parts += [lax.ppermute(scal, ALL, spread_pairs(slot)) for slot in range(2)]]
    all_to_all x3, blocking collectives: 55.1 us -> 49.7 us  [exchange(): pieces = lax.all_to_all(part, 'z', 0, 0, tiled=True)]
    all_gather x4, blocking collectives: 75.9 us -> 70.9 us  [exchange(): return lax.all_gather(jnp.concatenate(parts, axis=0), TERM, axis=0)]
    ppermute x3, waiting for transfers between devices: 6.59 us -> 9.67 us  [exchange(): parts.append(lax.ppermute(rows, ALL, halo_pairs()))]
    pallas_call x5, Pallas kernels: 10.6 us -> 13.4 us  [the longest x3 9.15 us: run_step(): pl.pallas_call(body, out_shape=(shape(SCAL, 128), shape(len(kept), M, M),...]
  transfers between devices with their start and end apart: 14 -> 14, of which waited for: 9 -> 9; matrix products, arithmetic and copies ran while one was open for 1% -> 0% of each run, Pallas kernels for 1% -> 0%
where the time goes in v2:
time: 257 us; the launch traced here: 256 us
  blocking collectives  139 us (54%)
  starting transfers between devices  64.4 us (25%)
  waiting for transfers between devices  25.1 us (10%)
  Pallas kernels  13.4 us (5%)
  local copies, waits for them, and re-layouts  9.24 us (4%)
  other arithmetic  2.88 us (1%)
    all_gather x4, blocking collectives, exchange(): return lax.all_gather(jnp.concatenate(parts, axis=0), TERM, axis=0)  70.9 us
    ppermute x8, starting transfers between devices, exchange(): parts += [lax.ppermute(scal, ALL, spread_pairs(slot)) for slot in range(2)]  51 us
    all_to_all x3, blocking collectives, exchange(): pieces = lax.all_to_all(part, 'z', 0, 0, tiled=True)  49.7 us
    ppermute x2, waiting for transfers between devices, halo_whole(): got = lax.ppermute(block, ALL, halo_pairs())  12.6 us
    ppermute x3, waiting for transfers between devices, exchange(): parts.append(lax.ppermute(rows, ALL, halo_pairs()))  9.67 us
    all_gather x4, blocking collectives, exchange(): both = lax.all_gather(jnp.sum(pieces, axis=0), 'core', axis=0)  9.65 us
    pallas_call x3, Pallas kernels, run_step(): pl.pallas_call(body, out_shape=(shape(SCAL, 128), shape(len(kept), M, M),...  9.15 us
    all_gather x2, blocking collectives, halo_whole(): return lax.all_gather(got, 'core', axis=0)  8.59 us
  transfers between devices with their start and end apart: 14, of which 9 were waited for; matrix products, arithmetic and copies ran while one was open for 0% of the time, Pallas kernels for 0%

profile of v2, /device:TPU:1, one launch (start us, length us, event | category | flops | bytes accessed | tf_op | source)
XLA Modules:
  0.0 255.5 jit_solution(302048509765532959)
XLA Ops:
  1.4 1.1 bitcast_select_fusion.x_own.refs_6_
  2.5 1.3 collective-permute-start
  3.8 0.7 pad_add_fusion.info.refs_0_
  4.5 5.7 %collective-permute-done = f32[256,256]{1,0:T(8,128)S(1)} collective-permute-done((f32[256,256]{1,0:T(8,128)S(1)}, f32[256,256]{1,0:T(8,128)S(1)}, u32[]{:S(2)}, u32[]{:S(2)}) %collective-permute-start) | collective-permute-done | bytes 262176 | tf_op jit(solution)/shard_map/ppermute | solution.py:315
  10.2 6.1 %all-gather = f32[512,256]{1,0:T(8,128)S(1)} all-gather(f32[256,256]{1,0:T(8,128)S(1)} %collective-permute-done), channel_id=2, replica_groups=mesh['z'=8,'core'=2,'block'=32] {'core'}, dimensions={0}, use_global_device_ids=true | all-gather | bytes 786432 | tf_op jit(solution)/shard_map/all_gather | solution.py:316
  16.3 1.2 copy-done.1
  17.5 2.6 %first.1 = f32[8,72,128]{2,1,0:T(8,128)} custom-call(s32[6]{0:T(128)S(1)} %pad_add_fusion.info.refs_0_, f32[4,256,256]{2,1,0:T(8,128)S(1)} %bitcast.45, f32[4,256,256]{2,1,0:T(8,128)S(1)} %bitcast.49, f32[256,256]{1,0:T(8,128)S(1)} %bitcast_select_fusion.x_own.refs_6_, f32[2,256,256]{2,1,0:T(8,128)S(1)} %bitcast.56), custom_call_target="tpu_custom_call" | custom-call | tf_op jit(solution)/shard_map/first/pallas_call | solution.py:244
  20.2 6.9 %all-to-all-start = ((f32[8,72,128]{2,1,0:T(8,128)}), f32[8,72,128]{2,1,0:T(8,128)}, u32[]{:S(2)}, u32[]{:S(2)}) async-start(f32[8,72,128]{2,1,0:T(8,128)} %first.1), calls=%async_computation | async-start | bytes 589824 | tf_op jit(solution)/shard_map/all_to_all | solution.py:320
  27.1 1.3 collective-permute-start.4
  28.4 7.0 %collective-permute-done.4 = f32[256,256]{1,0:T(8,128)S(1)} collective-permute-done((f32[256,256]{1,0:T(8,128)S(1)}, f32[256,256]{1,0:T(8,128)S(1)}, u32[]{:S(2)}, u32[]{:S(2)}) %collective-permute-start.4) | collective-permute-done | bytes 262176 | tf_op jit(solution)/shard_map/ppermute | solution.py:315
  35.3 2.5 all-gather.3
  37.8 1.8 all-to-all-done
  39.6 1.0 reduce_sum.36
  40.6 2.6 %all-gather.1 = f32[144,128]{1,0:T(8,128)S(1)} all-gather(f32[72,128]{1,0:T(8,128)S(1)} %reduce_sum.36), channel_id=3, replica_groups=mesh['z'=8,'core'=2,'block'=32] {'core'}, dimensions={0}, use_global_device_ids=true | all-gather | bytes 110592 | tf_op jit(solution)/shard_map/all_gather | solution.py:321
  43.2 9.4 %collective-permute-start.3 = (f32[8,128]{1,0:T(8,128)S(1)}, f32[8,128]{1,0:T(8,128)S(1)}, u32[]{:S(2)}, u32[]{:S(2)}) collective-permute-start(f32[8,128]{1,0:T(8,128)S(1)} %slice_bitcast_fusion.3), channel_id=1, source_target_pairs={{18,0},{19,1},{16,2},{17,3},{22,4},{23,5},{20,6},{21,7},{26,8},{27... | collective-permute-start | bytes 12296 | tf_op jit(solution)/shard_map/ppermute | solution.py:328
  52.6 7.6 %collective-permute-start.2 = (f32[8,128]{1,0:T(8,128)S(1)}, f32[8,128]{1,0:T(8,128)S(1)}, u32[]{:S(2)}, u32[]{:S(2)}) collective-permute-start(f32[8,128]{1,0:T(8,128)S(1)} %slice_bitcast_fusion.3), channel_id=1, source_target_pairs={{0,0},{1,1},{2,2},{3,3},{4,4},{5,5},{6,6},{7,7},{8,8},{9,9},{10,10... | collective-permute-start | bytes 12296 | tf_op jit(solution)/shard_map/ppermute | solution.py:328
  60.2 1.3 collective-permute-start.1
  61.5 3.3 %collective-permute-done.1 = f32[64,128]{1,0:T(8,128)S(1)} collective-permute-done((f32[64,128]{1,0:T(8,128)S(1)}, f32[64,128]{1,0:T(8,128)S(1)}, u32[]{:S(2)}, u32[]{:S(2)}) %collective-permute-start.1) | collective-permute-done | bytes 32800 | tf_op jit(solution)/shard_map/ppermute | solution.py:326
  64.8 18.3 %all-gather.2 = f32[1792,128]{1,0:T(8,128)S(1)} all-gather(f32[112,128]{1,0:T(8,128)S(1)} %pad_maximum_fusion), channel_id=4, replica_groups=mesh['z'=8,'core'=2,'block'=32] {'z','core'}, dimensions={0}, use_global_device_ids=true | all-gather | bytes 974848 | tf_op jit(solution)/shard_map/all_gather | solution.py:329
  83.1 2.8 %step.3 = (f32[8,128]{1,0:T(8,128)S(1)}, f32[3,256,256]{2,1,0:T(8,128)S(1)}, f32[3,256,256]{2,1,0:T(8,128)S(1)}, f32[8,72,128]{2,1,0:T(8,128)S(1)}) custom-call(s32[6]{0:T(128)S(1)} %pad_add_fusion.info.refs_0_, f32[4,256,256]{2,1,0:T(8,128)S(1)} %bitcast.46, f32[4,256,256]{2,1,0:T(8,128)S(1)} %bitcast.50, f32[16,112,128]{2,1,0:T(8,128)S(1)} %bitcast.65, ...), custom_call_target="tpu_custom_call" | custom-call | tf_op jit(solution)/shard_map/step/pallas_call | solution.py:262
  85.9 0.9 copy-done.10
  86.8 0.9 copy-done.12
  87.7 18.4 %all_to_all.20 = f32[8,72,128]{2,1,0:T(8,128)S(1)} all-to-all(f32[8,72,128]{2,1,0:T(8,128)S(1)} %get-tuple-element.18), channel_id=1, replica_groups=mesh['z'=8,'core'=2,'block'=32] {'z'}, dimensions={0} | all-to-all | bytes 589824 | tf_op jit(solution)/shard_map/all_to_all | solution.py:320
  106.2 2.4 all-gather.4
  108.5 3.1 %collective-permute-start.7 = (f32[8,128]{1,0:T(8,128)S(1)}, f32[8,128]{1,0:T(8,128)S(1)}, u32[]{:S(2)}, u32[]{:S(2)}) collective-permute-start(f32[8,128]{1,0:T(8,128)S(1)} %slice_bitcast_fusion.2), channel_id=1, source_target_pairs={{18,0},{19,1},{16,2},{17,3},{22,4},{23,5},{20,6},{21,7},{26,8},{27... | collective-permute-start | bytes 12296 | tf_op jit(solution)/shard_map/ppermute | solution.py:328
  111.6 5.6 %collective-permute-start.6 = (f32[8,128]{1,0:T(8,128)S(1)}, f32[8,128]{1,0:T(8,128)S(1)}, u32[]{:S(2)}, u32[]{:S(2)}) collective-permute-start(f32[8,128]{1,0:T(8,128)S(1)} %slice_bitcast_fusion.2), channel_id=1, source_target_pairs={{0,0},{1,1},{2,2},{3,3},{4,4},{5,5},{6,6},{7,7},{8,8},{9,9},{10,10... | collective-permute-start | bytes 12296 | tf_op jit(solution)/shard_map/ppermute | solution.py:328
  117.3 1.3 collective-permute-start.5
  118.9 3.0 %collective-permute-done.5 = f32[64,128]{1,0:T(8,128)S(1)} collective-permute-done((f32[64,128]{1,0:T(8,128)S(1)}, f32[64,128]{1,0:T(8,128)S(1)}, u32[]{:S(2)}, u32[]{:S(2)}) %collective-permute-start.5) | collective-permute-done | bytes 32800 | tf_op jit(solution)/shard_map/ppermute | solution.py:326
  121.9 17.3 %all-gather.5 = f32[1792,128]{1,0:T(8,128)S(1)} all-gather(f32[112,128]{1,0:T(8,128)S(1)} %pad_maximum_fusion.1), channel_id=7, replica_groups=mesh['z'=8,'core'=2,'block'=32] {'z','core'}, dimensions={0}, use_global_device_ids=true | all-gather | bytes 974848 | tf_op jit(solution)/shard_map/all_gather | solution.py:329
  139.2 1.1 copy-done.13
  140.3 3.2 %step.4 = (f32[8,128]{1,0:T(8,128)S(1)}, f32[3,256,256]{2,1,0:T(8,128)S(1)}, f32[3,256,256]{2,1,0:T(8,128)S(1)}, f32[8,72,128]{2,1,0:T(8,128)S(1)}) custom-call(s32[6]{0:T(128)S(1)} %pad_add_fusion.info.refs_0_, f32[4,256,256]{2,1,0:T(8,128)S(1)} %bitcast.47, f32[4,256,256]{2,1,0:T(8,128)S(1)} %bitcast.51, f32[16,112,128]{2,1,0:T(8,128)S(1)} %bitcast.64, ...), custom_call_target="tpu_custom_call" | custom-call | tf_op jit(solution)/shard_map/step/pallas_call | solution.py:262
  143.6 0.9 copy-done.6
  144.4 0.9 copy-done.8
  145.3 16.2 %all_to_all.21 = f32[8,72,128]{2,1,0:T(8,128)S(1)} all-to-all(f32[8,72,128]{2,1,0:T(8,128)S(1)} %get-tuple-element.22), channel_id=1, replica_groups=mesh['z'=8,'core'=2,'block'=32] {'z'}, dimensions={0} | all-to-all | bytes 589824 | tf_op jit(solution)/shard_map/all_to_all | solution.py:320
  161.6 2.3 all-gather.6
  163.9 7.3 %collective-permute-start.10 = (f32[8,128]{1,0:T(8,128)S(1)}, f32[8,128]{1,0:T(8,128)S(1)}, u32[]{:S(2)}, u32[]{:S(2)}) collective-permute-start(f32[8,128]{1,0:T(8,128)S(1)} %slice_bitcast_fusion.1), channel_id=1, source_target_pairs={{18,0},{19,1},{16,2},{17,3},{22,4},{23,5},{20,6},{21,7},{26,8},{27... | collective-permute-start | bytes 12296 | tf_op jit(solution)/shard_map/ppermute | solution.py:328
  171.3 8.2 %collective-permute-start.9 = (f32[8,128]{1,0:T(8,128)S(1)}, f32[8,128]{1,0:T(8,128)S(1)}, u32[]{:S(2)}, u32[]{:S(2)}) collective-permute-start(f32[8,128]{1,0:T(8,128)S(1)} %slice_bitcast_fusion.1), channel_id=1, source_target_pairs={{0,0},{1,1},{2,2},{3,3},{4,4},{5,5},{6,6},{7,7},{8,8},{9,9},{10,10... | collective-permute-start | bytes 12296 | tf_op jit(solution)/shard_map/ppermute | solution.py:328
  179.5 1.3 collective-permute-start.8
  180.8 3.3 %collective-permute-done.8 = f32[64,128]{1,0:T(8,128)S(1)} collective-permute-done((f32[64,128]{1,0:T(8,128)S(1)}, f32[64,128]{1,0:T(8,128)S(1)}, u32[]{:S(2)}, u32[]{:S(2)}) %collective-permute-start.8) | collective-permute-done | bytes 32800 | tf_op jit(solution)/shard_map/ppermute | solution.py:326
  184.1 17.0 %all-gather.7 = f32[1792,128]{1,0:T(8,128)S(1)} all-gather(f32[112,128]{1,0:T(8,128)S(1)} %pad_maximum_fusion.2), channel_id=9, replica_groups=mesh['z'=8,'core'=2,'block'=32] {'z','core'}, dimensions={0}, use_global_device_ids=true | all-gather | bytes 974848 | tf_op jit(solution)/shard_map/all_gather | solution.py:329
  201.1 1.1 copy-done.9
  202.2 3.1 %step.5 = (f32[8,128]{1,0:T(8,128)S(1)}, f32[1,256,256]{2,1,0:T(8,128)S(1)}, f32[1,256,256]{2,1,0:T(8,128)S(1)}, f32[8,72,128]{2,1,0:T(8,128)S(1)}) custom-call(s32[6]{0:T(128)S(1)} %pad_add_fusion.info.refs_0_, f32[4,256,256]{2,1,0:T(8,128)S(1)} %bitcast.48, f32[4,256,256]{2,1,0:T(8,128)S(1)} %bitcast.52, f32[16,112,128]{2,1,0:T(8,128)S(1)} %bitcast.63, ...), custom_call_target="tpu_custom_call" | custom-call | tf_op jit(solution)/shard_map/step/pallas_call | solution.py:262
  206.8 15.1 %all_to_all.22 = f32[8,72,128]{2,1,0:T(8,128)S(1)} all-to-all(f32[8,72,128]{2,1,0:T(8,128)S(1)} %get-tuple-element.26), channel_id=1, replica_groups=mesh['z'=8,'core'=2,'block'=32] {'z'}, dimensions={0} | all-to-all | bytes 589824 | tf_op jit(solution)/shard_map/all_to_all | solution.py:320
  221.9 2.3 all-gather.8
  224.2 5.2 %collective-permute-start.12 = (f32[8,128]{1,0:T(8,128)S(1)}, f32[8,128]{1,0:T(8,128)S(1)}, u32[]{:S(2)}, u32[]{:S(2)}) collective-permute-start(f32[8,128]{1,0:T(8,128)S(1)} %slice_bitcast_fusion), channel_id=1, source_target_pairs={{18,0},{19,1},{16,2},{17,3},{22,4},{23,5},{20,6},{21,7},{26,8},{27... | collective-permute-start | bytes 12296 | tf_op jit(solution)/shard_map/ppermute | solution.py:328
  229.5 4.6 %collective-permute-start.11 = (f32[8,128]{1,0:T(8,128)S(1)}, f32[8,128]{1,0:T(8,128)S(1)}, u32[]{:S(2)}, u32[]{:S(2)}) collective-permute-start(f32[8,128]{1,0:T(8,128)S(1)} %slice_bitcast_fusion), channel_id=1, source_target_pairs={{0,0},{1,1},{2,2},{3,3},{4,4},{5,5},{6,6},{7,7},{8,8},{9,9},{10,10... | collective-permute-start | bytes 12296 | tf_op jit(solution)/shard_map/ppermute | solution.py:328
  234.9 18.4 %all-gather.9 = f32[768,128]{1,0:T(8,128)S(1)} all-gather(f32[48,128]{1,0:T(8,128)S(1)} %pad_maximum_fusion.3), channel_id=11, replica_groups=mesh['z'=8,'core'=2,'block'=32] {'z','core'}, dimensions={0}, use_global_device_ids=true | all-gather | bytes 417792 | tf_op jit(solution)/shard_map/all_gather | solution.py:329
  253.3 1.7 last.1
  (62 shorter events, 3.3 us)
Async XLA Ops:
  0.6 15.7 %copy-start = (f32[4,1,256,256]{3,2,1,0:T(8,128)S(1)}, f32[4,1,256,256]{3,2,1,0:T(8,128)}, u32[]{:S(2)}) copy-start(f32[4,1,256,256]{3,2,1,0:T(8,128)} %param.8) | copy-start | bytes 3145732
  2.4 13.9 %copy-start.4 = (f32[256,256]{1,0:T(8,128)}, f32[256,256]{1,0:T(8,128)S(1)}, u32[]{:S(2)}) copy-start(f32[256,256]{1,0:T(8,128)S(1)} %bitcast_select_fusion.x_own.refs_6_) | copy-start | bytes 786436
  2.5 7.7 %collective-permute-start = (f32[256,256]{1,0:T(8,128)S(1)}, f32[256,256]{1,0:T(8,128)S(1)}, u32[]{:S(2)}, u32[]{:S(2)}) collective-permute-start(f32[256,256]{1,0:T(8,128)S(1)} %bitcast_select_fusion.x_own.refs_6_), channel_id=1, source_target_pairs={{0,1},{1,2},{2,3},{3,4},{4,5},{5,6},{6,7},{7,8},{8,9},{9,10},{10,1... | collective-permute-start | bytes 786440 | tf_op jit(solution)/shard_map/ppermute | solution.py:315
  16.3 1.2 copy-start.1
  20.2 6.9 %copy-start.3 = (f32[1,256,256]{2,1,0:T(8,128)S(1)}, f32[1,256,256]{2,1,0:T(8,128)}, u32[]{:S(2)}) copy-start(f32[1,256,256]{2,1,0:T(8,128)} %param.7) | copy-start | bytes 786436
  20.2 19.4 %all-to-all-start = ((f32[8,72,128]{2,1,0:T(8,128)}), f32[8,72,128]{2,1,0:T(8,128)}, u32[]{:S(2)}, u32[]{:S(2)}) async-start(f32[8,72,128]{2,1,0:T(8,128)} %first.1), calls=%async_computation | async-start | bytes 589824 | tf_op jit(solution)/shard_map/all_to_all | solution.py:320
  27.1 8.3 %collective-permute-start.4 = (f32[256,256]{1,0:T(8,128)S(1)}, f32[256,256]{1,0:T(8,128)S(1)}, u32[]{:S(2)}, u32[]{:S(2)}) collective-permute-start(f32[256,256]{1,0:T(8,128)S(1)} %bitcast.58), channel_id=1, source_target_pairs={{0,1},{1,2},{2,3},{3,4},{4,5},{5,6},{6,7},{7,8},{8,9},{9,10},{10,1... | collective-permute-start | bytes 786440 | tf_op jit(solution)/shard_map/ppermute | solution.py:315
  37.8 45.3 %copy-start.2 = (f32[4,1,256,256]{3,2,1,0:T(8,128)S(1)}, f32[4,1,256,256]{3,2,1,0:T(8,128)}, u32[]{:S(2)}) copy-start(f32[4,1,256,256]{3,2,1,0:T(8,128)} %param.9) | copy-start | bytes 3145732
  43.2 18.3 %collective-permute-start.3 = (f32[8,128]{1,0:T(8,128)S(1)}, f32[8,128]{1,0:T(8,128)S(1)}, u32[]{:S(2)}, u32[]{:S(2)}) collective-permute-start(f32[8,128]{1,0:T(8,128)S(1)} %slice_bitcast_fusion.3), channel_id=1, source_target_pairs={{18,0},{19,1},{16,2},{17,3},{22,4},{23,5},{20,6},{21,7},{26,8},{27... | collective-permute-start | bytes 12296 | tf_op jit(solution)/shard_map/ppermute | solution.py:328
  52.6 8.9 %collective-permute-start.2 = (f32[8,128]{1,0:T(8,128)S(1)}, f32[8,128]{1,0:T(8,128)S(1)}, u32[]{:S(2)}, u32[]{:S(2)}) collective-permute-start(f32[8,128]{1,0:T(8,128)S(1)} %slice_bitcast_fusion.3), channel_id=1, source_target_pairs={{0,0},{1,1},{2,2},{3,3},{4,4},{5,5},{6,6},{7,7},{8,8},{9,9},{10,10... | collective-permute-start | bytes 12296 | tf_op jit(solution)/shard_map/ppermute | solution.py:328
  60.2 4.7 %collective-permute-start.1 = (f32[64,128]{1,0:T(8,128)S(1)}, f32[64,128]{1,0:T(8,128)S(1)}, u32[]{:S(2)}, u32[]{:S(2)}) collective-permute-start(f32[64,128]{1,0:T(8,128)S(1)} %get-tuple-element.37), channel_id=1, source_target_pairs={{0,1},{1,2},{2,3},{3,4},{4,5},{5,6},{6,7},{7,8},{8,9},{9,10},{10,1... | collective-permute-start | bytes 98312 | tf_op jit(solution)/shard_map/ppermute | solution.py:326
  64.8 18.3 %copy-start.5 = (f32[256,256]{1,0:T(8,128)S(1)}, f32[256,256]{1,0:T(8,128)}, u32[]{:S(2)}) copy-start(f32[256,256]{1,0:T(8,128)} %copy-done.4) | copy-start | bytes 786436
  85.9 0.9 copy-start.10
  86.8 0.9 copy-start.12
  106.1 33.0 %copy-start.11 = (f32[3,256,256]{2,1,0:T(8,128)S(1)}, f32[3,256,256]{2,1,0:T(8,128)}, u32[]{:S(2)}) copy-start(f32[3,256,256]{2,1,0:T(8,128)} %copy-done.10) | copy-start | bytes 2359300
  108.5 10.4 %collective-permute-start.7 = (f32[8,128]{1,0:T(8,128)S(1)}, f32[8,128]{1,0:T(8,128)S(1)}, u32[]{:S(2)}, u32[]{:S(2)}) collective-permute-start(f32[8,128]{1,0:T(8,128)S(1)} %slice_bitcast_fusion.2), channel_id=1, source_target_pairs={{18,0},{19,1},{16,2},{17,3},{22,4},{23,5},{20,6},{21,7},{26,8},{27... | collective-permute-start | bytes 12296 | tf_op jit(solution)/shard_map/ppermute | solution.py:328
  111.6 7.2 %collective-permute-start.6 = (f32[8,128]{1,0:T(8,128)S(1)}, f32[8,128]{1,0:T(8,128)S(1)}, u32[]{:S(2)}, u32[]{:S(2)}) collective-permute-start(f32[8,128]{1,0:T(8,128)S(1)} %slice_bitcast_fusion.2), channel_id=1, source_target_pairs={{0,0},{1,1},{2,2},{3,3},{4,4},{5,5},{6,6},{7,7},{8,8},{9,9},{10,10... | collective-permute-start | bytes 12296 | tf_op jit(solution)/shard_map/ppermute | solution.py:328
  117.3 4.7 %collective-permute-start.5 = (f32[64,128]{1,0:T(8,128)S(1)}, f32[64,128]{1,0:T(8,128)S(1)}, u32[]{:S(2)}, u32[]{:S(2)}) collective-permute-start(f32[64,128]{1,0:T(8,128)S(1)} %get-tuple-element.35), channel_id=1, source_target_pairs={{0,1},{1,2},{2,3},{3,4},{4,5},{5,6},{6,7},{7,8},{8,9},{9,10},{10,1... | collective-permute-start | bytes 98312 | tf_op jit(solution)/shard_map/ppermute | solution.py:326
  139.2 1.1 copy-start.13
  143.5 0.9 copy-start.6
  144.4 0.9 copy-start.8
  161.6 39.5 %copy-start.7 = (f32[3,256,256]{2,1,0:T(8,128)S(1)}, f32[3,256,256]{2,1,0:T(8,128)}, u32[]{:S(2)}) copy-start(f32[3,256,256]{2,1,0:T(8,128)} %copy-done.6) | copy-start | bytes 2359300
  163.9 16.9 %collective-permute-start.10 = (f32[8,128]{1,0:T(8,128)S(1)}, f32[8,128]{1,0:T(8,128)S(1)}, u32[]{:S(2)}, u32[]{:S(2)}) collective-permute-start(f32[8,128]{1,0:T(8,128)S(1)} %slice_bitcast_fusion.1), channel_id=1, source_target_pairs={{18,0},{19,1},{16,2},{17,3},{22,4},{23,5},{20,6},{21,7},{26,8},{27... | collective-permute-start | bytes 12296 | tf_op jit(solution)/shard_map/ppermute | solution.py:328
  171.3 9.5 %collective-permute-start.9 = (f32[8,128]{1,0:T(8,128)S(1)}, f32[8,128]{1,0:T(8,128)S(1)}, u32[]{:S(2)}, u32[]{:S(2)}) collective-permute-start(f32[8,128]{1,0:T(8,128)S(1)} %slice_bitcast_fusion.1), channel_id=1, source_target_pairs={{0,0},{1,1},{2,2},{3,3},{4,4},{5,5},{6,6},{7,7},{8,8},{9,9},{10,10... | collective-permute-start | bytes 12296 | tf_op jit(solution)/shard_map/ppermute | solution.py:328
  179.5 4.7 %collective-permute-start.8 = (f32[64,128]{1,0:T(8,128)S(1)}, f32[64,128]{1,0:T(8,128)S(1)}, u32[]{:S(2)}, u32[]{:S(2)}) collective-permute-start(f32[64,128]{1,0:T(8,128)S(1)} %get-tuple-element.33), channel_id=1, source_target_pairs={{0,1},{1,2},{2,3},{3,4},{4,5},{5,6},{6,7},{7,8},{8,9},{9,10},{10,1... | collective-permute-start | bytes 98312 | tf_op jit(solution)/shard_map/ppermute | solution.py:326
  201.1 1.1 copy-start.9
  205.4 0.7 copy-start.14
  206.1 0.7 copy-start.16
  224.2 29.0 %copy-start.17 = (f32[1,256,256]{2,1,0:T(8,128)S(1)}, f32[1,256,256]{2,1,0:T(8,128)}, u32[]{:S(2)}) copy-start(f32[1,256,256]{2,1,0:T(8,128)} %copy-done.16) | copy-start | bytes 786436
  224.2 29.0 %copy-start.15 = (f32[1,256,256]{2,1,0:T(8,128)S(1)}, f32[1,256,256]{2,1,0:T(8,128)}, u32[]{:S(2)}) copy-start(f32[1,256,256]{2,1,0:T(8,128)} %copy-done.14) | copy-start | bytes 786436
  224.2 10.5 %collective-permute-start.12 = (f32[8,128]{1,0:T(8,128)S(1)}, f32[8,128]{1,0:T(8,128)S(1)}, u32[]{:S(2)}, u32[]{:S(2)}) collective-permute-start(f32[8,128]{1,0:T(8,128)S(1)} %slice_bitcast_fusion), channel_id=1, source_target_pairs={{18,0},{19,1},{16,2},{17,3},{22,4},{23,5},{20,6},{21,7},{26,8},{27... | collective-permute-start | bytes 12296 | tf_op jit(solution)/shard_map/ppermute | solution.py:328
  229.5 5.4 %collective-permute-start.11 = (f32[8,128]{1,0:T(8,128)S(1)}, f32[8,128]{1,0:T(8,128)S(1)}, u32[]{:S(2)}, u32[]{:S(2)}) collective-permute-start(f32[8,128]{1,0:T(8,128)S(1)} %slice_bitcast_fusion), channel_id=1, source_target_pairs={{0,0},{1,1},{2,2},{3,3},{4,4},{5,5},{6,6},{7,7},{8,8},{9,9},{10,10... | collective-permute-start | bytes 12296 | tf_op jit(solution)/shard_map/ppermute | solution.py:328

commit v3 on v2

--- a/solution.py
+++ b/solution.py
@@ -22,7 +22,6 @@
 ALL = ("z", "core", "block")
 VMEM = pl.BlockSpec(memory_space=pltpu.VMEM)
 SMEM = pl.BlockSpec(memory_space=pltpu.SMEM)
-HBM = pl.BlockSpec(memory_space=pltpu.HBM)
 BF16, F32 = jnp.bfloat16, jnp.float32
 
 
@@ -74,11 +73,11 @@
         part[z, ROWS:] = scal
 
 
-def first_kernel(info, left, right, x_own, x_side, part, t_high, t_low):
+def first_kernel(info, left, right, own, x_side, part, t_high, t_low):
     t_high[0], t_low[0] = split(x_side[0])
-    t_high[1], t_low[1] = split(x_own[...])
+    t_high[1], t_low[1] = split(own[0])
     t_high[2], t_low[2] = split(x_side[1])
-    apply_terms(info, left, right, t_high, t_low, x_own[...], None, None, part)
+    apply_terms(info, left, right, t_high, t_low, own[0], None, None, part)
 
 
 def global_sums(info, gathered, row):
@@ -146,87 +145,52 @@
     return r, r / jnp.maximum(jnp.abs(diag - rho), 1.0)
 
 
-def copies_in(pairs, sems):
-    made = [
-        [pltpu.make_async_copy(src, dst, sems.at[i, k]) for k, (src, dst) in enumerate(group)]
-        for i, group in enumerate(pairs)
-    ]
-    for group in made:
-        for copy in group:
-            copy.start()
-    return made
-
-
-def step_kernel(iteration, kept, *refs):
+def step_kernel(iteration, *refs):
     first = iteration == 0
     if first:
-        (info, left, right, gathered, d_own, d_side, x_own, x_side, state_out, v_out, w_out, part,
-         t_high, t_low, d_buf, v_buf, w_buf, in_sems, out_sems) = refs
-        state = None
+        (info, left, right, gathered, own, x_side, d_side, state_out, out, part, t_high, t_low) = refs
+        old = state = None
     else:
-        (info, left, right, gathered, d_own, d_side, v_in, w_in, state, state_out, v_out, w_out, part,
-         t_high, t_low, d_buf, v_buf, w_buf, in_sems, out_sems) = refs
-
-    def side(own, sides, block):
-        return own if block == 1 else sides.at[block // 2]
-
-    loads = []
-    for block in range(3):
-        group = [(side(d_own, d_side, block), d_buf.at[block])]
-        if first:
-            group.append((side(x_own, x_side, block), v_buf.at[block]))
-        else:
-            group += [(v_in.at[block], v_buf.at[block]), (w_in.at[block], w_buf.at[block])]
-        loads.append(group)
-    loads = copies_in(loads, in_sems)
-
+        (info, left, right, gathered, own, x_side, d_side, old, state, state_out, out, part, t_high, t_low) = refs
     scal = scalars(first, global_sums(info, gathered, ROWS + PIECE), None if first else state)
     rho = scal[5]
     state_out[...] = state_rows(first, scal, state, iteration)
     old_rho = None if first else state[0:1, 0:1]
-    stores = []
     for block in (0, 2, 1):
-        for copy in loads[block]:
-            copy.wait()
         for z in range(ZS):
             rows = pl.ds(z * PIECE, PIECE)
             if block == 1:
                 halves = [gathered[CORES * z + c, ROWS : ROWS + PIECE] for c in range(CORES)]
+                x, diag = own[0, rows], own[1, rows]
             else:
                 halves = [gathered[CORES * z + block // 2, c * PIECE : (c + 1) * PIECE] for c in range(CORES)]
+                x, diag = x_side[block // 2, rows], d_side[block // 2, rows]
             image = jnp.concatenate(halves, axis=1)
-            diag = d_buf[block, rows]
             if first:
-                v, w = combine(True, scal, None, None, v_buf[block, rows], image)
+                v, w = combine(True, scal, None, None, x, image)
             else:
-                v, w = v_buf[block, rows], w_buf[block, rows]
+                v, w = old[block, rows], old[3 + block, rows]
                 v, w = combine(False, scal, v, w, trial(v, w, diag, old_rho)[1], image)
             t = trial(v, w, diag, rho)[1]
-            v_buf[block, rows] = v
-            w_buf[block, rows] = w
+            out[block, rows] = v
+            out[3 + block, rows] = w
             t_high[block, rows], t_low[block, rows] = split(t)
-        if block in kept:
-            at = kept.index(block)
-            for k, (buf, out) in enumerate(((v_buf, v_out), (w_buf, w_out))):
-                copy = pltpu.make_async_copy(buf.at[block], out.at[at], out_sems.at[k, at])
-                copy.start()
-                stores.append(copy)
-    v_own = v_buf[1]
-    r_own, t_own = trial(v_own, w_buf[1], d_buf[1], rho)
+    v_own = out[1]
+    r_own, t_own = trial(v_own, out[4], own[1], rho)
     apply_terms(info, left, right, t_high, t_low, t_own, v_own, r_own, part)
-    for copy in stores:
-        copy.wait()
-
-
-def last_kernel(factor, info, gathered, d_own, v_in, w_in, state, wave, image, state_out):
+
+
+def last_kernel(factor, info, gathered, own, old, state, wave, image, energies):
     scal = scalars(False, global_sums(info, gathered, PIECE), state)
-    state_out[...] = state_rows(False, scal, state, ITERS)
+    rows = state_rows(False, scal, state, ITERS)
+    for i in range(ITERS):
+        energies[i] = rows[2 + i, 0]
     old_rho = state[0:1, 0:1]
     for z in range(ZS):
         rows = pl.ds(z * PIECE, PIECE)
         got = jnp.concatenate([gathered[CORES * z + c, :PIECE] for c in range(CORES)], axis=1)
-        v, w = v_in[0, rows], w_in[0, rows]
-        v, w = combine(False, scal, v, w, trial(v, w, d_own[rows], old_rho)[1], got)
+        v, w = old[1, rows], old[4, rows]
+        v, w = combine(False, scal, v, w, trial(v, w, own[1, rows], old_rho)[1], got)
         wave[0, rows] = v * factor
         image[0, rows] = w * factor
 
@@ -235,12 +199,12 @@
     return jax.ShapeDtypeStruct(dims, F32)
 
 
-PARAMS = pltpu.CompilerParams(vmem_limit_bytes=24 * 1024 * 1024)
+PARAMS = pltpu.CompilerParams(vmem_limit_bytes=16 * 1024 * 1024)
 SPLITS = [pltpu.VMEM((3, M, M), BF16), pltpu.VMEM((3, M, M), BF16)]
 PART = shape(ZS, ROWS + SCAL, LANES)
 
 
-def run_first(info, left, right, x_own, x_side):
+def run_first(info, left, right, own, x_side):
     return pl.pallas_call(
         first_kernel,
         out_shape=PART,
@@ -249,26 +213,23 @@
         scratch_shapes=SPLITS,
         compiler_params=PARAMS,
         name="first",
-    )(info, left, right, x_own, x_side)
-
-
-def run_step(iteration, info, left, right, gathered, *arrays):
-    kept = (0, 1, 2) if iteration < ITERS - 1 else (1,)
-
+    )(info, left, right, own, x_side)
+
+
+def run_step(iteration, info, *arrays):
     def body(*refs):
-        step_kernel(iteration, kept, *refs)
-
-    state = [] if iteration == 0 else [VMEM]
+        step_kernel(iteration, *refs)
+
     return pl.pallas_call(
         body,
-        out_shape=(shape(SCAL, 128), shape(len(kept), M, M), shape(len(kept), M, M), PART),
-        in_specs=[SMEM] + [VMEM] * 3 + [HBM] * 4 + state,
-        out_specs=(VMEM, HBM, HBM, VMEM),
-        scratch_shapes=SPLITS + [pltpu.VMEM((3, M, M), F32)] * 3 + [
-            pltpu.SemaphoreType.DMA((3, 3)), pltpu.SemaphoreType.DMA((2, 3))],
+        out_shape=(shape(SCAL, 128), shape(6, M, M), PART),
+        in_specs=[SMEM] + [VMEM] * len(arrays),
+        out_specs=(VMEM,) * 3,
+        scratch_shapes=SPLITS,
+        input_output_aliases={7: 1} if iteration else {},
         compiler_params=PARAMS,
         name="step",
-    )(info, left, right, gathered, *arrays)
+    )(info, *arrays)
 
 
 def run_last(info, *arrays):
@@ -279,9 +240,9 @@
 
     return pl.pallas_call(
         body,
-        out_shape=(shape(1, M, M), shape(1, M, M), shape(SCAL, 128)),
-        in_specs=[SMEM] + [VMEM] * 5,
-        out_specs=(VMEM,) * 3,
+        out_shape=(shape(1, M, M), shape(1, M, M), shape(ITERS)),
+        in_specs=[SMEM] + [VMEM] * 4,
+        out_specs=(VMEM, VMEM, SMEM),
         compiler_params=PARAMS,
         name="last",
     )(info, *arrays)
@@ -311,14 +272,14 @@
     return pairs
 
 
-def halo_whole(block):
-    got = lax.ppermute(block, ALL, halo_pairs())
-    return lax.all_gather(got, "core", axis=0)
+def halo_whole(blocks):
+    got = lax.ppermute(blocks, ALL, halo_pairs())
+    return [lax.all_gather(got[i], "core", axis=0) for i in range(2)]
 
 
 def exchange(part, with_halo):
     pieces = lax.all_to_all(part, "z", 0, 0, tiled=True)
-    both = lax.all_gather(jnp.sum(pieces, axis=0), "core", axis=0)
+    both = lax.all_gather(sum(pieces[z] for z in range(1, ZS)) + pieces[0], "core", axis=0)
     mine = both[0] + both[1]
     rows, scal = mine[:ROWS], mine[ROWS:]
     parts = []
@@ -333,19 +294,17 @@
     left, right = left_ops[:, 0], right_ops[:, 0]
     info = jnp.concatenate([lax.axis_index("block")[None].astype(jnp.int32), sizes, offsets[:, 0]])
     live = jnp.arange(M, dtype=jnp.int32) < sizes[0]
-    x_own = jnp.where(live[:, None] & live[None, :], start[0], 0.0)
-    x_side = halo_whole(x_own)
-    part = run_first(info, left, right, x_own, x_side)
-    d_own = diagonal[0]
-    d_side = halo_whole(d_own)
+    own = jnp.stack([jnp.where(live[:, None] & live[None, :], start[0], 0.0), diagonal[0]])
+    x_side, d_side = halo_whole(own)
+    part = run_first(info, left, right, own, x_side)
     gathered = exchange(part, True)
-    state, v, w, part = run_step(0, info, left, right, gathered, d_own, d_side, x_own, x_side)
+    state, pair, part = run_step(0, info, left, right, gathered, own, x_side, d_side)
     for iteration in range(1, ITERS):
         gathered = exchange(part, True)
-        state, v, w, part = run_step(iteration, info, left, right, gathered, d_own, d_side, v, w, state)
+        state, pair, part = run_step(iteration, info, left, right, gathered, own, x_side, d_side, pair, state)
     gathered = exchange(part, False)
-    wave, image, state = run_last(info, gathered, d_own, v, w, state)
-    return wave, image, state[2 : 2 + ITERS, 0]
+    wave, image, energies = run_last(info, gathered, own, pair, state)
+    return wave, image, energies
 
 
 def solution(mesh):

time: 257 us -> 244 us (0.949)
  local copies, waits for them, and re-layouts: 9.24 us -> 0.85 us
  blocking collectives: 139 us -> 134 us
    unnamed x36 -> x8, local copies, waits for them, and re-layouts: 8.53 us -> 0.02 us
    all_to_all x1, waiting for transfers between devices: 1.79 us -> 6.8 us  [exchange(): pieces = lax.all_to_all(part, 'z', 0, 0, tiled=True)]
    all_to_all x3, blocking collectives: 49.7 us -> 45.2 us  [exchange(): pieces = lax.all_to_all(part, 'z', 0, 0, tiled=True)]
    all_gather x4, blocking collectives: 70.9 us -> 66.8 us  [exchange(): return lax.all_gather(jnp.concatenate(parts, axis=0), TERM, axis=0)]
    ppermute x2 -> x1, waiting for transfers between devices: 12.6 us -> 9.12 us  [halo_whole(): got = lax.ppermute(blocks, ALL, halo_pairs())]
    ppermute x8, starting transfers between devices: 51 us -> 54.4 us  [exchange(): parts += [lax.ppermute(scal, ALL, spread_pairs(slot)) for slot in range(2)]]
    all_gather x6, blocking collectives: 18.2 us -> 21.6 us  [the longest x2 11.7 us: halo_whole(): return [lax.all_gather(got[i], 'core', axis=0) for i in range(2)]]
  transfers between devices with their start and end apart: 14 -> 13, of which waited for: 9 -> 6; matrix products, arithmetic and copies ran while one was open for 0% -> 0% of each run, Pallas kernels for 0% -> 0%
where the time goes in v3:
time: 244 us; the launch traced here: 243 us
  blocking collectives  134 us (55%)
  starting transfers between devices  66.3 us (27%)
  waiting for transfers between devices  26.9 us (11%)
  Pallas kernels  11.9 us (5%)
    all_gather x4, blocking collectives, exchange(): return lax.all_gather(jnp.concatenate(parts, axis=0), TERM, axis=0)  66.8 us
    ppermute x8, starting transfers between devices, exchange(): parts += [lax.ppermute(scal, ALL, spread_pairs(slot)) for slot in range(2)]  54.4 us
    all_to_all x3, blocking collectives, exchange(): pieces = lax.all_to_all(part, 'z', 0, 0, tiled=True)  45.2 us
    all_gather x2, blocking collectives, halo_whole(): return [lax.all_gather(got[i], 'core', axis=0) for i in range(2)]  11.7 us
    ppermute x3, waiting for transfers between devices, exchange(): parts.append(lax.ppermute(rows, ALL, halo_pairs()))  10.3 us
    all_gather x4, blocking collectives, exchange(): lax.all_gather(sum((pieces[z] for z in range(1, ZS))) + pieces[0], 'core'...  9.82 us
    ppermute x1, waiting for transfers between devices, halo_whole(): got = lax.ppermute(blocks, ALL, halo_pairs())  9.12 us
    pallas_call x3, Pallas kernels, run_step(): pl.pallas_call(body, out_shape=(shape(SCAL, 128), shape(6, M, M), PART),...  7.59 us
  transfers between devices with their start and end apart: 13, of which 6 were waited for; matrix products, arithmetic and copies ran while one was open for 0% of the time, Pallas kernels for 0%

profile of v3, /device:TPU:1, one launch (start us, length us, event | category | flops | bytes accessed | tf_op | source)
XLA Modules:
  0.0 243.5 jit_solution(15910918774114523061)
XLA Ops:
  1.3 1.1 and_select_fusion
  2.4 0.0 copy-start
  2.4 0.0 copy-start.1
  2.4 1.1 pad_maximum_fusion.own.refs_4_.refs_2_
  3.5 1.3 collective-permute-start
  4.8 0.1 pad_add_fusion.info.refs_0_
  4.9 9.1 %collective-permute-done = f32[2,256,256]{2,1,0:T(8,128)S(1)} collective-permute-done((f32[2,256,256]{2,1,0:T(8,128)S(1)}, f32[2,256,256]{2,1,0:T(8,128)S(1)}, u32[]{:S(2)}, u32[]{:S(2)}) %collective-permute-start) | collective-permute-done | bytes 524320 | tf_op jit(solution)/shard_map/ppermute | solution.py:276
  14.0 0.7 fusion
  14.8 6.1 %all_gather.46.x_side.refs_5_ = f32[2,256,256]{2,1,0:T(8,128)S(1)} all-gather(f32[1,256,256]{2,1,0:T(8,128)S(1)} %get-tuple-element.22), channel_id=1, replica_groups=mesh['z'=8,'core'=2,'block'=32] {'core'}, dimensions={0}, use_global_device_ids=true | all-gather | bytes 786432 | tf_op jit(solution)/shard_map/all_gather | solution.py:277
  20.9 2.6 %first.1 = f32[8,72,128]{2,1,0:T(8,128)} custom-call(s32[6]{0:T(128)S(1)} %pad_add_fusion.info.refs_0_, f32[4,256,256]{2,1,0:T(8,128)S(1)} %bitcast.32, f32[4,256,256]{2,1,0:T(8,128)S(1)} %bitcast.36, f32[2,256,256]{2,1,0:T(8,128)S(1)} %pad_maximum_fusion.own.refs_4_.refs_2_, f32[2,256,256]{2,1,0:T(8,128)S(1)} %all_gather.46.x_side.refs_5_), custom_call_target="tpu_custom_call" | custom-call | tf_op jit(solution)/shard_map/first/pallas_call | solution.py:208
  23.5 6.8 %all-to-all-start = ((f32[8,72,128]{2,1,0:T(8,128)}), f32[8,72,128]{2,1,0:T(8,128)S(1)}, u32[]{:S(2)}, u32[]{:S(2)}) async-start(f32[8,72,128]{2,1,0:T(8,128)} %first.1), calls=%async_computation | async-start | bytes 589824 | tf_op jit(solution)/shard_map/all_to_all | solution.py:281
  30.3 5.6 %all_gather.50.refs_6_ = f32[2,256,256]{2,1,0:T(8,128)} all-gather(f32[1,256,256]{2,1,0:T(8,128)} %get-tuple-element.21), channel_id=1, replica_groups=mesh['z'=8,'core'=2,'block'=32] {'core'}, dimensions={0}, use_global_device_ids=true | all-gather | bytes 786432 | tf_op jit(solution)/shard_map/all_gather | solution.py:277
  35.9 6.8 %all-to-all-done = f32[8,72,128]{2,1,0:T(8,128)S(1)} async-done(((f32[8,72,128]{2,1,0:T(8,128)}), f32[8,72,128]{2,1,0:T(8,128)S(1)}, u32[]{:S(2)}, u32[]{:S(2)}) %all-to-all-start) | async-done | bytes 294944 | tf_op jit(solution)/shard_map/all_to_all | solution.py:281
  42.7 2.8 %all_gather.47 = f32[2,72,128]{2,1,0:T(8,128)S(1)} all-gather(f32[1,72,128]{2,1,0:T(8,128)S(1)} %slice_add_fusion.25), channel_id=1, replica_groups=mesh['z'=8,'core'=2,'block'=32] {'core'}, dimensions={0}, use_global_device_ids=true | all-gather | bytes 110592 | tf_op jit(solution)/shard_map/all_gather | solution.py:282
  45.5 9.4 %collective-permute-start.3 = (f32[8,128]{1,0:T(8,128)S(1)}, f32[8,128]{1,0:T(8,128)S(1)}, u32[]{:S(2)}, u32[]{:S(2)}) collective-permute-start(f32[8,128]{1,0:T(8,128)S(1)} %slice_bitcast_fusion.3), channel_id=1, source_target_pairs={{18,0},{19,1},{16,2},{17,3},{22,4},{23,5},{20,6},{21,7},{26,8},{27... | collective-permute-start | bytes 12296 | tf_op jit(solution)/shard_map/ppermute | solution.py:289
  54.9 6.7 %collective-permute-start.2 = (f32[8,128]{1,0:T(8,128)S(1)}, f32[8,128]{1,0:T(8,128)S(1)}, u32[]{:S(2)}, u32[]{:S(2)}) collective-permute-start(f32[8,128]{1,0:T(8,128)S(1)} %slice_bitcast_fusion.3), channel_id=1, source_target_pairs={{0,0},{1,1},{2,2},{3,3},{4,4},{5,5},{6,6},{7,7},{8,8},{9,9},{10,10... | collective-permute-start | bytes 12296 | tf_op jit(solution)/shard_map/ppermute | solution.py:289
  61.6 1.3 collective-permute-start.1
  62.9 0.0 collective-permute-done.3
  62.9 0.0 collective-permute-done.2
  63.0 3.3 %collective-permute-done.1 = f32[64,128]{1,0:T(8,128)S(1)} collective-permute-done((f32[64,128]{1,0:T(8,128)S(1)}, f32[64,128]{1,0:T(8,128)S(1)}, u32[]{:S(2)}, u32[]{:S(2)}) %collective-permute-start.1) | collective-permute-done | bytes 32800 | tf_op jit(solution)/shard_map/ppermute | solution.py:287
  66.3 17.0 %all-gather = f32[1792,128]{1,0:T(8,128)S(1)} all-gather(f32[112,128]{1,0:T(8,128)S(1)} %pad_maximum_fusion.1), channel_id=2, replica_groups=mesh['z'=8,'core'=2,'block'=32] {'z','core'}, dimensions={0}, use_global_device_ids=true | all-gather | bytes 974848 | tf_op jit(solution)/shard_map/all_gather | solution.py:290
  83.3 2.3 step.3
  85.6 15.1 %all_to_all.20 = f32[8,72,128]{2,1,0:T(8,128)S(1)} all-to-all(f32[8,72,128]{2,1,0:T(8,128)S(1)} %get-tuple-element.12), channel_id=1, replica_groups=mesh['z'=8,'core'=2,'block'=32] {'z'}, dimensions={0} | all-to-all | bytes 589824 | tf_op jit(solution)/shard_map/all_to_all | solution.py:281
  100.6 2.3 all_gather.51
  103.0 5.1 %collective-permute-start.6 = (f32[8,128]{1,0:T(8,128)S(1)}, f32[8,128]{1,0:T(8,128)S(1)}, u32[]{:S(2)}, u32[]{:S(2)}) collective-permute-start(f32[8,128]{1,0:T(8,128)S(1)} %slice_bitcast_fusion.2), channel_id=1, source_target_pairs={{18,0},{19,1},{16,2},{17,3},{22,4},{23,5},{20,6},{21,7},{26,8},{27... | collective-permute-start | bytes 12296 | tf_op jit(solution)/shard_map/ppermute | solution.py:289
  108.1 6.9 %collective-permute-start.5 = (f32[8,128]{1,0:T(8,128)S(1)}, f32[8,128]{1,0:T(8,128)S(1)}, u32[]{:S(2)}, u32[]{:S(2)}) collective-permute-start(f32[8,128]{1,0:T(8,128)S(1)} %slice_bitcast_fusion.2), channel_id=1, source_target_pairs={{0,0},{1,1},{2,2},{3,3},{4,4},{5,5},{6,6},{7,7},{8,8},{9,9},{10,10... | collective-permute-start | bytes 12296 | tf_op jit(solution)/shard_map/ppermute | solution.py:289
  115.1 1.3 collective-permute-start.4
  116.4 0.0 collective-permute-done.6
  116.4 3.3 %collective-permute-done.4 = f32[64,128]{1,0:T(8,128)S(1)} collective-permute-done((f32[64,128]{1,0:T(8,128)S(1)}, f32[64,128]{1,0:T(8,128)S(1)}, u32[]{:S(2)}, u32[]{:S(2)}) %collective-permute-start.4) | collective-permute-done | bytes 32800 | tf_op jit(solution)/shard_map/ppermute | solution.py:287
  119.8 17.0 %all-gather.1 = f32[1792,128]{1,0:T(8,128)S(1)} all-gather(f32[112,128]{1,0:T(8,128)S(1)} %pad_maximum_fusion.2), channel_id=3, replica_groups=mesh['z'=8,'core'=2,'block'=32] {'z','core'}, dimensions={0}, use_global_device_ids=true | all-gather | bytes 974848 | tf_op jit(solution)/shard_map/all_gather | solution.py:290
  136.7 2.6 %step.4 = (f32[8,128]{1,0:T(8,128)S(1)}, f32[6,256,256]{2,1,0:T(8,128)S(1)}, f32[8,72,128]{2,1,0:T(8,128)S(1)}) custom-call(s32[6]{0:T(128)S(1)} %pad_add_fusion.info.refs_0_, f32[4,256,256]{2,1,0:T(8,128)S(1)} %bitcast.34, f32[4,256,256]{2,1,0:T(8,128)S(1)} %bitcast.38, f32[16,112,128]{2,1,0:T(8,128)S(1)} %bitcast.42, ...), custom_call_target="tpu_custom_call", output_to_operand_aliasing={{1}: (7, {})} | custom-call | tf_op jit(solution)/shard_map/step/pallas_call | solution.py:223
  139.4 15.1 %all_to_all.21 = f32[8,72,128]{2,1,0:T(8,128)S(1)} all-to-all(f32[8,72,128]{2,1,0:T(8,128)S(1)} %get-tuple-element.15), channel_id=1, replica_groups=mesh['z'=8,'core'=2,'block'=32] {'z'}, dimensions={0} | all-to-all | bytes 589824 | tf_op jit(solution)/shard_map/all_to_all | solution.py:281
  154.5 2.3 all_gather.54
  156.8 6.1 %collective-permute-start.9 = (f32[8,128]{1,0:T(8,128)S(1)}, f32[8,128]{1,0:T(8,128)S(1)}, u32[]{:S(2)}, u32[]{:S(2)}) collective-permute-start(f32[8,128]{1,0:T(8,128)S(1)} %slice_bitcast_fusion.1), channel_id=1, source_target_pairs={{18,0},{19,1},{16,2},{17,3},{22,4},{23,5},{20,6},{21,7},{26,8},{27... | collective-permute-start | bytes 12296 | tf_op jit(solution)/shard_map/ppermute | solution.py:289
  162.9 8.2 %collective-permute-start.8 = (f32[8,128]{1,0:T(8,128)S(1)}, f32[8,128]{1,0:T(8,128)S(1)}, u32[]{:S(2)}, u32[]{:S(2)}) collective-permute-start(f32[8,128]{1,0:T(8,128)S(1)} %slice_bitcast_fusion.1), channel_id=1, source_target_pairs={{0,0},{1,1},{2,2},{3,3},{4,4},{5,5},{6,6},{7,7},{8,8},{9,9},{10,10... | collective-permute-start | bytes 12296 | tf_op jit(solution)/shard_map/ppermute | solution.py:289
  171.1 1.3 collective-permute-start.7
  172.4 0.0 collective-permute-done.9
  172.4 0.0 collective-permute-done.8
  172.5 3.6 %collective-permute-done.7 = f32[64,128]{1,0:T(8,128)S(1)} collective-permute-done((f32[64,128]{1,0:T(8,128)S(1)}, f32[64,128]{1,0:T(8,128)S(1)}, u32[]{:S(2)}, u32[]{:S(2)}) %collective-permute-start.7) | collective-permute-done | bytes 32800 | tf_op jit(solution)/shard_map/ppermute | solution.py:287
  176.1 17.0 %all-gather.2 = f32[1792,128]{1,0:T(8,128)S(1)} all-gather(f32[112,128]{1,0:T(8,128)S(1)} %pad_maximum_fusion.3), channel_id=4, replica_groups=mesh['z'=8,'core'=2,'block'=32] {'z','core'}, dimensions={0}, use_global_device_ids=true | all-gather | bytes 974848 | tf_op jit(solution)/shard_map/all_gather | solution.py:290
  193.0 2.7 %step.5 = (f32[8,128]{1,0:T(8,128)S(1)}, f32[6,256,256]{2,1,0:T(8,128)S(1)}, f32[8,72,128]{2,1,0:T(8,128)S(1)}) custom-call(s32[6]{0:T(128)S(1)} %pad_add_fusion.info.refs_0_, f32[4,256,256]{2,1,0:T(8,128)S(1)} %bitcast.35, f32[4,256,256]{2,1,0:T(8,128)S(1)} %bitcast.39, f32[16,112,128]{2,1,0:T(8,128)S(1)} %bitcast.41, ...), custom_call_target="tpu_custom_call", output_to_operand_aliasing={{1}: (7, {})} | custom-call | tf_op jit(solution)/shard_map/step/pallas_call | solution.py:223
  195.7 15.1 %all_to_all.22 = f32[8,72,128]{2,1,0:T(8,128)S(1)} all-to-all(f32[8,72,128]{2,1,0:T(8,128)S(1)} %get-tuple-element.18), channel_id=1, replica_groups=mesh['z'=8,'core'=2,'block'=32] {'z'}, dimensions={0} | all-to-all | bytes 589824 | tf_op jit(solution)/shard_map/all_to_all | solution.py:281
  210.8 2.3 all_gather.57
  213.2 4.8 %collective-permute-start.11 = (f32[8,128]{1,0:T(8,128)S(1)}, f32[8,128]{1,0:T(8,128)S(1)}, u32[]{:S(2)}, u32[]{:S(2)}) collective-permute-start(f32[8,128]{1,0:T(8,128)S(1)} %slice_bitcast_fusion), channel_id=1, source_target_pairs={{18,0},{19,1},{16,2},{17,3},{22,4},{23,5},{20,6},{21,7},{26,8},{27... | collective-permute-start | bytes 12296 | tf_op jit(solution)/shard_map/ppermute | solution.py:289
  218.0 7.2 %collective-permute-start.10 = (f32[8,128]{1,0:T(8,128)S(1)}, f32[8,128]{1,0:T(8,128)S(1)}, u32[]{:S(2)}, u32[]{:S(2)}) collective-permute-start(f32[8,128]{1,0:T(8,128)S(1)} %slice_bitcast_fusion), channel_id=1, source_target_pairs={{0,0},{1,1},{2,2},{3,3},{4,4},{5,5},{6,6},{7,7},{8,8},{9,9},{10,10... | collective-permute-start | bytes 12296 | tf_op jit(solution)/shard_map/ppermute | solution.py:289
  225.2 0.7 collective-permute-done.10
  225.9 15.8 %all-gather.3 = f32[768,128]{1,0:T(8,128)S(1)} all-gather(f32[48,128]{1,0:T(8,128)S(1)} %pad_maximum_fusion.4), channel_id=5, replica_groups=mesh['z'=8,'core'=2,'block'=32] {'z','core'}, dimensions={0}, use_global_device_ids=true | all-gather | bytes 417792 | tf_op jit(solution)/shard_map/all_gather | solution.py:290
  241.7 1.7 last.1
  (33 shorter events, 0.2 us)
Async XLA Ops:
  0.6 4.2 %copy-start.3 = (s32[4,1]{0,1:T(1,128)S(1)}, s32[4,1]{0,1:T(1,128)}, u32[]{:S(2)}) copy-start(s32[4,1]{0,1:T(1,128)} %param.10) | copy-start | bytes 52
  2.4 18.6 %copy-start = (f32[4,1,256,256]{3,2,1,0:T(8,128)S(1)}, f32[4,1,256,256]{3,2,1,0:T(8,128)}, u32[]{:S(2)}) copy-start(f32[4,1,256,256]{3,2,1,0:T(8,128)} %param.8) | copy-start | bytes 3145732
  2.4 18.5 %copy-start.1 = (f32[4,1,256,256]{3,2,1,0:T(8,128)S(1)}, f32[4,1,256,256]{3,2,1,0:T(8,128)}, u32[]{:S(2)}) copy-start(f32[4,1,256,256]{3,2,1,0:T(8,128)} %param.9) | copy-start | bytes 3145732
  3.5 10.5 %collective-permute-start = (f32[2,256,256]{2,1,0:T(8,128)S(1)}, f32[2,256,256]{2,1,0:T(8,128)S(1)}, u32[]{:S(2)}, u32[]{:S(2)}) collective-permute-start(f32[2,256,256]{2,1,0:T(8,128)S(1)} %pad_maximum_fusion.own.refs_4_.refs_2_), channel_id=1, source_target_pairs={{0,1},{1,2},{2,3},{3,4},{4,5},{5,6},{6,7},{7,8},{8,9},{9,10},{10,1... | collective-permute-start | bytes 1572872 | tf_op jit(solution)/shard_map/ppermute | solution.py:276
  23.5 19.2 %all-to-all-start = ((f32[8,72,128]{2,1,0:T(8,128)}), f32[8,72,128]{2,1,0:T(8,128)S(1)}, u32[]{:S(2)}, u32[]{:S(2)}) async-start(f32[8,72,128]{2,1,0:T(8,128)} %first.1), calls=%async_computation | async-start | bytes 589824 | tf_op jit(solution)/shard_map/all_to_all | solution.py:281
  42.7 40.5 %copy-start.2 = (f32[2,256,256]{2,1,0:T(8,128)S(1)}, f32[2,256,256]{2,1,0:T(8,128)}, u32[]{:S(2)}) copy-start(f32[2,256,256]{2,1,0:T(8,128)} %all_gather.50.refs_6_) | copy-start | bytes 1572868
  45.5 17.4 %collective-permute-start.3 = (f32[8,128]{1,0:T(8,128)S(1)}, f32[8,128]{1,0:T(8,128)S(1)}, u32[]{:S(2)}, u32[]{:S(2)}) collective-permute-start(f32[8,128]{1,0:T(8,128)S(1)} %slice_bitcast_fusion.3), channel_id=1, source_target_pairs={{18,0},{19,1},{16,2},{17,3},{22,4},{23,5},{20,6},{21,7},{26,8},{27... | collective-permute-start | bytes 12296 | tf_op jit(solution)/shard_map/ppermute | solution.py:289
  54.9 8.0 %collective-permute-start.2 = (f32[8,128]{1,0:T(8,128)S(1)}, f32[8,128]{1,0:T(8,128)S(1)}, u32[]{:S(2)}, u32[]{:S(2)}) collective-permute-start(f32[8,128]{1,0:T(8,128)S(1)} %slice_bitcast_fusion.3), channel_id=1, source_target_pairs={{0,0},{1,1},{2,2},{3,3},{4,4},{5,5},{6,6},{7,7},{8,8},{9,9},{10,10... | collective-permute-start | bytes 12296 | tf_op jit(solution)/shard_map/ppermute | solution.py:289
  61.6 4.7 %collective-permute-start.1 = (f32[64,128]{1,0:T(8,128)S(1)}, f32[64,128]{1,0:T(8,128)S(1)}, u32[]{:S(2)}, u32[]{:S(2)}) collective-permute-start(f32[64,128]{1,0:T(8,128)S(1)} %get-tuple-element.27), channel_id=1, source_target_pairs={{0,1},{1,2},{2,3},{3,4},{4,5},{5,6},{6,7},{7,8},{8,9},{9,10},{10,1... | collective-permute-start | bytes 98312 | tf_op jit(solution)/shard_map/ppermute | solution.py:287
  103.0 13.4 %collective-permute-start.6 = (f32[8,128]{1,0:T(8,128)S(1)}, f32[8,128]{1,0:T(8,128)S(1)}, u32[]{:S(2)}, u32[]{:S(2)}) collective-permute-start(f32[8,128]{1,0:T(8,128)S(1)} %slice_bitcast_fusion.2), channel_id=1, source_target_pairs={{18,0},{19,1},{16,2},{17,3},{22,4},{23,5},{20,6},{21,7},{26,8},{27... | collective-permute-start | bytes 12296 | tf_op jit(solution)/shard_map/ppermute | solution.py:289
  108.1 8.3 %collective-permute-start.5 = (f32[8,128]{1,0:T(8,128)S(1)}, f32[8,128]{1,0:T(8,128)S(1)}, u32[]{:S(2)}, u32[]{:S(2)}) collective-permute-start(f32[8,128]{1,0:T(8,128)S(1)} %slice_bitcast_fusion.2), channel_id=1, source_target_pairs={{0,0},{1,1},{2,2},{3,3},{4,4},{5,5},{6,6},{7,7},{8,8},{9,9},{10,10... | collective-permute-start | bytes 12296 | tf_op jit(solution)/shard_map/ppermute | solution.py:289
  115.1 4.7 %collective-permute-start.4 = (f32[64,128]{1,0:T(8,128)S(1)}, f32[64,128]{1,0:T(8,128)S(1)}, u32[]{:S(2)}, u32[]{:S(2)}) collective-permute-start(f32[64,128]{1,0:T(8,128)S(1)} %get-tuple-element.25), channel_id=1, source_target_pairs={{0,1},{1,2},{2,3},{3,4},{4,5},{5,6},{6,7},{7,8},{8,9},{9,10},{10,1... | collective-permute-start | bytes 98312 | tf_op jit(solution)/shard_map/ppermute | solution.py:287
  156.8 15.6 %collective-permute-start.9 = (f32[8,128]{1,0:T(8,128)S(1)}, f32[8,128]{1,0:T(8,128)S(1)}, u32[]{:S(2)}, u32[]{:S(2)}) collective-permute-start(f32[8,128]{1,0:T(8,128)S(1)} %slice_bitcast_fusion.1), channel_id=1, source_target_pairs={{18,0},{19,1},{16,2},{17,3},{22,4},{23,5},{20,6},{21,7},{26,8},{27... | collective-permute-start | bytes 12296 | tf_op jit(solution)/shard_map/ppermute | solution.py:289
  162.9 9.5 %collective-permute-start.8 = (f32[8,128]{1,0:T(8,128)S(1)}, f32[8,128]{1,0:T(8,128)S(1)}, u32[]{:S(2)}, u32[]{:S(2)}) collective-permute-start(f32[8,128]{1,0:T(8,128)S(1)} %slice_bitcast_fusion.1), channel_id=1, source_target_pairs={{0,0},{1,1},{2,2},{3,3},{4,4},{5,5},{6,6},{7,7},{8,8},{9,9},{10,10... | collective-permute-start | bytes 12296 | tf_op jit(solution)/shard_map/ppermute | solution.py:289
  171.1 5.0 %collective-permute-start.7 = (f32[64,128]{1,0:T(8,128)S(1)}, f32[64,128]{1,0:T(8,128)S(1)}, u32[]{:S(2)}, u32[]{:S(2)}) collective-permute-start(f32[64,128]{1,0:T(8,128)S(1)} %get-tuple-element.23), channel_id=1, source_target_pairs={{0,1},{1,2},{2,3},{3,4},{4,5},{5,6},{6,7},{7,8},{8,9},{9,10},{10,1... | collective-permute-start | bytes 98312 | tf_op jit(solution)/shard_map/ppermute | solution.py:287
  213.2 12.0 %collective-permute-start.11 = (f32[8,128]{1,0:T(8,128)S(1)}, f32[8,128]{1,0:T(8,128)S(1)}, u32[]{:S(2)}, u32[]{:S(2)}) collective-permute-start(f32[8,128]{1,0:T(8,128)S(1)} %slice_bitcast_fusion), channel_id=1, source_target_pairs={{18,0},{19,1},{16,2},{17,3},{22,4},{23,5},{20,6},{21,7},{26,8},{27... | collective-permute-start | bytes 12296 | tf_op jit(solution)/shard_map/ppermute | solution.py:289
  218.0 7.9 %collective-permute-start.10 = (f32[8,128]{1,0:T(8,128)S(1)}, f32[8,128]{1,0:T(8,128)S(1)}, u32[]{:S(2)}, u32[]{:S(2)}) collective-permute-start(f32[8,128]{1,0:T(8,128)S(1)} %slice_bitcast_fusion), channel_id=1, source_target_pairs={{0,0},{1,1},{2,2},{3,3},{4,4},{5,5},{6,6},{7,7},{8,8},{9,9},{10,10... | collective-permute-start | bytes 12296 | tf_op jit(solution)/shard_map/ppermute | solution.py:289

commit v4 on v3

v4 whole, which is shorter than its diff:
```python
import math

import jax
import jax.numpy as jnp
import numpy as np
from jax import lax
from jax.experimental import pallas as pl
from jax.experimental.pallas import tpu as pltpu
from jax.sharding import Mesh, PartitionSpec as P

ITERS = 3
ZS, CORES, BLOCKS = 8, 2, 32
GROUP = ZS * CORES
M = 256
PIECE = M // ZS
LANES = M // CORES
ROWS = PIECE * CORES
SCAL = 8
XS = 4
YS = BLOCKS // XS
TERM = ("z", "core")
BLOCK = ("y", "xh", "xl")
ALL = TERM + BLOCK
VMEM = pl.BlockSpec(memory_space=pltpu.VMEM)
SMEM = pl.BlockSpec(memory_space=pltpu.SMEM)
BF16, F32 = jnp.bfloat16, jnp.float32


def split(x):
    high = x.astype(BF16)
    return high, (x - high.astype(F32)).astype(BF16)


def dot3(a, b):
    def mm(x, y):
        return lax.dot_general(x, y, (((1,), (0,)), ((), ())), preferred_element_type=F32)

    return mm(a[0], b[0]) + (mm(a[0], b[1]) + mm(a[1], b[0]))


def column_sum(x):
    folded = x[:, :LANES] + x[:, LANES:]
    return jnp.sum(folded, axis=0, keepdims=True)


def prepare_kernel(left, right, left_high, left_low, right_high, right_low):
    for term in range(left.shape[0]):
        left_high[term], left_low[term] = split(left[term])
        right_high[term], right_low[term] = split(right[term])


def apply_terms(info, ops, t_high, t_low, t_own, v_own, r_own, part):
    total = jnp.zeros((M, M), F32)
    left_high, left_low, right_high, right_low = ops
    for term in range(left_high.shape[0]):
        sel = 1 - info[2 + term]
        half = dot3((left_high[term], left_low[term]), (t_high[sel], t_low[sel]))
        total = total + dot3(split(half), (right_high[term], right_low[term]))
    size = info[1]
    live = (lax.broadcasted_iota(jnp.int32, (M, M), 0) < size) & (
        lax.broadcasted_iota(jnp.int32, (M, M), 1) < size
    )
    total = jnp.where(live, total, 0.0)
    share = 1.0 / GROUP
    rows = [
        column_sum(t_own * t_own) * share,
        column_sum(t_own * total),
    ]
    if v_own is not None:
        rows += [
            column_sum(v_own * t_own) * share,
            column_sum(t_own * r_own) * share,
            column_sum(v_own * total),
        ]
    rows.append(jnp.zeros((SCAL - len(rows), LANES), F32))
    scal = jnp.concatenate(rows, axis=0)
    for z in range(ZS):
        for core in range(CORES):
            part[z, core * PIECE : (core + 1) * PIECE] = total[
                z * PIECE : (z + 1) * PIECE, core * LANES : (core + 1) * LANES]
        part[z, ROWS:] = scal


def first_kernel(info, lh, ll, rh, rl, x_own, x_side, part, t_high, t_low):
    t_high[0], t_low[0] = split(x_side[0])
    t_high[1], t_low[1] = split(x_own[...])
    t_high[2], t_low[2] = split(x_side[1])
    apply_terms(info, (lh, ll, rh, rl), t_high, t_low, x_own[...], None, None, part)


def global_sums(info, gathered, row):
    y, xh = lax.shift_right_logical(info[0], 2), lax.shift_right_logical(info[0], 1) & 1
    total = None
    for pair in range(GROUP):
        member = CORES * ((pair // CORES - y) & (YS - 1)) + ((pair % CORES - xh) & 1)
        piece = gathered[member, row : row + SCAL]
        total = piece if total is None else total + piece
    return jnp.sum(total, axis=1, keepdims=True)


def scalars(first, sums, state):
    tt, th = sums[0:1], sums[1:2]
    if first:
        scale = tt + 1e-12
        return None, jnp.sqrt(scale), None, None, None, th / scale, tt / scale, None
    p, tr, vh = sums[2:3], sums[3:4], sums[4:5]
    rho, vv = state[0:1, 0:1], state[1:2, 0:1]
    norm_sq = jnp.maximum(tt - 2.0 * p * p + p * p * vv, 0.0)
    n_sq = norm_sq + 1e-12
    n = jnp.sqrt(n_sq)
    tw = tr + rho * p
    coupling = tr / n
    curvature = (th - p * tw - p * vh + p * p * rho) / n_sq
    lowest = 0.5 * (rho + curvature) - jnp.sqrt((0.5 * (rho - curvature)) ** 2 + coupling * coupling)
    gap = curvature - lowest
    len_sq = gap * gap + coupling * coupling
    length = jnp.sqrt(len_sq)
    v_image = (vh - p * rho) / n
    v_unit = (p - p * vv) / n
    unit_sq = norm_sq / n_sq
    next_rho = (gap * gap * rho - gap * coupling * (v_image + coupling) + coupling * coupling * curvature) / len_sq
    next_vv = (gap * gap * vv - 2.0 * gap * coupling * v_unit + coupling * coupling * unit_sq) / len_sq
    return p, n, gap, coupling, length, next_rho, next_vv, lowest


def combine(first, scal, v, w, t, y):
    p, n, gap, coupling, length = scal[:5]
    if first:
        return t / n, y / n
    by_unit = coupling / (n * length)
    by_old = gap / length + p * by_unit
    return by_old * v - by_unit * t, by_old * w - by_unit * y


def state_rows(first, scal, state, iteration):
    rows = [scal[5], scal[6]]
    for i in range(ITERS):
        if i < iteration - 1:
            rows.append(state[2 + i : 3 + i, 0:1])
        elif i == iteration - 1 and not first:
            rows.append(scal[7])
        else:
            rows.append(jnp.zeros((1, 1), F32))
    rows.append(jnp.zeros((SCAL - len(rows), 1), F32))
    return jnp.broadcast_to(jnp.concatenate(rows, axis=0), (SCAL, 128))


def trial(v, w, diag, rho):
    return (w - rho * v) / jnp.maximum(jnp.abs(diag - rho), 1.0)


def step_kernel(iteration, *refs):
    first = iteration == 0
    if first:
        (info, lh, ll, rh, rl, gathered, x_own, x_side, d_own, d_side, state_out, out, part, t_high, t_low) = refs
        old = state = None
    else:
        (info, lh, ll, rh, rl, gathered, d_own, d_side, old, state, state_out, out, part, t_high, t_low) = refs
    scal = scalars(first, global_sums(info, gathered, 3 * PIECE), None if first else state)
    rho = scal[5]
    state_out[...] = state_rows(first, scal, state, iteration)
    odd = info[0] & 1
    for block in (0, 2, 1):
        at = 0 if block == 1 else pl.multiple_of(PIECE * (2 - odd if block == 0 else 1 + odd), PIECE)
        for z in range(ZS):
            rows = pl.ds(z * PIECE, PIECE)
            halves = [gathered[CORES * z + c, pl.ds(at, PIECE)] for c in range(CORES)]
            diag = d_own[rows] if block == 1 else d_side[block // 2, rows]
            image = jnp.concatenate(halves, axis=1)
            if first:
                x = x_own[rows] if block == 1 else x_side[block // 2, rows]
                v, w = combine(True, scal, None, None, x, image)
            else:
                v, w, t = (old[3 * k + block, rows] for k in range(3))
                v, w = combine(False, scal, v, w, t, image)
            t = trial(v, w, diag, rho)
            out[block, rows] = v
            out[3 + block, rows] = w
            out[6 + block, rows] = t
            t_high[block, rows], t_low[block, rows] = split(t)
    v_own = out[1]
    apply_terms(info, (lh, ll, rh, rl), t_high, t_low, out[7], v_own, out[4] - rho * v_own, part)


def last_kernel(factor, info, gathered, old, state, wave, image, energies):
    scal = scalars(False, global_sums(info, gathered, PIECE), state)
    rows = state_rows(False, scal, state, ITERS)
    for i in range(ITERS):
        energies[i] = rows[2 + i, 0]
    for z in range(ZS):
        rows = pl.ds(z * PIECE, PIECE)
        got = jnp.concatenate([gathered[CORES * z + c, :PIECE] for c in range(CORES)], axis=1)
        v, w = combine(False, scal, old[1, rows], old[4, rows], old[7, rows], got)
        wave[0, rows] = v * factor
        image[0, rows] = w * factor


def shape(*dims):
    return jax.ShapeDtypeStruct(dims, F32)


PARAMS = pltpu.CompilerParams(vmem_limit_bytes=16 * 1024 * 1024)
SPLITS = [pltpu.VMEM((3, M, M), BF16), pltpu.VMEM((3, M, M), BF16)]
PART = shape(ZS, ROWS + SCAL, LANES)


def run_prepare(left, right):
    part = jax.ShapeDtypeStruct(left.shape, BF16)
    return pl.pallas_call(
        prepare_kernel,
        out_shape=(part,) * 4,
        in_specs=[VMEM] * 2,
        out_specs=(VMEM,) * 4,
        compiler_params=PARAMS,
        cost_estimate=pl.CostEstimate(flops=4 * left.size, bytes_accessed=16 * left.size, transcendentals=0),
        name="prepare",
    )(left, right)


def run_first(info, *arrays):
    return pl.pallas_call(
        first_kernel,
        out_shape=PART,
        in_specs=[SMEM] + [VMEM] * len(arrays),
        out_specs=VMEM,
        scratch_shapes=SPLITS,
        compiler_params=PARAMS,
        name="first",
    )(info, *arrays)


def run_step(iteration, info, *arrays):
    def body(*refs):
        step_kernel(iteration, *refs)

    return pl.pallas_call(
        body,
        out_shape=(shape(SCAL, 128), shape(9, M, M), PART),
        in_specs=[SMEM] + [VMEM] * len(arrays),
        out_specs=(VMEM,) * 3,
        scratch_shapes=SPLITS,
        input_output_aliases={8: 1} if iteration else {},
        compiler_params=PARAMS,
        name="step",
    )(info, *arrays)


def run_last(info, *arrays):
    factor = math.sqrt(BLOCKS * M * M)

    def body(*refs):
        last_kernel(factor, *refs)

    return pl.pallas_call(
        body,
        out_shape=(shape(1, M, M), shape(1, M, M), shape(ITERS)),
        in_specs=[SMEM] + [VMEM] * 3,
        out_specs=(VMEM, VMEM, SMEM),
        compiler_params=PARAMS,
        name="last",
    )(info, *arrays)


def halo_pairs():
    pairs = []
    for z in range(ZS):
        for core in range(CORES):
            for b in range(BLOCKS):
                source = b - 1 if core == 0 else b + 1
                if 0 <= source < BLOCKS:
                    base = (z * CORES + core) * BLOCKS
                    pairs.append((base + source, base + b))
    return pairs


def spread_pairs():
    pairs = []
    for z in range(ZS):
        for core in range(CORES):
            for b in range(BLOCKS):
                y, x = (b // XS + z) % YS, (b % XS + 2 * core) % XS
                base = (z * CORES + core) * BLOCKS
                pairs.append((base + y * XS + x, base + b))
    return pairs


def gather_core(block):
    return lax.all_gather(block, "core", axis=0)


def exchange(part, place, with_halo):
    pieces = lax.all_to_all(part, "z", 0, 0, tiled=True)
    summed = sum(pieces[z] for z in range(1, ZS)) + pieces[0]
    four = lax.all_gather(summed, ("xl", "core"), axis=0)
    low, high = four[0] + four[1], four[2] + four[3]
    spread = lax.ppermute(low[ROWS:] + high[ROWS:], ALL, spread_pairs())
    odd, core, edge = place

    def half(rows):
        return jnp.where(core, rows[PIECE:ROWS], rows[:PIECE])

    own = half(jnp.where(odd, high, low))
    parts = [own]
    if with_halo:
        parts.append(half(jnp.where(odd, low, high)))
        shifted = [[b, (b + 1) % BLOCKS] for b in range(1, BLOCKS, 2)]
        two = lax.all_gather(own, BLOCK, axis=0, axis_index_groups=shifted)
        parts.append(jnp.where(edge, 0.0, jnp.where(odd, two[1], two[0])))
    return lax.all_gather(jnp.concatenate(parts + [spread], axis=0), TERM, axis=0)


def per_device(start, diagonal, left_ops, right_ops, offsets, sizes):
    info = jnp.concatenate([lax.axis_index(BLOCK)[None].astype(jnp.int32), sizes, offsets[:, 0]])
    live = jnp.arange(M, dtype=jnp.int32) < sizes[0]
    x_own = jnp.where(live[:, None] & live[None, :], start[0], 0.0)
    d_own = diagonal[0]
    b = lax.axis_index(BLOCK)
    place = (lax.axis_index("xl") == 1, lax.axis_index("core") == 1, (b == 0) | (b == BLOCKS - 1))
    x_side, d_side, place = lax.optimization_barrier(
        (gather_core(lax.ppermute(x_own, ALL, halo_pairs())),
         gather_core(lax.ppermute(d_own, ALL, halo_pairs())), place))
    ops = run_prepare(left_ops[:, 0], right_ops[:, 0])
    part = run_first(info, *ops, x_own, x_side)
    gathered = exchange(part, place, True)
    state, kept, part = run_step(0, info, *ops, gathered, x_own, x_side, d_own, d_side)
    for iteration in range(1, ITERS):
        gathered = exchange(part, place, True)
        state, kept, part = run_step(iteration, info, *ops, gathered, d_own, d_side, kept, state)
    gathered = exchange(part, place, False)
    wave, image, energies = run_last(info, gathered, kept, state)
    return wave, image, energies


def solution(mesh):
    grid = Mesh(np.asarray(mesh.devices).reshape(ZS, CORES, YS, 2, 2), ALL)
    return jax.shard_map(
        per_device,
        mesh=grid,
        in_specs=(
            P(BLOCK, None, None),
            P(BLOCK, None, None),
            P(TERM, BLOCK, None, None),
            P(TERM, BLOCK, None, None),
            P(TERM, BLOCK),
            P(BLOCK),
        ),
        out_specs=(P(BLOCK, None, None), P(BLOCK, None, None), P()),
        check_vma=False,
    )
```

time: 244 us -> 236 us (0.967)
  blocking collectives: 134 us -> 201 us
  starting transfers between devices: 66.3 us -> 12.7 us
  waiting for transfers between devices: 26.9 us -> 6.14 us
    ppermute x12 -> x6, starting transfers between devices: 59.5 us -> 12.7 us  [the longest x4 10.1 us: exchange(): spread = lax.ppermute(low[ROWS:] + high[ROWS:], ALL, spread_pairs())]
    all_gather x10 -> x13, blocking collectives: 88.3 us -> 129 us  [the longest x4 75.4 us: exchange(): lax.all_gather(jnp.concatenate(parts + [spread], axis=0), TERM, axis=0)]
    all_to_all x3 -> x4, blocking collectives: 45.2 us -> 71.7 us  [exchange(): pieces = lax.all_to_all(part, 'z', 0, 0, tiled=True)]
    ppermute x12 -> x6, waiting for transfers between devices: 20.1 us -> 6.14 us  [the longest x4 3.92 us: exchange(): spread = lax.ppermute(low[ROWS:] + high[ROWS:], ALL, spread_pairs())]
    all_to_all x1 -> x0, waiting for transfers between devices: 6.8 us -> none  [exchange(): pieces = lax.all_to_all(part, 'z', 0, 0, tiled=True)]
    all_to_all x1 -> x0, starting transfers between devices: 6.77 us -> none  [exchange(): pieces = lax.all_to_all(part, 'z', 0, 0, tiled=True)]
    pallas_call x4 -> x5, Pallas kernels: 10.2 us -> 9.23 us  [the longest x3 7.03 us: run_step(): pl.pallas_call(body, out_shape=(shape(SCAL, 128), shape(9, M, M), PART),...]
  transfers between devices with their start and end apart: 13 -> 6, of which waited for: 6 -> 2; matrix products, arithmetic and copies ran while one was open for 0% -> 0% of each run, Pallas kernels for 0% -> 0%
where the time goes in v4:
time: 236 us
  blocking collectives  201 us (85%)
  starting transfers between devices  12.7 us (5%)
  Pallas kernels  10.8 us (5%)
  waiting for transfers between devices  6.14 us (3%)
  local copies, waits for them, and re-layouts  2.45 us (1%)
    all_gather x4, blocking collectives, exchange(): lax.all_gather(jnp.concatenate(parts + [spread], axis=0), TERM, axis=0)  75.4 us
    all_to_all x4, blocking collectives, exchange(): pieces = lax.all_to_all(part, 'z', 0, 0, tiled=True)  71.7 us
    all_gather x4, blocking collectives, exchange(): four = lax.all_gather(summed, ('xl', 'core'), axis=0)  24.7 us
    all_gather x3, blocking collectives, exchange(): two = lax.all_gather(own, BLOCK, axis=0, axis_index_groups=shifted)  19.8 us
    ppermute x4, starting transfers between devices, exchange(): spread = lax.ppermute(low[ROWS:] + high[ROWS:], ALL, spread_pairs())  10.1 us
    all_gather x2, blocking collectives, gather_core(): return lax.all_gather(block, 'core', axis=0)  9.05 us
    pallas_call x3, Pallas kernels, run_step(): pl.pallas_call(body, out_shape=(shape(SCAL, 128), shape(9, M, M), PART),...  7.03 us
  transfers between devices with their start and end apart: 6, of which 2 were waited for; matrix products, arithmetic and copies ran while one was open for 0% of the time, Pallas kernels for 0%

profile of v4, /device:TPU:1, one launch (start us, length us, event | category | flops | bytes accessed | tf_op | source)
XLA Modules:
  0.0 235.8 jit_solution(13792457555851104582)
XLA Ops:
  0.6 0.0 copy-start.3
  1.3 1.1 bitcast_select_fusion.x_own.refs_6_
  2.4 1.3 collective-permute-start
  3.7 1.3 collective-permute-start.1
  5.0 0.0 copy-start.1
  5.0 1.2 copy-done.1
  6.2 0.0 copy-start.2
  6.2 1.2 copy-done.2
  7.4 0.3 prepare.1
  7.8 0.0 copy-done.3
  7.8 0.1 pad_add_fusion.info.refs_0_
  7.9 2.2 collective-permute-done
  10.1 6.5 %all-gather = f32[512,256]{1,0:T(8,128)S(1)} all-gather(f32[256,256]{1,0:T(8,128)S(1)} %collective-permute-done), channel_id=2, replica_groups=mesh['z'=8,'core'=2,'y'=8,'xh'=2,'xl'=2] {'core'}, dimensions={0}, use_global_device_ids=true | all-gather | bytes 786432 | tf_op jit(solution)/shard_map/all_gather | solution.py:288
  16.6 0.0 collective-permute-done.1
  16.6 2.6 %all-gather.1 = f32[512,256]{1,0:T(8,128)S(1)} all-gather(f32[256,256]{1,0:T(8,128)S(1)} %collective-permute-done.1), channel_id=3, replica_groups=mesh['z'=8,'core'=2,'y'=8,'xh'=2,'xl'=2] {'core'}, dimensions={0}, use_global_device_ids=true | all-gather | bytes 786432 | tf_op jit(solution)/shard_map/all_gather | solution.py:288
  19.1 0.0 copy-start
  19.1 1.9 first.1
  21.0 20.5 %all_to_all.20 = f32[8,72,128]{2,1,0:T(8,128)S(1)} all-to-all(f32[8,72,128]{2,1,0:T(8,128)S(1)} %first.1), channel_id=1, replica_groups=mesh['z'=8,'core'=2,'y'=8,'xh'=2,'xl'=2] {'z'}, dimensions={0} | all-to-all | bytes 589824 | tf_op jit(solution)/shard_map/all_to_all | solution.py:292
  41.5 6.6 %all_gather.68 = f32[4,72,128]{2,1,0:T(8,128)S(1)} all-gather(f32[1,72,128]{2,1,0:T(8,128)S(1)} %slice_add_fusion.29), channel_id=1, replica_groups=mesh['z'=8,'core'=2,'y'=8,'xh'=2,'xl'=2] {'xl','core'}, dimensions={0}, use_global_device_ids=true | all-gather | bytes 184320 | tf_op jit(solution)/shard_map/all_gather | solution.py:294
  48.2 4.4 %collective-permute-start.2 = (f32[8,128]{1,0:T(8,128)S(1)}, f32[8,128]{1,0:T(8,128)S(1)}, u32[]{:S(2)}, u32[]{:S(2)}) collective-permute-start(f32[8,128]{1,0:T(8,128)S(1)} %fusion.13), channel_id=1, source_target_pairs={{0,0},{1,1},{2,2},{3,3},{4,4},{5,5},{6,6},{7,7},{8,8},{9,9},{10,10... | collective-permute-start | bytes 12296 | tf_op jit(solution)/shard_map/ppermute | solution.py:296
  52.6 6.6 %all_gather.69 = f32[2,32,128]{2,1,0:T(8,128)S(1)} all-gather(f32[1,32,128]{2,1,0:T(8,128)S(1)} %slice_select_fusion.9), channel_id=1, replica_groups={{1,2},{3,4},{5,6},{7,8},{9,10},{11,12},{13,14},{15,16},{17,18},{19,20},..., dimensions={0}, use_global_device_ids=true | all-gather | bytes 49152 | tf_op jit(solution)/shard_map/all_gather | solution.py:307
  59.2 0.0 collective-permute-done.2
  59.2 21.3 %all-gather.2 = f32[1664,128]{1,0:T(8,128)S(1)} all-gather(f32[104,128]{1,0:T(8,128)S(1)} %pad_maximum_fusion), channel_id=4, replica_groups=mesh['z'=8,'core'=2,'y'=8,'xh'=2,'xl'=2] {'z','core'}, dimensions={0}, use_global_device_ids=true | all-gather | bytes 905216 | tf_op jit(solution)/shard_map/all_gather | solution.py:309
  80.5 0.0 copy-done
  80.5 2.2 step.3
  82.7 17.8 %all_to_all.21 = f32[8,72,128]{2,1,0:T(8,128)S(1)} all-to-all(f32[8,72,128]{2,1,0:T(8,128)S(1)} %get-tuple-element.30), channel_id=1, replica_groups=mesh['z'=8,'core'=2,'y'=8,'xh'=2,'xl'=2] {'z'}, dimensions={0} | all-to-all | bytes 589824 | tf_op jit(solution)/shard_map/all_to_all | solution.py:292
  100.5 6.0 %all_gather.72 = f32[4,72,128]{2,1,0:T(8,128)S(1)} all-gather(f32[1,72,128]{2,1,0:T(8,128)S(1)} %slice_add_fusion.20), channel_id=1, replica_groups=mesh['z'=8,'core'=2,'y'=8,'xh'=2,'xl'=2] {'xl','core'}, dimensions={0}, use_global_device_ids=true | all-gather | bytes 184320 | tf_op jit(solution)/shard_map/all_gather | solution.py:294
  106.6 1.9 collective-permute-start.3
  108.5 6.6 %all_gather.73 = f32[2,32,128]{2,1,0:T(8,128)S(1)} all-gather(f32[1,32,128]{2,1,0:T(8,128)S(1)} %slice_select_fusion.6), channel_id=1, replica_groups={{1,2},{3,4},{5,6},{7,8},{9,10},{11,12},{13,14},{15,16},{17,18},{19,20},..., dimensions={0}, use_global_device_ids=true | all-gather | bytes 49152 | tf_op jit(solution)/shard_map/all_gather | solution.py:307
  115.1 0.0 collective-permute-done.3
  115.1 19.5 %all-gather.3 = f32[1664,128]{1,0:T(8,128)S(1)} all-gather(f32[104,128]{1,0:T(8,128)S(1)} %pad_maximum_fusion.1), channel_id=5, replica_groups=mesh['z'=8,'core'=2,'y'=8,'xh'=2,'xl'=2] {'z','core'}, dimensions={0}, use_global_device_ids=true | all-gather | bytes 905216 | tf_op jit(solution)/shard_map/all_gather | solution.py:309
  134.7 2.4 %step.4 = (f32[8,128]{1,0:T(8,128)S(1)}, f32[9,256,256]{2,1,0:T(8,128)S(1)}, f32[8,72,128]{2,1,0:T(8,128)S(1)}) custom-call(s32[6]{0:T(128)S(1)} %pad_add_fusion.info.refs_0_, bf16[4,256,256]{2,1,0:T(8,128)(2,1)S(1)} %get-tuple-element.23.lh.refs_1_, bf16[4,256,256]{2,1,0:T(8,128)(2,1)S(1)} %get-tuple-element.24.ll.refs_2_, ...), custom_call_target="tpu_custom_call", output_to_operand_aliasing={{1}: (8, {})} | custom-call | tf_op jit(solution)/shard_map/step/pallas_call | solution.py:236
  137.1 16.0 %all_to_all.22 = f32[8,72,128]{2,1,0:T(8,128)S(1)} all-to-all(f32[8,72,128]{2,1,0:T(8,128)S(1)} %get-tuple-element.33), channel_id=1, replica_groups=mesh['z'=8,'core'=2,'y'=8,'xh'=2,'xl'=2] {'z'}, dimensions={0} | all-to-all | bytes 589824 | tf_op jit(solution)/shard_map/all_to_all | solution.py:292
  153.1 6.0 %all_gather.76 = f32[4,72,128]{2,1,0:T(8,128)S(1)} all-gather(f32[1,72,128]{2,1,0:T(8,128)S(1)} %slice_add_fusion.11), channel_id=1, replica_groups=mesh['z'=8,'core'=2,'y'=8,'xh'=2,'xl'=2] {'xl','core'}, dimensions={0}, use_global_device_ids=true | all-gather | bytes 184320 | tf_op jit(solution)/shard_map/all_gather | solution.py:294
  159.2 1.9 collective-permute-start.4
  161.1 6.6 %all_gather.77 = f32[2,32,128]{2,1,0:T(8,128)S(1)} all-gather(f32[1,32,128]{2,1,0:T(8,128)S(1)} %slice_select_fusion.3), channel_id=1, replica_groups={{1,2},{3,4},{5,6},{7,8},{9,10},{11,12},{13,14},{15,16},{17,18},{19,20},..., dimensions={0}, use_global_device_ids=true | all-gather | bytes 49152 | tf_op jit(solution)/shard_map/all_gather | solution.py:307
  167.7 0.0 collective-permute-done.4
  167.7 18.4 %all-gather.4 = f32[1664,128]{1,0:T(8,128)S(1)} all-gather(f32[104,128]{1,0:T(8,128)S(1)} %pad_maximum_fusion.2), channel_id=6, replica_groups=mesh['z'=8,'core'=2,'y'=8,'xh'=2,'xl'=2] {'z','core'}, dimensions={0}, use_global_device_ids=true | all-gather | bytes 905216 | tf_op jit(solution)/shard_map/all_gather | solution.py:309
  186.2 2.4 %step.5 = (f32[8,128]{1,0:T(8,128)S(1)}, f32[9,256,256]{2,1,0:T(8,128)S(1)}, f32[8,72,128]{2,1,0:T(8,128)S(1)}) custom-call(s32[6]{0:T(128)S(1)} %pad_add_fusion.info.refs_0_, bf16[4,256,256]{2,1,0:T(8,128)(2,1)S(1)} %get-tuple-element.23.lh.refs_1_, bf16[4,256,256]{2,1,0:T(8,128)(2,1)S(1)} %get-tuple-element.24.ll.refs_2_, ...), custom_call_target="tpu_custom_call", output_to_operand_aliasing={{1}: (8, {})} | custom-call | tf_op jit(solution)/shard_map/step/pallas_call | solution.py:236
  188.6 17.5 %all_to_all.23 = f32[8,72,128]{2,1,0:T(8,128)S(1)} all-to-all(f32[8,72,128]{2,1,0:T(8,128)S(1)} %get-tuple-element.36), channel_id=1, replica_groups=mesh['z'=8,'core'=2,'y'=8,'xh'=2,'xl'=2] {'z'}, dimensions={0} | all-to-all | bytes 589824 | tf_op jit(solution)/shard_map/all_to_all | solution.py:292
  206.1 6.0 %all_gather.80 = f32[4,72,128]{2,1,0:T(8,128)S(1)} all-gather(f32[1,72,128]{2,1,0:T(8,128)S(1)} %slice_add_fusion.2), channel_id=1, replica_groups=mesh['z'=8,'core'=2,'y'=8,'xh'=2,'xl'=2] {'xl','core'}, dimensions={0}, use_global_device_ids=true | all-gather | bytes 184320 | tf_op jit(solution)/shard_map/all_gather | solution.py:294
  212.1 1.9 collective-permute-start.5
  214.1 3.9 %collective-permute-done.5 = f32[8,128]{1,0:T(8,128)S(1)} collective-permute-done((f32[8,128]{1,0:T(8,128)S(1)}, f32[8,128]{1,0:T(8,128)S(1)}, u32[]{:S(2)}, u32[]{:S(2)}) %collective-permute-start.5) | collective-permute-done | bytes 4128 | tf_op jit(solution)/shard_map/ppermute | solution.py:296
  218.0 16.2 %all-gather.5 = f32[640,128]{1,0:T(8,128)S(1)} all-gather(f32[40,128]{1,0:T(8,128)S(1)} %pad_maximum_fusion.3), channel_id=7, replica_groups=mesh['z'=8,'core'=2,'y'=8,'xh'=2,'xl'=2] {'z','core'}, dimensions={0}, use_global_device_ids=true | all-gather | bytes 348160 | tf_op jit(solution)/shard_map/all_gather | solution.py:309
  234.2 1.6 last.1
  (33 shorter events, 0.3 us)
Async XLA Ops:
  0.6 7.1 %copy-start.3 = (s32[4,1]{0,1:T(1,128)S(1)}, s32[4,1]{0,1:T(1,128)}, u32[]{:S(2)}) copy-start(s32[4,1]{0,1:T(1,128)} %param.10) | copy-start | bytes 52
  2.4 7.7 %collective-permute-start = (f32[256,256]{1,0:T(8,128)S(1)}, f32[256,256]{1,0:T(8,128)S(1)}, u32[]{:S(2)}, u32[]{:S(2)}) collective-permute-start(f32[256,256]{1,0:T(8,128)S(1)} %bitcast_select_fusion.x_own.refs_6_), channel_id=1, source_target_pairs={{0,1},{1,2},{2,3},{3,4},{4,5},{5,6},{6,7},{7,8},{8,9},{9,10},{10,1... | collective-permute-start | bytes 786440 | tf_op jit(solution)/shard_map/ppermute | solution.py:320
  3.7 12.9 %collective-permute-start.1 = (f32[256,256]{1,0:T(8,128)}, f32[256,256]{1,0:T(8,128)S(1)}, u32[]{:S(2)}, u32[]{:S(2)}) collective-permute-start(f32[256,256]{1,0:T(8,128)} %bitcast.51), channel_id=1, source_target_pairs={{0,1},{1,2},{2,3},{3,4},{4,5},{5,6},{6,7},{7,8},{8,9},{9,10},{10,1... | collective-permute-start | bytes 786440 | tf_op jit(solution)/shard_map/ppermute | solution.py:321
  5.0 1.2 copy-start.1
  6.2 1.2 copy-start.2
  19.1 61.4 %copy-start = (f32[1,256,256]{2,1,0:T(8,128)S(1)}, f32[1,256,256]{2,1,0:T(8,128)}, u32[]{:S(2)}) copy-start(f32[1,256,256]{2,1,0:T(8,128)} %param.7) | copy-start | bytes 786436
  48.2 11.0 %collective-permute-start.2 = (f32[8,128]{1,0:T(8,128)S(1)}, f32[8,128]{1,0:T(8,128)S(1)}, u32[]{:S(2)}, u32[]{:S(2)}) collective-permute-start(f32[8,128]{1,0:T(8,128)S(1)} %fusion.13), channel_id=1, source_target_pairs={{0,0},{1,1},{2,2},{3,3},{4,4},{5,5},{6,6},{7,7},{8,8},{9,9},{10,10... | collective-permute-start | bytes 12296 | tf_op jit(solution)/shard_map/ppermute | solution.py:296
  106.6 8.5 %collective-permute-start.3 = (f32[8,128]{1,0:T(8,128)S(1)}, f32[8,128]{1,0:T(8,128)S(1)}, u32[]{:S(2)}, u32[]{:S(2)}) collective-permute-start(f32[8,128]{1,0:T(8,128)S(1)} %fusion.12), channel_id=1, source_target_pairs={{0,0},{1,1},{2,2},{3,3},{4,4},{5,5},{6,6},{7,7},{8,8},{9,9},{10,10... | collective-permute-start | bytes 12296 | tf_op jit(solution)/shard_map/ppermute | solution.py:296
  159.2 8.5 %collective-permute-start.4 = (f32[8,128]{1,0:T(8,128)S(1)}, f32[8,128]{1,0:T(8,128)S(1)}, u32[]{:S(2)}, u32[]{:S(2)}) collective-permute-start(f32[8,128]{1,0:T(8,128)S(1)} %fusion.11), channel_id=1, source_target_pairs={{0,0},{1,1},{2,2},{3,3},{4,4},{5,5},{6,6},{7,7},{8,8},{9,9},{10,10... | collective-permute-start | bytes 12296 | tf_op jit(solution)/shard_map/ppermute | solution.py:296
  212.1 5.9 %collective-permute-start.5 = (f32[8,128]{1,0:T(8,128)S(1)}, f32[8,128]{1,0:T(8,128)S(1)}, u32[]{:S(2)}, u32[]{:S(2)}) collective-permute-start(f32[8,128]{1,0:T(8,128)S(1)} %fusion.10), channel_id=1, source_target_pairs={{0,0},{1,1},{2,2},{3,3},{4,4},{5,5},{6,6},{7,7},{8,8},{9,9},{10,10... | collective-permute-start | bytes 12296 | tf_op jit(solution)/shard_map/ppermute | solution.py:296

commit v5 on v4

--- a/solution.py
+++ b/solution.py
@@ -16,6 +16,7 @@
 LANES = M // CORES
 ROWS = PIECE * CORES
 SCAL = 8
+FIRST_SCALE = 2.0**-14
 XS = 4
 YS = BLOCKS // XS
 TERM = ("z", "core")
@@ -62,9 +63,11 @@
     )
     total = jnp.where(live, total, 0.0)
     share = 1.0 / GROUP
+    level = total if v_own is not None else total * FIRST_SCALE
     rows = [
         column_sum(t_own * t_own) * share,
         column_sum(t_own * total),
+        column_sum(level * level),
     ]
     if v_own is not None:
         rows += [
@@ -100,53 +103,61 @@
 
 def scalars(first, sums, state):
     tt, th = sums[0:1], sums[1:2]
+    reach = math.sqrt(GROUP) * jnp.sqrt(sums[2:3])
     if first:
-        scale = tt + 1e-12
-        return None, jnp.sqrt(scale), None, None, None, th / scale, tt / scale, None
-    p, tr, vh = sums[2:3], sums[3:4], sums[4:5]
-    rho, vv = state[0:1, 0:1], state[1:2, 0:1]
-    norm_sq = jnp.maximum(tt - 2.0 * p * p + p * p * vv, 0.0)
-    n_sq = norm_sq + 1e-12
-    n = jnp.sqrt(n_sq)
-    tw = tr + rho * p
-    coupling = tr / n
-    curvature = (th - p * tw - p * vh + p * p * rho) / n_sq
-    lowest = 0.5 * (rho + curvature) - jnp.sqrt((0.5 * (rho - curvature)) ** 2 + coupling * coupling)
-    gap = curvature - lowest
-    len_sq = gap * gap + coupling * coupling
-    length = jnp.sqrt(len_sq)
-    v_image = (vh - p * rho) / n
-    v_unit = (p - p * vv) / n
-    unit_sq = norm_sq / n_sq
-    next_rho = (gap * gap * rho - gap * coupling * (v_image + coupling) + coupling * coupling * curvature) / len_sq
-    next_vv = (gap * gap * vv - 2.0 * gap * coupling * v_unit + coupling * coupling * unit_sq) / len_sq
-    return p, n, gap, coupling, length, next_rho, next_vv, lowest
-
-
-def combine(first, scal, v, w, t, y):
-    p, n, gap, coupling, length = scal[:5]
-    if first:
-        return t / n, y / n
-    by_unit = coupling / (n * length)
-    by_old = gap / length + p * by_unit
+        n_sq = tt + 1e-12
+        n = jnp.sqrt(n_sq)
+        rho, vv, lowest = th / n_sq, tt / n_sq, None
+        bound = reach / n * (1.0 / FIRST_SCALE)
+        weights = (n,)
+    else:
+        p, tr, vh = sums[3:4], sums[4:5], sums[5:6]
+        rho, vv, bound, scale = (state[i : i + 1, 0:1] for i in range(4))
+        norm_sq = jnp.maximum(tt - 2.0 * p * p + p * p * vv, 0.0)
+        n_sq = norm_sq + jnp.maximum(1e-12 * (scale * scale), 1e-36)
+        n = jnp.sqrt(n_sq)
+        tw = tr + rho * p
+        coupling = tr / n
+        curvature = (th - p * tw - p * vh + p * p * rho) / n_sq
+        lowest = 0.5 * (rho + curvature) - jnp.sqrt((0.5 * (rho - curvature)) ** 2 + coupling * coupling)
+        gap = curvature - lowest
+        length = jnp.sqrt(gap * gap + coupling * coupling)
+        cos, sin = gap / length, coupling / length
+        v_image = (vh - p * rho) / n
+        v_unit = (p - p * vv) / n
+        unit_sq = norm_sq / n_sq
+        rho = cos * cos * rho - cos * sin * (v_image + coupling) + sin * sin * curvature
+        vv = cos * cos * vv - 2.0 * cos * sin * v_unit + sin * sin * unit_sq
+        by_unit = sin / n
+        by_old = cos + p * by_unit
+        bound = jnp.abs(by_old) * bound + jnp.abs(by_unit) * reach
+        weights = (by_old, by_unit)
+    scale = 1.0 / jnp.maximum(bound + jnp.abs(rho) * jnp.sqrt(jnp.maximum(vv, 0.0)), 1.0)
+    return weights, (rho, vv, bound, scale), lowest
+
+
+def combine(weights, v, w, t, y):
+    if len(weights) == 1:
+        return t / weights[0], y / weights[0]
+    by_old, by_unit = weights
     return by_old * v - by_unit * t, by_old * w - by_unit * y
 
 
-def state_rows(first, scal, state, iteration):
-    rows = [scal[5], scal[6]]
+def state_rows(now, lowest, state, iteration):
+    rows = list(now)
     for i in range(ITERS):
         if i < iteration - 1:
-            rows.append(state[2 + i : 3 + i, 0:1])
-        elif i == iteration - 1 and not first:
-            rows.append(scal[7])
+            rows.append(state[4 + i : 5 + i, 0:1])
+        elif i == iteration - 1:
+            rows.append(lowest)
         else:
             rows.append(jnp.zeros((1, 1), F32))
     rows.append(jnp.zeros((SCAL - len(rows), 1), F32))
     return jnp.broadcast_to(jnp.concatenate(rows, axis=0), (SCAL, 128))
 
 
-def trial(v, w, diag, rho):
-    return (w - rho * v) / jnp.maximum(jnp.abs(diag - rho), 1.0)
+def trial(v, w, diag, rho, scale):
+    return (w - rho * v) * scale / jnp.maximum(jnp.abs(diag - rho), 1.0)
 
 
 def step_kernel(iteration, *refs):
@@ -156,9 +167,9 @@
         old = state = None
     else:
         (info, lh, ll, rh, rl, gathered, d_own, d_side, old, state, state_out, out, part, t_high, t_low) = refs
-    scal = scalars(first, global_sums(info, gathered, 3 * PIECE), None if first else state)
-    rho = scal[5]
-    state_out[...] = state_rows(first, scal, state, iteration)
+    weights, now, lowest = scalars(first, global_sums(info, gathered, 3 * PIECE), state)
+    rho, scale = now[0], now[3]
+    state_out[...] = state_rows(now, lowest, state, iteration)
     odd = info[0] & 1
     for block in (0, 2, 1):
         at = 0 if block == 1 else pl.multiple_of(PIECE * (2 - odd if block == 0 else 1 + odd), PIECE)
@@ -169,11 +180,11 @@
             image = jnp.concatenate(halves, axis=1)
             if first:
                 x = x_own[rows] if block == 1 else x_side[block // 2, rows]
-                v, w = combine(True, scal, None, None, x, image)
+                v, w = combine(weights, None, None, x, image)
             else:
                 v, w, t = (old[3 * k + block, rows] for k in range(3))
-                v, w = combine(False, scal, v, w, t, image)
-            t = trial(v, w, diag, rho)
+                v, w = combine(weights, v, w, t, image)
+            t = trial(v, w, diag, rho, scale)
             out[block, rows] = v
             out[3 + block, rows] = w
             out[6 + block, rows] = t
@@ -183,14 +194,14 @@
 
 
 def last_kernel(factor, info, gathered, old, state, wave, image, energies):
-    scal = scalars(False, global_sums(info, gathered, PIECE), state)
-    rows = state_rows(False, scal, state, ITERS)
+    weights, now, lowest = scalars(False, global_sums(info, gathered, PIECE), state)
+    rows = state_rows(now, lowest, state, ITERS)
     for i in range(ITERS):
-        energies[i] = rows[2 + i, 0]
+        energies[i] = rows[4 + i, 0]
     for z in range(ZS):
         rows = pl.ds(z * PIECE, PIECE)
         got = jnp.concatenate([gathered[CORES * z + c, :PIECE] for c in range(CORES)], axis=1)
-        v, w = combine(False, scal, old[1, rows], old[4, rows], old[7, rows], got)
+        v, w = combine(weights, old[1, rows], old[4, rows], old[7, rows], got)
         wave[0, rows] = v * factor
         image[0, rows] = w * factor
 
@@ -278,7 +289,7 @@
     for z in range(ZS):
         for core in range(CORES):
             for b in range(BLOCKS):
-                y, x = (b // XS + z) % YS, (b % XS + 2 * core) % XS
+                y, x = (b // XS + z) % YS, XS - 1 - b % XS if core else b % XS
                 base = (z * CORES + core) * BLOCKS
                 pairs.append((base + y * XS + x, base + b))
     return pairs

time: 236 us -> 237 us (level)
  no operation moved by 1% of the time
where the time goes in v5:
time: 237 us; the launch traced here: 236 us
  blocking collectives  201 us (85%)
  starting transfers between devices  12.7 us (5%)
  Pallas kernels  10.9 us (5%)
  waiting for transfers between devices  5.85 us (2%)
  local copies, waits for them, and re-layouts  2.45 us (1%)
    all_gather x4, blocking collectives, exchange(): lax.all_gather(jnp.concatenate(parts + [spread], axis=0), TERM, axis=0)  75.4 us
    all_to_all x4, blocking collectives, exchange(): pieces = lax.all_to_all(part, 'z', 0, 0, tiled=True)  71.6 us
    all_gather x4, blocking collectives, exchange(): four = lax.all_gather(summed, ('xl', 'core'), axis=0)  24.7 us
    all_gather x3, blocking collectives, exchange(): two = lax.all_gather(own, BLOCK, axis=0, axis_index_groups=shifted)  20.2 us
    ppermute x4, starting transfers between devices, exchange(): spread = lax.ppermute(low[ROWS:] + high[ROWS:], ALL, spread_pairs())  10.1 us
    all_gather x2, blocking collectives, gather_core(): return lax.all_gather(block, 'core', axis=0)  9.05 us
    pallas_call x3, Pallas kernels, run_step(): pl.pallas_call(body, out_shape=(shape(SCAL, 128), shape(9, M, M), PART),...  7.07 us
  transfers between devices with their start and end apart: 6, of which 2 were waited for; matrix products, arithmetic and copies ran while one was open for 0% of the time, Pallas kernels for 0%

profile of v5, /device:TPU:1, one launch (start us, length us, event | category | flops | bytes accessed | tf_op | source)
XLA Modules:
  0.0 235.9 jit_solution(13366954822911905646)
XLA Ops:
  0.6 0.0 copy-start.3
  1.3 1.1 bitcast_select_fusion.x_own.refs_6_
  2.4 1.3 collective-permute-start
  3.7 1.3 collective-permute-start.1
  5.0 0.0 copy-start.1
  5.0 1.2 copy-done.1
  6.2 0.0 copy-start.2
  6.2 1.2 copy-done.2
  7.4 0.3 prepare.1
  7.8 0.0 copy-done.3
  7.8 0.1 pad_add_fusion.info.refs_0_
  7.9 2.2 collective-permute-done
  10.1 6.5 %all-gather = f32[512,256]{1,0:T(8,128)S(1)} all-gather(f32[256,256]{1,0:T(8,128)S(1)} %collective-permute-done), channel_id=2, replica_groups=mesh['z'=8,'core'=2,'y'=8,'xh'=2,'xl'=2] {'core'}, dimensions={0}, use_global_device_ids=true | all-gather | bytes 786432 | tf_op jit(solution)/shard_map/all_gather | solution.py:299
  16.6 0.0 collective-permute-done.1
  16.6 2.6 %all-gather.1 = f32[512,256]{1,0:T(8,128)S(1)} all-gather(f32[256,256]{1,0:T(8,128)S(1)} %collective-permute-done.1), channel_id=3, replica_groups=mesh['z'=8,'core'=2,'y'=8,'xh'=2,'xl'=2] {'core'}, dimensions={0}, use_global_device_ids=true | all-gather | bytes 786432 | tf_op jit(solution)/shard_map/all_gather | solution.py:299
  19.1 0.0 copy-start
  19.1 1.9 first.1
  21.0 20.5 %all_to_all.20 = f32[8,72,128]{2,1,0:T(8,128)S(1)} all-to-all(f32[8,72,128]{2,1,0:T(8,128)S(1)} %first.1), channel_id=1, replica_groups=mesh['z'=8,'core'=2,'y'=8,'xh'=2,'xl'=2] {'z'}, dimensions={0} | all-to-all | bytes 589824 | tf_op jit(solution)/shard_map/all_to_all | solution.py:303
  41.5 6.6 %all_gather.68 = f32[4,72,128]{2,1,0:T(8,128)S(1)} all-gather(f32[1,72,128]{2,1,0:T(8,128)S(1)} %slice_add_fusion.29), channel_id=1, replica_groups=mesh['z'=8,'core'=2,'y'=8,'xh'=2,'xl'=2] {'xl','core'}, dimensions={0}, use_global_device_ids=true | all-gather | bytes 184320 | tf_op jit(solution)/shard_map/all_gather | solution.py:305
  48.2 4.4 %collective-permute-start.2 = (f32[8,128]{1,0:T(8,128)S(1)}, f32[8,128]{1,0:T(8,128)S(1)}, u32[]{:S(2)}, u32[]{:S(2)}) collective-permute-start(f32[8,128]{1,0:T(8,128)S(1)} %fusion.13), channel_id=1, source_target_pairs={{0,0},{1,1},{2,2},{3,3},{4,4},{5,5},{6,6},{7,7},{8,8},{9,9},{10,10... | collective-permute-start | bytes 12296 | tf_op jit(solution)/shard_map/ppermute | solution.py:307
  52.6 7.0 %all_gather.69 = f32[2,32,128]{2,1,0:T(8,128)S(1)} all-gather(f32[1,32,128]{2,1,0:T(8,128)S(1)} %slice_select_fusion.9), channel_id=1, replica_groups={{1,2},{3,4},{5,6},{7,8},{9,10},{11,12},{13,14},{15,16},{17,18},{19,20},..., dimensions={0}, use_global_device_ids=true | all-gather | bytes 49152 | tf_op jit(solution)/shard_map/all_gather | solution.py:318
  59.6 0.0 collective-permute-done.2
  59.6 20.9 %all-gather.2 = f32[1664,128]{1,0:T(8,128)S(1)} all-gather(f32[104,128]{1,0:T(8,128)S(1)} %pad_maximum_fusion), channel_id=4, replica_groups=mesh['z'=8,'core'=2,'y'=8,'xh'=2,'xl'=2] {'z','core'}, dimensions={0}, use_global_device_ids=true | all-gather | bytes 905216 | tf_op jit(solution)/shard_map/all_gather | solution.py:320
  80.5 0.0 copy-done
  80.5 2.2 step.3
  82.8 17.8 %all_to_all.21 = f32[8,72,128]{2,1,0:T(8,128)S(1)} all-to-all(f32[8,72,128]{2,1,0:T(8,128)S(1)} %get-tuple-element.30), channel_id=1, replica_groups=mesh['z'=8,'core'=2,'y'=8,'xh'=2,'xl'=2] {'z'}, dimensions={0} | all-to-all | bytes 589824 | tf_op jit(solution)/shard_map/all_to_all | solution.py:303
  100.6 6.0 %all_gather.72 = f32[4,72,128]{2,1,0:T(8,128)S(1)} all-gather(f32[1,72,128]{2,1,0:T(8,128)S(1)} %slice_add_fusion.20), channel_id=1, replica_groups=mesh['z'=8,'core'=2,'y'=8,'xh'=2,'xl'=2] {'xl','core'}, dimensions={0}, use_global_device_ids=true | all-gather | bytes 184320 | tf_op jit(solution)/shard_map/all_gather | solution.py:305
  106.7 1.9 collective-permute-start.3
  108.6 6.6 %all_gather.73 = f32[2,32,128]{2,1,0:T(8,128)S(1)} all-gather(f32[1,32,128]{2,1,0:T(8,128)S(1)} %slice_select_fusion.6), channel_id=1, replica_groups={{1,2},{3,4},{5,6},{7,8},{9,10},{11,12},{13,14},{15,16},{17,18},{19,20},..., dimensions={0}, use_global_device_ids=true | all-gather | bytes 49152 | tf_op jit(solution)/shard_map/all_gather | solution.py:318
  115.2 0.0 collective-permute-done.3
  115.2 19.5 %all-gather.3 = f32[1664,128]{1,0:T(8,128)S(1)} all-gather(f32[104,128]{1,0:T(8,128)S(1)} %pad_maximum_fusion.1), channel_id=5, replica_groups=mesh['z'=8,'core'=2,'y'=8,'xh'=2,'xl'=2] {'z','core'}, dimensions={0}, use_global_device_ids=true | all-gather | bytes 905216 | tf_op jit(solution)/shard_map/all_gather | solution.py:320
  134.7 2.4 %step.4 = (f32[8,128]{1,0:T(8,128)S(1)}, f32[9,256,256]{2,1,0:T(8,128)S(1)}, f32[8,72,128]{2,1,0:T(8,128)S(1)}) custom-call(s32[6]{0:T(128)S(1)} %pad_add_fusion.info.refs_0_, bf16[4,256,256]{2,1,0:T(8,128)(2,1)S(1)} %get-tuple-element.23.lh.refs_1_, bf16[4,256,256]{2,1,0:T(8,128)(2,1)S(1)} %get-tuple-element.24.ll.refs_2_, ...), custom_call_target="tpu_custom_call", output_to_operand_aliasing={{1}: (8, {})} | custom-call | tf_op jit(solution)/shard_map/step/pallas_call | solution.py:247
  137.1 16.0 %all_to_all.22 = f32[8,72,128]{2,1,0:T(8,128)S(1)} all-to-all(f32[8,72,128]{2,1,0:T(8,128)S(1)} %get-tuple-element.33), channel_id=1, replica_groups=mesh['z'=8,'core'=2,'y'=8,'xh'=2,'xl'=2] {'z'}, dimensions={0} | all-to-all | bytes 589824 | tf_op jit(solution)/shard_map/all_to_all | solution.py:303
  153.1 6.0 %all_gather.76 = f32[4,72,128]{2,1,0:T(8,128)S(1)} all-gather(f32[1,72,128]{2,1,0:T(8,128)S(1)} %slice_add_fusion.11), channel_id=1, replica_groups=mesh['z'=8,'core'=2,'y'=8,'xh'=2,'xl'=2] {'xl','core'}, dimensions={0}, use_global_device_ids=true | all-gather | bytes 184320 | tf_op jit(solution)/shard_map/all_gather | solution.py:305
  159.2 1.9 collective-permute-start.4
  161.2 6.6 %all_gather.77 = f32[2,32,128]{2,1,0:T(8,128)S(1)} all-gather(f32[1,32,128]{2,1,0:T(8,128)S(1)} %slice_select_fusion.3), channel_id=1, replica_groups={{1,2},{3,4},{5,6},{7,8},{9,10},{11,12},{13,14},{15,16},{17,18},{19,20},..., dimensions={0}, use_global_device_ids=true | all-gather | bytes 49152 | tf_op jit(solution)/shard_map/all_gather | solution.py:318
  167.8 0.0 collective-permute-done.4
  167.8 18.5 %all-gather.4 = f32[1664,128]{1,0:T(8,128)S(1)} all-gather(f32[104,128]{1,0:T(8,128)S(1)} %pad_maximum_fusion.2), channel_id=6, replica_groups=mesh['z'=8,'core'=2,'y'=8,'xh'=2,'xl'=2] {'z','core'}, dimensions={0}, use_global_device_ids=true | all-gather | bytes 905216 | tf_op jit(solution)/shard_map/all_gather | solution.py:320
  186.3 2.4 %step.5 = (f32[8,128]{1,0:T(8,128)S(1)}, f32[9,256,256]{2,1,0:T(8,128)S(1)}, f32[8,72,128]{2,1,0:T(8,128)S(1)}) custom-call(s32[6]{0:T(128)S(1)} %pad_add_fusion.info.refs_0_, bf16[4,256,256]{2,1,0:T(8,128)(2,1)S(1)} %get-tuple-element.23.lh.refs_1_, bf16[4,256,256]{2,1,0:T(8,128)(2,1)S(1)} %get-tuple-element.24.ll.refs_2_, ...), custom_call_target="tpu_custom_call", output_to_operand_aliasing={{1}: (8, {})} | custom-call | tf_op jit(solution)/shard_map/step/pallas_call | solution.py:247
  188.7 17.4 %all_to_all.23 = f32[8,72,128]{2,1,0:T(8,128)S(1)} all-to-all(f32[8,72,128]{2,1,0:T(8,128)S(1)} %get-tuple-element.36), channel_id=1, replica_groups=mesh['z'=8,'core'=2,'y'=8,'xh'=2,'xl'=2] {'z'}, dimensions={0} | all-to-all | bytes 589824 | tf_op jit(solution)/shard_map/all_to_all | solution.py:303
  206.2 6.0 %all_gather.80 = f32[4,72,128]{2,1,0:T(8,128)S(1)} all-gather(f32[1,72,128]{2,1,0:T(8,128)S(1)} %slice_add_fusion.2), channel_id=1, replica_groups=mesh['z'=8,'core'=2,'y'=8,'xh'=2,'xl'=2] {'xl','core'}, dimensions={0}, use_global_device_ids=true | all-gather | bytes 184320 | tf_op jit(solution)/shard_map/all_gather | solution.py:305
  212.2 1.9 collective-permute-start.5
  214.1 3.6 %collective-permute-done.5 = f32[8,128]{1,0:T(8,128)S(1)} collective-permute-done((f32[8,128]{1,0:T(8,128)S(1)}, f32[8,128]{1,0:T(8,128)S(1)}, u32[]{:S(2)}, u32[]{:S(2)}) %collective-permute-start.5) | collective-permute-done | bytes 4128 | tf_op jit(solution)/shard_map/ppermute | solution.py:307
  217.8 16.5 %all-gather.5 = f32[640,128]{1,0:T(8,128)S(1)} all-gather(f32[40,128]{1,0:T(8,128)S(1)} %pad_maximum_fusion.3), channel_id=7, replica_groups=mesh['z'=8,'core'=2,'y'=8,'xh'=2,'xl'=2] {'z','core'}, dimensions={0}, use_global_device_ids=true | all-gather | bytes 348160 | tf_op jit(solution)/shard_map/all_gather | solution.py:320
  234.2 1.6 last.1
  (33 shorter events, 0.3 us)
Async XLA Ops:
  0.6 7.1 %copy-start.3 = (s32[4,1]{0,1:T(1,128)S(1)}, s32[4,1]{0,1:T(1,128)}, u32[]{:S(2)}) copy-start(s32[4,1]{0,1:T(1,128)} %param.10) | copy-start | bytes 52
  2.4 7.7 %collective-permute-start = (f32[256,256]{1,0:T(8,128)S(1)}, f32[256,256]{1,0:T(8,128)S(1)}, u32[]{:S(2)}, u32[]{:S(2)}) collective-permute-start(f32[256,256]{1,0:T(8,128)S(1)} %bitcast_select_fusion.x_own.refs_6_), channel_id=1, source_target_pairs={{0,1},{1,2},{2,3},{3,4},{4,5},{5,6},{6,7},{7,8},{8,9},{9,10},{10,1... | collective-permute-start | bytes 786440 | tf_op jit(solution)/shard_map/ppermute | solution.py:331
  3.7 12.9 %collective-permute-start.1 = (f32[256,256]{1,0:T(8,128)}, f32[256,256]{1,0:T(8,128)S(1)}, u32[]{:S(2)}, u32[]{:S(2)}) collective-permute-start(f32[256,256]{1,0:T(8,128)} %bitcast.51), channel_id=1, source_target_pairs={{0,1},{1,2},{2,3},{3,4},{4,5},{5,6},{6,7},{7,8},{8,9},{9,10},{10,1... | collective-permute-start | bytes 786440 | tf_op jit(solution)/shard_map/ppermute | solution.py:332
  5.0 1.2 copy-start.1
  6.2 1.2 copy-start.2
  19.1 61.4 %copy-start = (f32[1,256,256]{2,1,0:T(8,128)S(1)}, f32[1,256,256]{2,1,0:T(8,128)}, u32[]{:S(2)}) copy-start(f32[1,256,256]{2,1,0:T(8,128)} %param.7) | copy-start | bytes 786436
  48.2 11.4 %collective-permute-start.2 = (f32[8,128]{1,0:T(8,128)S(1)}, f32[8,128]{1,0:T(8,128)S(1)}, u32[]{:S(2)}, u32[]{:S(2)}) collective-permute-start(f32[8,128]{1,0:T(8,128)S(1)} %fusion.13), channel_id=1, source_target_pairs={{0,0},{1,1},{2,2},{3,3},{4,4},{5,5},{6,6},{7,7},{8,8},{9,9},{10,10... | collective-permute-start | bytes 12296 | tf_op jit(solution)/shard_map/ppermute | solution.py:307
  106.7 8.5 %collective-permute-start.3 = (f32[8,128]{1,0:T(8,128)S(1)}, f32[8,128]{1,0:T(8,128)S(1)}, u32[]{:S(2)}, u32[]{:S(2)}) collective-permute-start(f32[8,128]{1,0:T(8,128)S(1)} %fusion.12), channel_id=1, source_target_pairs={{0,0},{1,1},{2,2},{3,3},{4,4},{5,5},{6,6},{7,7},{8,8},{9,9},{10,10... | collective-permute-start | bytes 12296 | tf_op jit(solution)/shard_map/ppermute | solution.py:307
  159.2 8.5 %collective-permute-start.4 = (f32[8,128]{1,0:T(8,128)S(1)}, f32[8,128]{1,0:T(8,128)S(1)}, u32[]{:S(2)}, u32[]{:S(2)}) collective-permute-start(f32[8,128]{1,0:T(8,128)S(1)} %fusion.11), channel_id=1, source_target_pairs={{0,0},{1,1},{2,2},{3,3},{4,4},{5,5},{6,6},{7,7},{8,8},{9,9},{10,10... | collective-permute-start | bytes 12296 | tf_op jit(solution)/shard_map/ppermute | solution.py:307
  212.2 5.6 %collective-permute-start.5 = (f32[8,128]{1,0:T(8,128)S(1)}, f32[8,128]{1,0:T(8,128)S(1)}, u32[]{:S(2)}, u32[]{:S(2)}) collective-permute-start(f32[8,128]{1,0:T(8,128)S(1)} %fusion.10), channel_id=1, source_target_pairs={{0,0},{1,1},{2,2},{3,3},{4,4},{5,5},{6,6},{7,7},{8,8},{9,9},{10,10... | collective-permute-start | bytes 12296 | tf_op jit(solution)/shard_map/ppermute | solution.py:307

commit v6 on v5

--- a/solution.py
+++ b/solution.py
@@ -45,9 +45,8 @@
 
 
 def prepare_kernel(left, right, left_high, left_low, right_high, right_low):
-    for term in range(left.shape[0]):
-        left_high[term], left_low[term] = split(left[term])
-        right_high[term], right_low[term] = split(right[term])
+    left_high[0], left_low[0] = split(left[0])
+    right_high[0], right_low[0] = split(right[0])
 
 
 def apply_terms(info, ops, t_high, t_low, t_own, v_own, r_own, part):
@@ -217,11 +216,13 @@
 
 def run_prepare(left, right):
     part = jax.ShapeDtypeStruct(left.shape, BF16)
+    one = pl.BlockSpec((1, M, M), lambda term: (term, 0, 0))
     return pl.pallas_call(
         prepare_kernel,
         out_shape=(part,) * 4,
-        in_specs=[VMEM] * 2,
-        out_specs=(VMEM,) * 4,
+        grid=(left.shape[0],),
+        in_specs=[one] * 2,
+        out_specs=(one,) * 4,
         compiler_params=PARAMS,
         cost_estimate=pl.CostEstimate(flops=4 * left.size, bytes_accessed=16 * left.size, transcendentals=0),
         name="prepare",

time: 237 us -> 237 us (level)
  no operation moved by 1% of the time
where the time goes in v6:
time: 237 us; the launch traced here: 236 us
  blocking collectives  201 us (85%)
  starting transfers between devices  12.7 us (5%)
  Pallas kernels  10.9 us (5%)
  waiting for transfers between devices  5.8 us (2%)
  local copies, waits for them, and re-layouts  2.45 us (1%)
    all_gather x4, blocking collectives, exchange(): lax.all_gather(jnp.concatenate(parts + [spread], axis=0), TERM, axis=0)  75.4 us
    all_to_all x4, blocking collectives, exchange(): pieces = lax.all_to_all(part, 'z', 0, 0, tiled=True)  71.7 us
    all_gather x4, blocking collectives, exchange(): four = lax.all_gather(summed, ('xl', 'core'), axis=0)  24.7 us
    all_gather x3, blocking collectives, exchange(): two = lax.all_gather(own, BLOCK, axis=0, axis_index_groups=shifted)  20.1 us
    ppermute x4, starting transfers between devices, exchange(): spread = lax.ppermute(low[ROWS:] + high[ROWS:], ALL, spread_pairs())  10.1 us
    all_gather x2, blocking collectives, gather_core(): return lax.all_gather(block, 'core', axis=0)  9.05 us
    pallas_call x3, Pallas kernels, run_step(): pl.pallas_call(body, out_shape=(shape(SCAL, 128), shape(9, M, M), PART),...  7.07 us
  transfers between devices with their start and end apart: 6, of which 2 were waited for; matrix products, arithmetic and copies ran while one was open for 0% of the time, Pallas kernels for 0%

profile of v6, /device:TPU:1, one launch (start us, length us, event | category | flops | bytes accessed | tf_op | source)
XLA Modules:
  0.0 235.9 jit_solution(3418515918746820600)
XLA Ops:
  0.6 0.0 copy-start.3
  1.3 1.1 bitcast_select_fusion.x_own.refs_6_
  2.4 1.3 collective-permute-start
  3.7 1.3 collective-permute-start.1
  5.0 0.0 copy-start.1
  5.0 1.2 copy-done.1
  6.2 0.0 copy-start.2
  6.2 1.2 copy-done.2
  7.4 0.4 prepare.1
  7.8 0.0 copy-done.3
  7.8 0.1 pad_add_fusion.info.refs_0_
  7.9 2.2 collective-permute-done
  10.1 6.5 %all-gather = f32[512,256]{1,0:T(8,128)S(1)} all-gather(f32[256,256]{1,0:T(8,128)S(1)} %collective-permute-done), channel_id=2, replica_groups=mesh['z'=8,'core'=2,'y'=8,'xh'=2,'xl'=2] {'core'}, dimensions={0}, use_global_device_ids=true | all-gather | bytes 786432 | tf_op jit(solution)/shard_map/all_gather | solution.py:300
  16.6 0.0 collective-permute-done.1
  16.6 2.5 %all-gather.1 = f32[512,256]{1,0:T(8,128)S(1)} all-gather(f32[256,256]{1,0:T(8,128)S(1)} %collective-permute-done.1), channel_id=3, replica_groups=mesh['z'=8,'core'=2,'y'=8,'xh'=2,'xl'=2] {'core'}, dimensions={0}, use_global_device_ids=true | all-gather | bytes 786432 | tf_op jit(solution)/shard_map/all_gather | solution.py:300
  19.1 0.0 copy-start
  19.1 1.9 first.1
  21.0 20.5 %all_to_all.20 = f32[8,72,128]{2,1,0:T(8,128)S(1)} all-to-all(f32[8,72,128]{2,1,0:T(8,128)S(1)} %first.1), channel_id=1, replica_groups=mesh['z'=8,'core'=2,'y'=8,'xh'=2,'xl'=2] {'z'}, dimensions={0} | all-to-all | bytes 589824 | tf_op jit(solution)/shard_map/all_to_all | solution.py:304
  41.5 6.7 %all_gather.68 = f32[4,72,128]{2,1,0:T(8,128)S(1)} all-gather(f32[1,72,128]{2,1,0:T(8,128)S(1)} %slice_add_fusion.29), channel_id=1, replica_groups=mesh['z'=8,'core'=2,'y'=8,'xh'=2,'xl'=2] {'xl','core'}, dimensions={0}, use_global_device_ids=true | all-gather | bytes 184320 | tf_op jit(solution)/shard_map/all_gather | solution.py:306
  48.3 4.4 %collective-permute-start.2 = (f32[8,128]{1,0:T(8,128)S(1)}, f32[8,128]{1,0:T(8,128)S(1)}, u32[]{:S(2)}, u32[]{:S(2)}) collective-permute-start(f32[8,128]{1,0:T(8,128)S(1)} %fusion.13), channel_id=1, source_target_pairs={{0,0},{1,1},{2,2},{3,3},{4,4},{5,5},{6,6},{7,7},{8,8},{9,9},{10,10... | collective-permute-start | bytes 12296 | tf_op jit(solution)/shard_map/ppermute | solution.py:308
  52.7 6.9 %all_gather.69 = f32[2,32,128]{2,1,0:T(8,128)S(1)} all-gather(f32[1,32,128]{2,1,0:T(8,128)S(1)} %slice_select_fusion.9), channel_id=1, replica_groups={{1,2},{3,4},{5,6},{7,8},{9,10},{11,12},{13,14},{15,16},{17,18},{19,20},..., dimensions={0}, use_global_device_ids=true | all-gather | bytes 49152 | tf_op jit(solution)/shard_map/all_gather | solution.py:319
  59.6 0.0 collective-permute-done.2
  59.6 20.9 %all-gather.2 = f32[1664,128]{1,0:T(8,128)S(1)} all-gather(f32[104,128]{1,0:T(8,128)S(1)} %pad_maximum_fusion), channel_id=4, replica_groups=mesh['z'=8,'core'=2,'y'=8,'xh'=2,'xl'=2] {'z','core'}, dimensions={0}, use_global_device_ids=true | all-gather | bytes 905216 | tf_op jit(solution)/shard_map/all_gather | solution.py:321
  80.5 0.0 copy-done
  80.5 2.2 step.3
  82.8 17.8 %all_to_all.21 = f32[8,72,128]{2,1,0:T(8,128)S(1)} all-to-all(f32[8,72,128]{2,1,0:T(8,128)S(1)} %get-tuple-element.30), channel_id=1, replica_groups=mesh['z'=8,'core'=2,'y'=8,'xh'=2,'xl'=2] {'z'}, dimensions={0} | all-to-all | bytes 589824 | tf_op jit(solution)/shard_map/all_to_all | solution.py:304
  100.6 6.0 %all_gather.72 = f32[4,72,128]{2,1,0:T(8,128)S(1)} all-gather(f32[1,72,128]{2,1,0:T(8,128)S(1)} %slice_add_fusion.20), channel_id=1, replica_groups=mesh['z'=8,'core'=2,'y'=8,'xh'=2,'xl'=2] {'xl','core'}, dimensions={0}, use_global_device_ids=true | all-gather | bytes 184320 | tf_op jit(solution)/shard_map/all_gather | solution.py:306
  106.7 1.9 collective-permute-start.3
  108.6 6.6 %all_gather.73 = f32[2,32,128]{2,1,0:T(8,128)S(1)} all-gather(f32[1,32,128]{2,1,0:T(8,128)S(1)} %slice_select_fusion.6), channel_id=1, replica_groups={{1,2},{3,4},{5,6},{7,8},{9,10},{11,12},{13,14},{15,16},{17,18},{19,20},..., dimensions={0}, use_global_device_ids=true | all-gather | bytes 49152 | tf_op jit(solution)/shard_map/all_gather | solution.py:319
  115.2 0.0 collective-permute-done.3
  115.2 19.5 %all-gather.3 = f32[1664,128]{1,0:T(8,128)S(1)} all-gather(f32[104,128]{1,0:T(8,128)S(1)} %pad_maximum_fusion.1), channel_id=5, replica_groups=mesh['z'=8,'core'=2,'y'=8,'xh'=2,'xl'=2] {'z','core'}, dimensions={0}, use_global_device_ids=true | all-gather | bytes 905216 | tf_op jit(solution)/shard_map/all_gather | solution.py:321
  134.7 2.4 %step.4 = (f32[8,128]{1,0:T(8,128)S(1)}, f32[9,256,256]{2,1,0:T(8,128)S(1)}, f32[8,72,128]{2,1,0:T(8,128)S(1)}) custom-call(s32[6]{0:T(128)S(1)} %pad_add_fusion.info.refs_0_, bf16[4,256,256]{2,1,0:T(8,128)(2,1)S(1)} %get-tuple-element.23.lh.refs_1_, bf16[4,256,256]{2,1,0:T(8,128)(2,1)S(1)} %get-tuple-element.24.ll.refs_2_, ...), custom_call_target="tpu_custom_call", output_to_operand_aliasing={{1}: (8, {})} | custom-call | tf_op jit(solution)/shard_map/step/pallas_call | solution.py:248
  137.1 16.0 %all_to_all.22 = f32[8,72,128]{2,1,0:T(8,128)S(1)} all-to-all(f32[8,72,128]{2,1,0:T(8,128)S(1)} %get-tuple-element.33), channel_id=1, replica_groups=mesh['z'=8,'core'=2,'y'=8,'xh'=2,'xl'=2] {'z'}, dimensions={0} | all-to-all | bytes 589824 | tf_op jit(solution)/shard_map/all_to_all | solution.py:304
  153.1 6.0 %all_gather.76 = f32[4,72,128]{2,1,0:T(8,128)S(1)} all-gather(f32[1,72,128]{2,1,0:T(8,128)S(1)} %slice_add_fusion.11), channel_id=1, replica_groups=mesh['z'=8,'core'=2,'y'=8,'xh'=2,'xl'=2] {'xl','core'}, dimensions={0}, use_global_device_ids=true | all-gather | bytes 184320 | tf_op jit(solution)/shard_map/all_gather | solution.py:306
  159.2 1.9 collective-permute-start.4
  161.2 6.6 %all_gather.77 = f32[2,32,128]{2,1,0:T(8,128)S(1)} all-gather(f32[1,32,128]{2,1,0:T(8,128)S(1)} %slice_select_fusion.3), channel_id=1, replica_groups={{1,2},{3,4},{5,6},{7,8},{9,10},{11,12},{13,14},{15,16},{17,18},{19,20},..., dimensions={0}, use_global_device_ids=true | all-gather | bytes 49152 | tf_op jit(solution)/shard_map/all_gather | solution.py:319
  167.8 0.0 collective-permute-done.4
  167.8 18.5 %all-gather.4 = f32[1664,128]{1,0:T(8,128)S(1)} all-gather(f32[104,128]{1,0:T(8,128)S(1)} %pad_maximum_fusion.2), channel_id=6, replica_groups=mesh['z'=8,'core'=2,'y'=8,'xh'=2,'xl'=2] {'z','core'}, dimensions={0}, use_global_device_ids=true | all-gather | bytes 905216 | tf_op jit(solution)/shard_map/all_gather | solution.py:321
  186.3 2.4 %step.5 = (f32[8,128]{1,0:T(8,128)S(1)}, f32[9,256,256]{2,1,0:T(8,128)S(1)}, f32[8,72,128]{2,1,0:T(8,128)S(1)}) custom-call(s32[6]{0:T(128)S(1)} %pad_add_fusion.info.refs_0_, bf16[4,256,256]{2,1,0:T(8,128)(2,1)S(1)} %get-tuple-element.23.lh.refs_1_, bf16[4,256,256]{2,1,0:T(8,128)(2,1)S(1)} %get-tuple-element.24.ll.refs_2_, ...), custom_call_target="tpu_custom_call", output_to_operand_aliasing={{1}: (8, {})} | custom-call | tf_op jit(solution)/shard_map/step/pallas_call | solution.py:248
  188.7 17.4 %all_to_all.23 = f32[8,72,128]{2,1,0:T(8,128)S(1)} all-to-all(f32[8,72,128]{2,1,0:T(8,128)S(1)} %get-tuple-element.36), channel_id=1, replica_groups=mesh['z'=8,'core'=2,'y'=8,'xh'=2,'xl'=2] {'z'}, dimensions={0} | all-to-all | bytes 589824 | tf_op jit(solution)/shard_map/all_to_all | solution.py:304
  206.2 6.0 %all_gather.80 = f32[4,72,128]{2,1,0:T(8,128)S(1)} all-gather(f32[1,72,128]{2,1,0:T(8,128)S(1)} %slice_add_fusion.2), channel_id=1, replica_groups=mesh['z'=8,'core'=2,'y'=8,'xh'=2,'xl'=2] {'xl','core'}, dimensions={0}, use_global_device_ids=true | all-gather | bytes 184320 | tf_op jit(solution)/shard_map/all_gather | solution.py:306
  212.2 1.9 collective-permute-start.5
  214.1 3.6 %collective-permute-done.5 = f32[8,128]{1,0:T(8,128)S(1)} collective-permute-done((f32[8,128]{1,0:T(8,128)S(1)}, f32[8,128]{1,0:T(8,128)S(1)}, u32[]{:S(2)}, u32[]{:S(2)}) %collective-permute-start.5) | collective-permute-done | bytes 4128 | tf_op jit(solution)/shard_map/ppermute | solution.py:308
  217.8 16.5 %all-gather.5 = f32[640,128]{1,0:T(8,128)S(1)} all-gather(f32[40,128]{1,0:T(8,128)S(1)} %pad_maximum_fusion.3), channel_id=7, replica_groups=mesh['z'=8,'core'=2,'y'=8,'xh'=2,'xl'=2] {'z','core'}, dimensions={0}, use_global_device_ids=true | all-gather | bytes 348160 | tf_op jit(solution)/shard_map/all_gather | solution.py:321
  234.2 1.6 last.1
  (33 shorter events, 0.3 us)
Async XLA Ops:
  0.6 7.2 %copy-start.3 = (s32[4,1]{0,1:T(1,128)S(1)}, s32[4,1]{0,1:T(1,128)}, u32[]{:S(2)}) copy-start(s32[4,1]{0,1:T(1,128)} %param.10) | copy-start | bytes 52
  2.4 7.7 %collective-permute-start = (f32[256,256]{1,0:T(8,128)S(1)}, f32[256,256]{1,0:T(8,128)S(1)}, u32[]{:S(2)}, u32[]{:S(2)}) collective-permute-start(f32[256,256]{1,0:T(8,128)S(1)} %bitcast_select_fusion.x_own.refs_6_), channel_id=1, source_target_pairs={{0,1},{1,2},{2,3},{3,4},{4,5},{5,6},{6,7},{7,8},{8,9},{9,10},{10,1... | collective-permute-start | bytes 786440 | tf_op jit(solution)/shard_map/ppermute | solution.py:332
  3.7 12.9 %collective-permute-start.1 = (f32[256,256]{1,0:T(8,128)}, f32[256,256]{1,0:T(8,128)S(1)}, u32[]{:S(2)}, u32[]{:S(2)}) collective-permute-start(f32[256,256]{1,0:T(8,128)} %bitcast.51), channel_id=1, source_target_pairs={{0,1},{1,2},{2,3},{3,4},{4,5},{5,6},{6,7},{7,8},{8,9},{9,10},{10,1... | collective-permute-start | bytes 786440 | tf_op jit(solution)/shard_map/ppermute | solution.py:333
  5.0 1.2 copy-start.1
  6.2 1.2 copy-start.2
  19.1 61.4 %copy-start = (f32[1,256,256]{2,1,0:T(8,128)S(1)}, f32[1,256,256]{2,1,0:T(8,128)}, u32[]{:S(2)}) copy-start(f32[1,256,256]{2,1,0:T(8,128)} %param.7) | copy-start | bytes 786436
  48.3 11.3 %collective-permute-start.2 = (f32[8,128]{1,0:T(8,128)S(1)}, f32[8,128]{1,0:T(8,128)S(1)}, u32[]{:S(2)}, u32[]{:S(2)}) collective-permute-start(f32[8,128]{1,0:T(8,128)S(1)} %fusion.13), channel_id=1, source_target_pairs={{0,0},{1,1},{2,2},{3,3},{4,4},{5,5},{6,6},{7,7},{8,8},{9,9},{10,10... | collective-permute-start | bytes 12296 | tf_op jit(solution)/shard_map/ppermute | solution.py:308
  106.7 8.5 %collective-permute-start.3 = (f32[8,128]{1,0:T(8,128)S(1)}, f32[8,128]{1,0:T(8,128)S(1)}, u32[]{:S(2)}, u32[]{:S(2)}) collective-permute-start(f32[8,128]{1,0:T(8,128)S(1)} %fusion.12), channel_id=1, source_target_pairs={{0,0},{1,1},{2,2},{3,3},{4,4},{5,5},{6,6},{7,7},{8,8},{9,9},{10,10... | collective-permute-start | bytes 12296 | tf_op jit(solution)/shard_map/ppermute | solution.py:308
  159.2 8.5 %collective-permute-start.4 = (f32[8,128]{1,0:T(8,128)S(1)}, f32[8,128]{1,0:T(8,128)S(1)}, u32[]{:S(2)}, u32[]{:S(2)}) collective-permute-start(f32[8,128]{1,0:T(8,128)S(1)} %fusion.11), channel_id=1, source_target_pairs={{0,0},{1,1},{2,2},{3,3},{4,4},{5,5},{6,6},{7,7},{8,8},{9,9},{10,10... | collective-permute-start | bytes 12296 | tf_op jit(solution)/shard_map/ppermute | solution.py:308
  212.2 5.6 %collective-permute-start.5 = (f32[8,128]{1,0:T(8,128)S(1)}, f32[8,128]{1,0:T(8,128)S(1)}, u32[]{:S(2)}, u32[]{:S(2)}) collective-permute-start(f32[8,128]{1,0:T(8,128)S(1)} %fusion.10), channel_id=1, source_target_pairs={{0,0},{1,1},{2,2},{3,3},{4,4},{5,5},{6,6},{7,7},{8,8},{9,9},{10,10... | collective-permute-start | bytes 12296 | tf_op jit(solution)/shard_map/ppermute | solution.py:308

commit v7 on v5

--- a/solution.py
+++ b/solution.py
@@ -163,20 +163,21 @@
 def step_kernel(iteration, *refs):
     first = iteration == 0
     if first:
-        (info, lh, ll, rh, rl, gathered, x_own, x_side, d_own, d_side, state_out, out, part, t_high, t_low) = refs
+        (info, lh, ll, rh, rl, gathered, x_own, x_side, d_own, d_got, d_far, state_out, out, part, t_high, t_low) = refs
         old = state = None
     else:
-        (info, lh, ll, rh, rl, gathered, d_own, d_side, old, state, state_out, out, part, t_high, t_low) = refs
+        (info, lh, ll, rh, rl, gathered, d_own, d_got, d_far, old, state, state_out, out, part, t_high, t_low) = refs
     weights, now, lowest = scalars(first, global_sums(info, gathered, 3 * PIECE), state)
     rho, scale = now[0], now[3]
     state_out[...] = state_rows(now, lowest, state, iteration)
     odd = info[0] & 1
     for block in (0, 2, 1):
         at = 0 if block == 1 else pl.multiple_of(PIECE * (2 - odd if block == 0 else 1 + odd), PIECE)
+        near = info[6] == block // 2
         for z in range(ZS):
             rows = pl.ds(z * PIECE, PIECE)
             halves = [gathered[CORES * z + c, pl.ds(at, PIECE)] for c in range(CORES)]
-            diag = d_own[rows] if block == 1 else d_side[block // 2, rows]
+            diag = d_own[rows] if block == 1 else jnp.where(near, d_got[rows], d_far[rows])
             image = jnp.concatenate(halves, axis=1)
             if first:
                 x = x_own[rows] if block == 1 else x_side[block // 2, rows]
@@ -250,7 +251,7 @@
         in_specs=[SMEM] + [VMEM] * len(arrays),
         out_specs=(VMEM,) * 3,
         scratch_shapes=SPLITS,
-        input_output_aliases={8: 1} if iteration else {},
+        input_output_aliases={9: 1} if iteration else {},
         compiler_params=PARAMS,
         name="step",
     )(info, *arrays)
@@ -321,22 +322,23 @@
 
 
 def per_device(start, diagonal, left_ops, right_ops, offsets, sizes):
-    info = jnp.concatenate([lax.axis_index(BLOCK)[None].astype(jnp.int32), sizes, offsets[:, 0]])
+    info = jnp.concatenate([lax.axis_index(BLOCK)[None].astype(jnp.int32), sizes, offsets[:, 0],
+                            lax.axis_index("core")[None].astype(jnp.int32)])
     live = jnp.arange(M, dtype=jnp.int32) < sizes[0]
     x_own = jnp.where(live[:, None] & live[None, :], start[0], 0.0)
     d_own = diagonal[0]
     b = lax.axis_index(BLOCK)
     place = (lax.axis_index("xl") == 1, lax.axis_index("core") == 1, (b == 0) | (b == BLOCKS - 1))
-    x_side, d_side, place = lax.optimization_barrier(
-        (gather_core(lax.ppermute(x_own, ALL, halo_pairs())),
-         gather_core(lax.ppermute(d_own, ALL, halo_pairs())), place))
+    x_side, d_got, place = lax.optimization_barrier(
+        (gather_core(lax.ppermute(x_own, ALL, halo_pairs())), lax.ppermute(d_own, ALL, halo_pairs()), place))
+    d_side = (d_got, lax.ppermute(d_got, "core", [(0, 1), (1, 0)]))
     ops = run_prepare(left_ops[:, 0], right_ops[:, 0])
     part = run_first(info, *ops, x_own, x_side)
     gathered = exchange(part, place, True)
-    state, kept, part = run_step(0, info, *ops, gathered, x_own, x_side, d_own, d_side)
+    state, kept, part = run_step(0, info, *ops, gathered, x_own, x_side, d_own, *d_side)
     for iteration in range(1, ITERS):
         gathered = exchange(part, place, True)
-        state, kept, part = run_step(iteration, info, *ops, gathered, d_own, d_side, kept, state)
+        state, kept, part = run_step(iteration, info, *ops, gathered, d_own, *d_side, kept, state)
     gathered = exchange(part, place, False)
     wave, image, energies = run_last(info, gathered, kept, state)
     return wave, image, energies

time: 237 us -> 236 us (level)
  blocking collectives: 201 us -> 176 us
  starting transfers between devices: 12.7 us -> 24.6 us
  waiting for transfers between devices: 5.85 us -> 15.8 us
    all_to_all x4 -> x3, blocking collectives: 71.6 us -> 50.7 us  [exchange(): pieces = lax.all_to_all(part, 'z', 0, 0, tiled=True)]
    all_to_all x0 -> x1, waiting for transfers between devices: none -> 9.96 us  [exchange(): pieces = lax.all_to_all(part, 'z', 0, 0, tiled=True)]
    all_to_all x0 -> x1, starting transfers between devices: none -> 8.86 us  [exchange(): pieces = lax.all_to_all(part, 'z', 0, 0, tiled=True)]
    all_gather x2 -> x1, blocking collectives: 9.05 us -> 6.5 us  [gather_core(): return lax.all_gather(block, 'core', axis=0)]
    ppermute x0 -> x1, starting transfers between devices: none -> 2.55 us  [per_device(): d_side = (d_got, lax.ppermute(d_got, 'core', [(0, 1), (1, 0)]))]
  transfers between devices with their start and end apart: 6 -> 8, of which waited for: 2 -> 3; matrix products, arithmetic and copies ran while one was open for 0% -> 0% of each run, Pallas kernels for 0% -> 0%
where the time goes in v7:
time: 236 us; the launch traced here: 235 us
  blocking collectives  176 us (75%)
  starting transfers between devices  24.6 us (10%)
  waiting for transfers between devices  15.8 us (7%)
  Pallas kernels  10.9 us (5%)
  local copies, waits for them, and re-layouts  4.11 us (2%)
    all_gather x4, blocking collectives, exchange(): lax.all_gather(jnp.concatenate(parts + [spread], axis=0), TERM, axis=0)  74.2 us
    all_to_all x3, blocking collectives, exchange(): pieces = lax.all_to_all(part, 'z', 0, 0, tiled=True)  50.7 us
    all_gather x4, blocking collectives, exchange(): four = lax.all_gather(summed, ('xl', 'core'), axis=0)  24.5 us
    all_gather x3, blocking collectives, exchange(): two = lax.all_gather(own, BLOCK, axis=0, axis_index_groups=shifted)  19.8 us
    ppermute x4, starting transfers between devices, exchange(): spread = lax.ppermute(low[ROWS:] + high[ROWS:], ALL, spread_pairs())  10.6 us
    all_to_all x1, waiting for transfers between devices, exchange(): pieces = lax.all_to_all(part, 'z', 0, 0, tiled=True)  9.96 us
    all_to_all x1, starting transfers between devices, exchange(): pieces = lax.all_to_all(part, 'z', 0, 0, tiled=True)  8.86 us
    pallas_call x3, Pallas kernels, run_step(): pl.pallas_call(body, out_shape=(shape(SCAL, 128), shape(9, M, M), PART),...  7.11 us
  transfers between devices with their start and end apart: 8, of which 3 were waited for; matrix products, arithmetic and copies ran while one was open for 0% of the time, Pallas kernels for 0%

profile of v7, /device:TPU:1, one launch (start us, length us, event | category | flops | bytes accessed | tf_op | source)
XLA Modules:
  0.0 235.2 jit_solution(5795082741883835140)
XLA Ops:
  0.6 0.0 copy-start.6
  1.3 1.1 bitcast_select_fusion.x_own.refs_6_
  2.4 0.0 copy-start.1
  2.4 1.3 collective-permute-start
  3.7 1.3 collective-permute-start.1
  5.0 0.0 copy-start.4
  5.0 1.2 copy-done.4
  6.2 1.2 copy-done.5
  7.5 0.3 prepare.1
  7.8 0.0 copy-done.6
  7.8 0.1 pad_add_fusion.info.refs_0_
  7.9 2.2 collective-permute-done
  10.1 6.5 %all-gather = f32[512,256]{1,0:T(8,128)S(1)} all-gather(f32[256,256]{1,0:T(8,128)S(1)} %collective-permute-done), channel_id=2, replica_groups=mesh['z'=8,'core'=2,'y'=8,'xh'=2,'xl'=2] {'core'}, dimensions={0}, use_global_device_ids=true | all-gather | bytes 786432 | tf_op jit(solution)/shard_map/all_gather | solution.py:300
  16.6 0.0 collective-permute-done.1.refs_9_.refs_7_
  16.6 1.9 first.1
  18.5 0.7 copy-done.3
  19.2 8.9 %all-to-all-start = ((f32[8,72,128]{2,1,0:T(8,128)}), f32[8,72,128]{2,1,0:T(8,128)}, u32[]{:S(2)}, u32[]{:S(2)}) async-start(f32[8,72,128]{2,1,0:T(8,128)} %copy-done.3), calls=%async_computation | async-start | bytes 589824 | tf_op jit(solution)/shard_map/all_to_all | solution.py:304
  28.1 2.5 %collective-permute-start.3 = (f32[256,256]{1,0:T(8,128)S(1)}, f32[256,256]{1,0:T(8,128)S(1)}, u32[]{:S(2)}, u32[]{:S(2)}) collective-permute-start(f32[256,256]{1,0:T(8,128)S(1)} %collective-permute-done.1.refs_9_.refs_7_), channel_id=1, source_target_pairs={{0,32},{32,0},{1,33},{33,1},{2,34},{34,2},{3,35},{35,3},{4,36},{36... | collective-permute-start | bytes 786440 | tf_op jit(solution)/shard_map/ppermute | solution.py:334
  30.6 10.0 %all-to-all-done = f32[8,72,128]{2,1,0:T(8,128)} async-done(((f32[8,72,128]{2,1,0:T(8,128)}), f32[8,72,128]{2,1,0:T(8,128)}, u32[]{:S(2)}, u32[]{:S(2)}) %all-to-all-start) | async-done | bytes 294944 | tf_op jit(solution)/shard_map/all_to_all | solution.py:304
  40.6 0.9 slice_add_fusion.29
  41.5 6.4 %all_gather.60 = f32[4,72,128]{2,1,0:T(8,128)S(1)} all-gather(f32[1,72,128]{2,1,0:T(8,128)S(1)} %slice_add_fusion.29), channel_id=1, replica_groups=mesh['z'=8,'core'=2,'y'=8,'xh'=2,'xl'=2] {'xl','core'}, dimensions={0}, use_global_device_ids=true | all-gather | bytes 184320 | tf_op jit(solution)/shard_map/all_gather | solution.py:306
  48.0 4.4 %collective-permute-start.2 = (f32[8,128]{1,0:T(8,128)S(1)}, f32[8,128]{1,0:T(8,128)S(1)}, u32[]{:S(2)}, u32[]{:S(2)}) collective-permute-start(f32[8,128]{1,0:T(8,128)S(1)} %fusion.13), channel_id=1, source_target_pairs={{0,0},{1,1},{2,2},{3,3},{4,4},{5,5},{6,6},{7,7},{8,8},{9,9},{10,10... | collective-permute-start | bytes 12296 | tf_op jit(solution)/shard_map/ppermute | solution.py:308
  52.4 6.6 %all_gather.61 = f32[2,32,128]{2,1,0:T(8,128)S(1)} all-gather(f32[1,32,128]{2,1,0:T(8,128)S(1)} %slice_select_fusion.9), channel_id=1, replica_groups={{1,2},{3,4},{5,6},{7,8},{9,10},{11,12},{13,14},{15,16},{17,18},{19,20},..., dimensions={0}, use_global_device_ids=true | all-gather | bytes 49152 | tf_op jit(solution)/shard_map/all_gather | solution.py:319
  59.0 0.0 collective-permute-done.2
  59.0 19.8 %all-gather.1 = f32[1664,128]{1,0:T(8,128)S(1)} all-gather(f32[104,128]{1,0:T(8,128)S(1)} %pad_maximum_fusion), channel_id=3, replica_groups=mesh['z'=8,'core'=2,'y'=8,'xh'=2,'xl'=2] {'z','core'}, dimensions={0}, use_global_device_ids=true | all-gather | bytes 905216 | tf_op jit(solution)/shard_map/all_gather | solution.py:321
  78.8 0.0 collective-permute-done.3.refs_10_.refs_8_
  78.8 0.9 copy-done.2
  79.8 2.3 step.3
  82.0 17.7 %all_to_all.20 = f32[8,72,128]{2,1,0:T(8,128)S(1)} all-to-all(f32[8,72,128]{2,1,0:T(8,128)S(1)} %get-tuple-element.30), channel_id=1, replica_groups=mesh['z'=8,'core'=2,'y'=8,'xh'=2,'xl'=2] {'z'}, dimensions={0} | all-to-all | bytes 589824 | tf_op jit(solution)/shard_map/all_to_all | solution.py:304
  99.8 6.0 %all_gather.64 = f32[4,72,128]{2,1,0:T(8,128)S(1)} all-gather(f32[1,72,128]{2,1,0:T(8,128)S(1)} %slice_add_fusion.20), channel_id=1, replica_groups=mesh['z'=8,'core'=2,'y'=8,'xh'=2,'xl'=2] {'xl','core'}, dimensions={0}, use_global_device_ids=true | all-gather | bytes 184320 | tf_op jit(solution)/shard_map/all_gather | solution.py:306
  105.9 2.0 collective-permute-start.4
  107.9 6.6 %all_gather.65 = f32[2,32,128]{2,1,0:T(8,128)S(1)} all-gather(f32[1,32,128]{2,1,0:T(8,128)S(1)} %slice_select_fusion.6), channel_id=1, replica_groups={{1,2},{3,4},{5,6},{7,8},{9,10},{11,12},{13,14},{15,16},{17,18},{19,20},..., dimensions={0}, use_global_device_ids=true | all-gather | bytes 49152 | tf_op jit(solution)/shard_map/all_gather | solution.py:319
  114.5 0.0 collective-permute-done.4
  114.6 19.3 %all-gather.2 = f32[1664,128]{1,0:T(8,128)S(1)} all-gather(f32[104,128]{1,0:T(8,128)S(1)} %pad_maximum_fusion.1), channel_id=4, replica_groups=mesh['z'=8,'core'=2,'y'=8,'xh'=2,'xl'=2] {'z','core'}, dimensions={0}, use_global_device_ids=true | all-gather | bytes 905216 | tf_op jit(solution)/shard_map/all_gather | solution.py:321
  133.9 2.4 %step.4 = (f32[8,128]{1,0:T(8,128)S(1)}, f32[9,256,256]{2,1,0:T(8,128)S(1)}, f32[8,72,128]{2,1,0:T(8,128)S(1)}) custom-call(s32[7]{0:T(128)S(1)} %pad_add_fusion.info.refs_0_, bf16[4,256,256]{2,1,0:T(8,128)(2,1)S(1)} %get-tuple-element.23.lh.refs_1_, bf16[4,256,256]{2,1,0:T(8,128)(2,1)S(1)} %get-tuple-element.24.ll.refs_2_, ...), custom_call_target="tpu_custom_call", output_to_operand_aliasing={{1}: (9, {})} | custom-call | tf_op jit(solution)/shard_map/step/pallas_call | solution.py:248
  136.3 16.1 %all_to_all.21 = f32[8,72,128]{2,1,0:T(8,128)S(1)} all-to-all(f32[8,72,128]{2,1,0:T(8,128)S(1)} %get-tuple-element.33), channel_id=1, replica_groups=mesh['z'=8,'core'=2,'y'=8,'xh'=2,'xl'=2] {'z'}, dimensions={0} | all-to-all | bytes 589824 | tf_op jit(solution)/shard_map/all_to_all | solution.py:304
  152.4 6.0 %all_gather.68 = f32[4,72,128]{2,1,0:T(8,128)S(1)} all-gather(f32[1,72,128]{2,1,0:T(8,128)S(1)} %slice_add_fusion.11), channel_id=1, replica_groups=mesh['z'=8,'core'=2,'y'=8,'xh'=2,'xl'=2] {'xl','core'}, dimensions={0}, use_global_device_ids=true | all-gather | bytes 184320 | tf_op jit(solution)/shard_map/all_gather | solution.py:306
  158.5 2.3 collective-permute-start.5
  160.9 6.6 %all_gather.69 = f32[2,32,128]{2,1,0:T(8,128)S(1)} all-gather(f32[1,32,128]{2,1,0:T(8,128)S(1)} %slice_select_fusion.3), channel_id=1, replica_groups={{1,2},{3,4},{5,6},{7,8},{9,10},{11,12},{13,14},{15,16},{17,18},{19,20},..., dimensions={0}, use_global_device_ids=true | all-gather | bytes 49152 | tf_op jit(solution)/shard_map/all_gather | solution.py:319
  167.5 0.0 collective-permute-done.5
  167.5 18.6 %all-gather.3 = f32[1664,128]{1,0:T(8,128)S(1)} all-gather(f32[104,128]{1,0:T(8,128)S(1)} %pad_maximum_fusion.2), channel_id=5, replica_groups=mesh['z'=8,'core'=2,'y'=8,'xh'=2,'xl'=2] {'z','core'}, dimensions={0}, use_global_device_ids=true | all-gather | bytes 905216 | tf_op jit(solution)/shard_map/all_gather | solution.py:321
  186.1 2.4 %step.5 = (f32[8,128]{1,0:T(8,128)S(1)}, f32[9,256,256]{2,1,0:T(8,128)S(1)}, f32[8,72,128]{2,1,0:T(8,128)S(1)}) custom-call(s32[7]{0:T(128)S(1)} %pad_add_fusion.info.refs_0_, bf16[4,256,256]{2,1,0:T(8,128)(2,1)S(1)} %get-tuple-element.23.lh.refs_1_, bf16[4,256,256]{2,1,0:T(8,128)(2,1)S(1)} %get-tuple-element.24.ll.refs_2_, ...), custom_call_target="tpu_custom_call", output_to_operand_aliasing={{1}: (9, {})} | custom-call | tf_op jit(solution)/shard_map/step/pallas_call | solution.py:248
  188.5 16.9 %all_to_all.22 = f32[8,72,128]{2,1,0:T(8,128)S(1)} all-to-all(f32[8,72,128]{2,1,0:T(8,128)S(1)} %get-tuple-element.36), channel_id=1, replica_groups=mesh['z'=8,'core'=2,'y'=8,'xh'=2,'xl'=2] {'z'}, dimensions={0} | all-to-all | bytes 589824 | tf_op jit(solution)/shard_map/all_to_all | solution.py:304
  205.4 6.0 %all_gather.72 = f32[4,72,128]{2,1,0:T(8,128)S(1)} all-gather(f32[1,72,128]{2,1,0:T(8,128)S(1)} %slice_add_fusion.2), channel_id=1, replica_groups=mesh['z'=8,'core'=2,'y'=8,'xh'=2,'xl'=2] {'xl','core'}, dimensions={0}, use_global_device_ids=true | all-gather | bytes 184320 | tf_op jit(solution)/shard_map/all_gather | solution.py:306
  211.5 1.9 collective-permute-start.6
  213.4 3.6 %collective-permute-done.6 = f32[8,128]{1,0:T(8,128)S(1)} collective-permute-done((f32[8,128]{1,0:T(8,128)S(1)}, f32[8,128]{1,0:T(8,128)S(1)}, u32[]{:S(2)}, u32[]{:S(2)}) %collective-permute-start.6) | collective-permute-done | bytes 4128 | tf_op jit(solution)/shard_map/ppermute | solution.py:308
  217.1 16.5 %all-gather.4 = f32[640,128]{1,0:T(8,128)S(1)} all-gather(f32[40,128]{1,0:T(8,128)S(1)} %pad_maximum_fusion.3), channel_id=6, replica_groups=mesh['z'=8,'core'=2,'y'=8,'xh'=2,'xl'=2] {'z','core'}, dimensions={0}, use_global_device_ids=true | all-gather | bytes 348160 | tf_op jit(solution)/shard_map/all_gather | solution.py:321
  233.5 1.6 last.1
  (38 shorter events, 0.3 us)
Async XLA Ops:
  0.6 7.2 %copy-start.6 = (s32[4,1]{0,1:T(1,128)S(1)}, s32[4,1]{0,1:T(1,128)}, u32[]{:S(2)}) copy-start(s32[4,1]{0,1:T(1,128)} %param.10) | copy-start | bytes 52
  2.4 16.1 %copy-start.1 = (f32[256,256]{1,0:T(8,128)}, f32[256,256]{1,0:T(8,128)S(1)}, u32[]{:S(2)}) copy-start(f32[256,256]{1,0:T(8,128)S(1)} %bitcast_select_fusion.x_own.refs_6_) | copy-start | bytes 786436
  2.4 7.7 %collective-permute-start = (f32[256,256]{1,0:T(8,128)S(1)}, f32[256,256]{1,0:T(8,128)S(1)}, u32[]{:S(2)}, u32[]{:S(2)}) collective-permute-start(f32[256,256]{1,0:T(8,128)S(1)} %bitcast_select_fusion.x_own.refs_6_), channel_id=1, source_target_pairs={{0,1},{1,2},{2,3},{3,4},{4,5},{5,6},{6,7},{7,8},{8,9},{9,10},{10,1... | collective-permute-start | bytes 786440 | tf_op jit(solution)/shard_map/ppermute | solution.py:333
  3.7 12.9 %collective-permute-start.1 = (f32[256,256]{1,0:T(8,128)}, f32[256,256]{1,0:T(8,128)S(1)}, u32[]{:S(2)}, u32[]{:S(2)}) collective-permute-start(f32[256,256]{1,0:T(8,128)} %bitcast.48), channel_id=1, source_target_pairs={{0,1},{1,2},{2,3},{3,4},{4,5},{5,6},{6,7},{7,8},{8,9},{9,10},{10,1... | collective-permute-start | bytes 786440 | tf_op jit(solution)/shard_map/ppermute | solution.py:333
  5.0 1.2 copy-start.4
  6.2 1.2 copy-start.5
  16.6 62.2 %copy-start = (f32[1,256,256]{2,1,0:T(8,128)S(1)}, f32[1,256,256]{2,1,0:T(8,128)}, u32[]{:S(2)}) copy-start(f32[1,256,256]{2,1,0:T(8,128)} %param.7) | copy-start | bytes 786436
  18.5 0.7 copy-start.3
  19.2 21.4 %all-to-all-start = ((f32[8,72,128]{2,1,0:T(8,128)}), f32[8,72,128]{2,1,0:T(8,128)}, u32[]{:S(2)}, u32[]{:S(2)}) async-start(f32[8,72,128]{2,1,0:T(8,128)} %copy-done.3), calls=%async_computation | async-start | bytes 589824 | tf_op jit(solution)/shard_map/all_to_all | solution.py:304
  28.1 50.8 %collective-permute-start.3 = (f32[256,256]{1,0:T(8,128)S(1)}, f32[256,256]{1,0:T(8,128)S(1)}, u32[]{:S(2)}, u32[]{:S(2)}) collective-permute-start(f32[256,256]{1,0:T(8,128)S(1)} %collective-permute-done.1.refs_9_.refs_7_), channel_id=1, source_target_pairs={{0,32},{32,0},{1,33},{33,1},{2,34},{34,2},{3,35},{35,3},{4,36},{36... | collective-permute-start | bytes 786440 | tf_op jit(solution)/shard_map/ppermute | solution.py:334
  48.0 11.0 %collective-permute-start.2 = (f32[8,128]{1,0:T(8,128)S(1)}, f32[8,128]{1,0:T(8,128)S(1)}, u32[]{:S(2)}, u32[]{:S(2)}) collective-permute-start(f32[8,128]{1,0:T(8,128)S(1)} %fusion.13), channel_id=1, source_target_pairs={{0,0},{1,1},{2,2},{3,3},{4,4},{5,5},{6,6},{7,7},{8,8},{9,9},{10,10... | collective-permute-start | bytes 12296 | tf_op jit(solution)/shard_map/ppermute | solution.py:308
  78.8 1.0 copy-start.2
  105.9 8.6 %collective-permute-start.4 = (f32[8,128]{1,0:T(8,128)S(1)}, f32[8,128]{1,0:T(8,128)S(1)}, u32[]{:S(2)}, u32[]{:S(2)}) collective-permute-start(f32[8,128]{1,0:T(8,128)S(1)} %fusion.12), channel_id=1, source_target_pairs={{0,0},{1,1},{2,2},{3,3},{4,4},{5,5},{6,6},{7,7},{8,8},{9,9},{10,10... | collective-permute-start | bytes 12296 | tf_op jit(solution)/shard_map/ppermute | solution.py:308
  158.5 8.9 %collective-permute-start.5 = (f32[8,128]{1,0:T(8,128)S(1)}, f32[8,128]{1,0:T(8,128)S(1)}, u32[]{:S(2)}, u32[]{:S(2)}) collective-permute-start(f32[8,128]{1,0:T(8,128)S(1)} %fusion.11), channel_id=1, source_target_pairs={{0,0},{1,1},{2,2},{3,3},{4,4},{5,5},{6,6},{7,7},{8,8},{9,9},{10,10... | collective-permute-start | bytes 12296 | tf_op jit(solution)/shard_map/ppermute | solution.py:308
  211.5 5.6 %collective-permute-start.6 = (f32[8,128]{1,0:T(8,128)S(1)}, f32[8,128]{1,0:T(8,128)S(1)}, u32[]{:S(2)}, u32[]{:S(2)}) collective-permute-start(f32[8,128]{1,0:T(8,128)S(1)} %fusion.10), channel_id=1, source_target_pairs={{0,0},{1,1},{2,2},{3,3},{4,4},{5,5},{6,6},{7,7},{8,8},{9,9},{10,10... | collective-permute-start | bytes 12296 | tf_op jit(solution)/shard_map/ppermute | solution.py:308
